TPU v7x, 32 devices: a whole 2x2x4 slice. The times are simulated.
32 devices in a mesh: inst: 8 (over y, x, core), space: 4 (over z).
Axes of the slice: x: 2, y: 2, z: 4, core: 2. Of those that a mesh axis runs over, the one named last changes fastest.
Arguments:
- adjoint: float32 [8, 5, 16, 16, 128], P('inst', None, 'space'), may hold values from -6 to 6
- jacobian: float32 [8, 7, 5, 5, 16, 16, 128], P('inst', None, None, None, 'space'), may hold values from -4 to 4
- volume: float32 [16, 16, 128], P('space'), may hold values from 0.5 to 2
- source: float32 [8, 5, 16, 16, 128], P('inst', None, 'space'), may hold values from -6 to 6
- surface_out: float32 [5, 16, 128], P(None, 'space'), may hold values from -1 to 1
- surface_in: float32 [5, 16, 128], P(None, 'space'), may hold values from -6 to 6
- station: int32 [16, 128], P('space'), may hold values from 0 to 255
- phi: float32 [40, 256], replicated, may hold values from -0.375 to 0.375
- inv_stiff: float32 [40], replicated, may hold values from 0.5 to 8
Outputs:
- residual: float32 [8, 5, 16, 16, 128], P('inst', None, 'space')
- modal: float32 [8, 40], P('inst')
All inputs are finite; a program needn't handle non-finite values.
Results may differ from a plain program's by a relative error of at most 0.000078.
Values sent between devices are 32-bit elements; how exact they have to be, the bound alone decides.
No kernel may reach another device: no remote copies, remote signals or barrier semaphores. Data moves between devices by JAX's collectives and lax.ppermute only.
A program may use at most 64 MiB of HBM per device.

v0:
```python
import jax
import jax.numpy as jnp
from jax import lax
from jax.sharding import PartitionSpec as P


def padded(cells, sides, width):
    for axis, dim in sides:
        count = lax.axis_size(axis)
        head = lax.slice_in_dim(cells, 0, width, axis=dim)
        tail = lax.slice_in_dim(cells, cells.shape[dim] - width, cells.shape[dim], axis=dim)
        cells = jnp.concatenate(
            [
                lax.ppermute(tail, axis, [(i, (i + 1) % count) for i in range(count)]),
                cells,
                lax.ppermute(head, axis, [((i + 1) % count, i) for i in range(count)]),
            ],
            axis=dim,
        )
    return cells


def time_weights(count):
    index = jnp.arange(count)
    diff = index[:, None] - index[None, :]
    angle = jnp.pi * diff.astype(jnp.float32) / count
    parity = (1 - 2 * (diff % 2)).astype(jnp.float32)
    offdiag = diff != 0
    safe_sin = jnp.where(offdiag, jnp.sin(angle), jnp.float32(1.0))
    first = jnp.where(offdiag, 0.5 * parity * jnp.cos(angle) / safe_sin, jnp.float32(0.0))
    second = jnp.where(offdiag, -0.5 * parity / (safe_sin * safe_sin), -(count * count + 2) / 12.0)
    return first - 0.25 * second


def body(adjoint, jacobian, volume, source, surface_out, surface_in, station, phi, inv_stiff):
    lam = adjoint[0]
    count = lax.axis_size("inst")
    weights = time_weights(count)
    my_inst = lax.axis_index("inst")
    column = weights[:, my_inst]
    mixed = jnp.einsum(
        "m,mjxyz->jxyz",
        column,
        lax.all_gather(adjoint, "inst", axis=0, tiled=True),
        precision=lax.Precision.HIGHEST,
    )
    spectral = volume[None] * mixed
    face = jnp.sum(surface_out * lam[:, :, 0, :], axis=0)
    stations = phi.shape[1]
    onehot = (station.reshape(-1)[:, None] == jnp.arange(stations)[None, :]).astype(jnp.float32)
    local_loads = jnp.dot(face.reshape(-1), onehot, precision=lax.Precision.HIGHEST)
    loads = lax.psum(local_loads, "space")
    modal = inv_stiff * jnp.dot(phi, loads, precision=lax.Precision.HIGHEST)
    prod = jnp.einsum("dijxyz,ixyz->djxyz", jacobian[0], lam, precision=lax.Precision.HIGHEST)
    extended = padded(jnp.stack([prod[1], prod[2]]), (("space", 2),), 1)
    from_left = extended[0][:, :-2]
    from_right = extended[1][:, 2:]
    flux = prod[0] + from_left + from_right
    flux = flux + jnp.pad(prod[3], ((0, 0), (0, 0), (1, 0), (0, 0)))[:, :, :-1]
    flux = flux + jnp.pad(prod[4], ((0, 0), (0, 0), (0, 1), (0, 0)))[:, :, 1:]
    flux = flux + jnp.pad(prod[5], ((0, 0), (0, 0), (0, 0), (1, 0)))[:, :, :, :-1]
    flux = flux + jnp.pad(prod[6], ((0, 0), (0, 0), (0, 0), (0, 1)))[:, :, :, 1:]
    face_modes = jnp.dot(onehot, phi.T, precision=lax.Precision.HIGHEST)
    back = jnp.dot(face_modes, modal, precision=lax.Precision.HIGHEST).reshape(face.shape)
    residual = flux + spectral - source[0]
    residual = residual.at[:, :, 0, :].add(surface_in * back[None])
    return (residual[None], modal[None])


def solution(mesh):
    placed = (
        P("inst", None, "space", None, None),
        P("inst", None, None, None, "space", None, None),
        P("space", None, None),
        P("inst", None, "space", None, None),
        P(None, "space", None),
        P(None, "space", None),
        P("space", None),
        P(),
        P(),
    )
    return jax.shard_map(
        body,
        mesh=mesh,
        in_specs=placed,
        out_specs=(P("inst", None, "space", None, None), P("inst", None)),
        check_vma=False,
    )
```

profile of v0, /device:TPU:0, one launch (start us, length us, event | category | flops | bytes accessed | tf_op | source)
XLA Modules:
  0.0 48.7 jit_solution(2997577247698372779)
XLA Ops:
  7.2 0.0 copy-start
  7.2 0.0 all-gather.2.cloned.1.call-start
  7.2 0.7 %all-gather.2.cloned.1.call-update = ((f32[1,5,4,16,128]{4,3,2,1,0:T(8,128)}), f32[8,5,4,16,128]{4,3,2,1,0:T(8,128)}) async-update(((), (), s32[]{:S(2)}) %all-gather.2.cloned.1.call-start, f32[1,5,4,16,128]{4,3,2,1,0:T(8,128)} %param.11) | async-update | bytes 1638424
  7.9 1.0 %copy.41 = f32[1,5,4,16,128]{4,2,1,3,0:T(4,128)S(1)} copy(f32[1,5,4,16,128]{4,3,2,1,0:T(8,128)} %param.11) | data formatting | bytes 327680
  8.9 3.5 %fusion = f32[4,16,128,7,5]{2,1,0,4,3:T(8,128)S(1)} fusion(f32[1,7,5,5,4,16,128]{6,5,4,3,2,1,0:T(8,128)} %param.12, f32[4,16,128,5]{2,1,0,3:T(8,128)S(1)} %copy.31), kind=kLoop, calls=%fused_computation.1 | loop fusion | flops 2580480 | bytes 7045120
  12.5 0.0 copy-start.3
  12.5 0.0 copy-start.4
  12.5 0.0 copy-start.6
  12.5 0.0 copy-start.8
  12.5 0.4 copy.40
  13.0 0.1 fusion.29
  13.1 3.1 %collective-permute-start = (f32[2,5,1,16,128]{4,2,1,3,0:T(1,128)S(1)}, f32[2,5,1,16,128]{4,2,1,3,0:T(1,128)S(1)}, u32[]{:S(2)}, u32[]{:S(2)}) collective-permute-start(f32[2,5,1,16,128]{4,2,1,3,0:T(1,128)S(1)} %get-tuple-element.14), channel_id=1, source_target_pairs={{0,1},{1,2},{2,3},{3,0},{4,5},{5,6},{6,7},{7,4},{8,9},{9,10},{10,1... | collective-permute-start | bytes 245768 | tf_op jit(solution)/shard_map/ppermute | solution.py:14
  16.2 2.1 %collective-permute-start.1 = (f32[2,5,1,16,128]{4,2,1,3,0:T(1,128)S(1)}, f32[2,5,1,16,128]{4,2,1,3,0:T(1,128)S(1)}, u32[]{:S(2)}, u32[]{:S(2)}) collective-permute-start(f32[2,5,1,16,128]{4,2,1,3,0:T(1,128)S(1)} %get-tuple-element.15), channel_id=1, source_target_pairs={{1,0},{2,1},{3,2},{0,3},{5,4},{6,5},{7,6},{4,7},{9,8},{10,9},{11,1... | collective-permute-start | bytes 245768 | tf_op jit(solution)/shard_map/ppermute | solution.py:16
  18.3 0.0 copy-done.4
  18.4 0.3 fusion.4
  18.7 10.3 %psum.7 = f32[256]{0:T(256)S(1)} all-reduce(f32[256]{0:T(256)S(1)} %bitcast.91), channel_id=1, replica_groups=mesh['inst'=8,'space'=4] {'space'}, use_global_device_ids=true, to_apply=%region_1.2 | all-reduce | flops 256 | bytes 2048 | tf_op jit(solution)/shard_map/psum | solution.py:52
  29.0 0.1 fusion.3
  29.1 0.4 fusion.5
  29.6 0.3 fusion.25
  29.9 0.1 slice_bitcast_fusion.2
  30.0 0.1 multiply_subtract_fusion
  30.1 0.0 collective-permute-done
  30.1 0.0 collective-permute-done.1
  30.1 0.2 pad_maximum_fusion
  30.3 0.0 copy-start.1
  30.4 6.9 %all-gather.2.cloned.1.call-done = f32[8,5,4,16,128]{4,3,2,1,0:T(8,128)} async-done(((f32[1,5,4,16,128]{4,3,2,1,0:T(8,128)}), f32[8,5,4,16,128]{4,3,2,1,0:T(8,128)}) %all-gather.2.cloned.1.call-update) | async-done | bytes 1310736 | tf_op jit(solution)/shard_map/all_gather | solution.py:44
  37.2 3.1 %fusion.1 = f32[1,5,4,16,128]{4,0,3,2,1:T(1,128)S(1)} fusion(f32[8,5,4,16,128]{4,3,2,1,0:T(8,128)} %all-gather.2.cloned.1.call-done, f32[8,8]{0,1:T(8,128)S(1)} %multiply_subtract_fusion, s32[]{:T(128)S(6)} %select_n.25), kind=kOutput, calls=%fused_computation.2 | convolution fusion | flops 3932160 | bytes 1475076 | tf_op jit(solution)/shard_map/m,mjxyz->jxyz/dot_general | solution.py:41
  40.4 0.0 copy-start.5
  40.4 0.3 fusion.13
  40.7 0.4 copy-done.5
  41.1 0.0 copy-start.2
  41.2 0.7 %copy-done.2 = f32[1,5,4,16,128]{4,3,2,1,0:T(8,128)} copy-done((f32[1,5,4,16,128]{4,3,2,1,0:T(8,128)}, f32[1,5,4,16,128]{4,3,2,1,0:T(8,128)S(1)}, u32[]{:S(2)}) %copy-start.2) | copy-done | bytes 163864
  (15 shorter events, 0.2 us)
Async XLA Ops:
  7.2 21.8 %copy-start = (f32[40,256]{1,0:T(8,128)S(1)}, f32[40,256]{1,0:T(8,128)}, u32[]{:S(2)}) copy-start(f32[40,256]{1,0:T(8,128)} %param.18) | copy-start | bytes 122884
  7.2 30.1 %all-gather.2.cloned.1.call-start = ((), (), s32[]{:S(2)}) async-start(), calls=%async_computation | async-start | bytes 1474560 | tf_op jit(solution)/shard_map/all_gather | solution.py:44
  12.5 5.8 %copy-start.3 = (f32[4,16,128]{2,1,0:T(8,128)S(1)}, f32[4,16,128]{2,1,0:T(8,128)}, u32[]{:S(2)}) copy-start(f32[4,16,128]{2,1,0:T(8,128)} %param.13) | copy-start | bytes 98308
  12.5 5.9 %copy-start.4 = (f32[5,4,128]{2,1,0:T(4,128)S(1)}, f32[5,4,128]{2,1,0:T(4,128)}, u32[]{:S(2)}) copy-start(f32[5,4,128]{2,1,0:T(4,128)} %param.15) | copy-start | bytes 30724
  12.5 5.9 %copy-start.6 = (s32[4,128]{1,0:T(4,128)S(1)}, s32[4,128]{1,0:T(4,128)}, u32[]{:S(2)}) copy-start(s32[4,128]{1,0:T(4,128)} %param.17) | copy-start | bytes 6148
  12.5 16.5 %copy-start.8 = (f32[40]{0:T(128)S(1)}, f32[40]{0:T(128)}, u32[]{:S(2)}) copy-start(f32[40]{0:T(128)} %param.19) | copy-start | bytes 484
  13.1 17.0 %collective-permute-start = (f32[2,5,1,16,128]{4,2,1,3,0:T(1,128)S(1)}, f32[2,5,1,16,128]{4,2,1,3,0:T(1,128)S(1)}, u32[]{:S(2)}, u32[]{:S(2)}) collective-permute-start(f32[2,5,1,16,128]{4,2,1,3,0:T(1,128)S(1)} %get-tuple-element.14), channel_id=1, source_target_pairs={{0,1},{1,2},{2,3},{3,0},{4,5},{5,6},{6,7},{7,4},{8,9},{9,10},{10,1... | collective-permute-start | bytes 245768 | tf_op jit(solution)/shard_map/ppermute | solution.py:14
  16.2 13.9 %collective-permute-start.1 = (f32[2,5,1,16,128]{4,2,1,3,0:T(1,128)S(1)}, f32[2,5,1,16,128]{4,2,1,3,0:T(1,128)S(1)}, u32[]{:S(2)}, u32[]{:S(2)}) collective-permute-start(f32[2,5,1,16,128]{4,2,1,3,0:T(1,128)S(1)} %get-tuple-element.15), channel_id=1, source_target_pairs={{1,0},{2,1},{3,2},{0,3},{5,4},{6,5},{7,6},{4,7},{9,8},{10,9},{11,1... | collective-permute-start | bytes 245768 | tf_op jit(solution)/shard_map/ppermute | solution.py:16
  29.1 1.2 %copy-start.7 = (f32[40]{0:T(128)}, f32[40]{0:T(128)S(1)}, u32[]{:S(2)}) copy-start(f32[40]{0:T(128)S(1)} %fusion.3) | copy-start | bytes 484
  30.3 10.1 %copy-start.1 = (f32[1,5,4,16,128]{4,3,2,1,0:T(8,128)S(1)}, f32[1,5,4,16,128]{4,3,2,1,0:T(8,128)}, u32[]{:S(2)}) copy-start(f32[1,5,4,16,128]{4,3,2,1,0:T(8,128)} %param.14) | copy-start | bytes 491524
  40.4 0.7 %copy-start.5 = (f32[5,4,128]{2,1,0:T(4,128)S(1)}, f32[5,4,128]{2,1,0:T(4,128)}, u32[]{:S(2)}) copy-start(f32[5,4,128]{2,1,0:T(4,128)} %param.16) | copy-start | bytes 30724
  41.1 0.7 %copy-start.2 = (f32[1,5,4,16,128]{4,3,2,1,0:T(8,128)}, f32[1,5,4,16,128]{4,3,2,1,0:T(8,128)S(1)}, u32[]{:S(2)}) copy-start(f32[1,5,4,16,128]{4,3,2,1,0:T(8,128)S(1)} %scatter-add.4) | copy-start | bytes 491524
Sparse Core Ops, SparseCore 0:
  9.9 27.2 all-gather.1
where the time goes:
time: 48.9 us; the launch traced here: 48.7 us
  between operations  14.3 us (29%)
  blocking collectives  10.3 us (21%)
  waiting for transfers between devices  7.54 us (15%)
  starting transfers between devices  5.2 us (11%)
  matrix products  4.33 us (9%)
  other arithmetic  4.09 us (8%)
  local copies, waits for them, and re-layouts  2.89 us (6%)
    psum x1, blocking collectives, body(): loads = lax.psum(local_loads, 'space')  10.3 us
    all_gather x1, waiting for transfers between devices, body(): lax.all_gather(adjoint, 'inst', axis=0, tiled=True)  6.86 us
    unnamed x1, other arithmetic  3.53 us
    dot_general x1, matrix products, body(): jnp.einsum('m,mjxyz->jxyz', column, lax.all_gather(adjoint, 'inst', axis=...  3.14 us
    ppermute x1, starting transfers between devices, padded(): lax.ppermute(tail, axis, [(i, (i + 1) % count) for i in range(count)])  3.08 us
    unnamed x21, local copies, waits for them, and re-layouts  2.1 us
    ppermute x1, starting transfers between devices, padded(): lax.ppermute(head, axis, [((i + 1) % count, i) for i in range(count)])  2.09 us
  transfers between devices with their start and end apart: 3, of which 1 were waited for; matrix products, arithmetic and copies ran while one was open for 14% of the time, Pallas kernels for 0%

commit v1 on v0

v1 whole, which is shorter than its diff:
```python
import functools
import math

import jax
import jax.numpy as jnp
import numpy as np
from jax import lax
from jax.experimental import pallas as pl
from jax.experimental.pallas import tpu as pltpu
from jax.sharding import PartitionSpec as P

VMEM = pl.BlockSpec(memory_space=pltpu.VMEM)
HBM = pl.BlockSpec(memory_space=pltpu.HBM)
F32 = jnp.float32


def weight_table(count):
    table = []
    for k in range(count):
        if k == 0:
            first, second = 0.0, -(count * count + 2) / 12.0
        else:
            sign = 1.0 - 2.0 * (k % 2)
            sine = math.sin(math.pi * k / count)
            first = 0.5 * sign * math.cos(math.pi * k / count) / sine
            second = -0.5 * sign / (sine * sine)
        table.append(first - 0.25 * second)
    return np.asarray(table, np.float32)


def weight_of(count, source, target):
    gap = lax.rem(source - target + count, count)
    value = jnp.float32(0.0)
    for k, entry in enumerate(weight_table(count)):
        value = jnp.where(gap == k, jnp.float32(entry), value)
    return value


def prep_kernel(
    lam_in, source_in, volume_in, inward_in, outward_in, station_in, phi_in, stiff_in, jac,
    near, wrap, packed, modes, lam, source, volume, inward,
    block, outward, station, phi, inv_stiff, sem,
):
    nv, nx, ny, nz = lam.shape[1:]
    odd = lax.rem(lax.axis_index("space"), 2)
    sides = (odd, 1 - odd)
    moves = [(station_in, station), (phi_in, phi), (stiff_in, inv_stiff), (outward_in, outward), (lam_in, lam)]
    for slot, minus in enumerate(sides):
        moves.append((jac.at[0, 1 + minus, :, :, (nx - 1) * (1 - minus)], block.at[slot]))
    moves += [(source_in, source), (volume_in, volume), (inward_in, inward)]
    copies = [pltpu.make_async_copy(src, dst, sem.at[i]) for i, (src, dst) in enumerate(moves)]
    for copy in copies:
        copy.start()
    modes_k, stations = phi.shape
    copies[0].wait()
    copies[1].wait()
    full = phi[...]
    high = full.astype(jnp.bfloat16)
    rest = full - high.astype(F32)
    mid = rest.astype(jnp.bfloat16)
    low = (rest - mid.astype(F32)).astype(jnp.bfloat16)
    rows = lax.broadcasted_iota(jnp.int32, (stations, nz), 0)
    for x in range(nx):
        hot = (rows == station[x : x + 1, :]).astype(F32).astype(jnp.bfloat16)
        modes[x] = (
            jnp.dot(low, hot, preferred_element_type=F32)
            + jnp.dot(mid, hot, preferred_element_type=F32)
            + jnp.dot(high, hot, preferred_element_type=F32)
        )
    for copy in copies[2:5]:
        copy.wait()
    share = jnp.zeros((modes_k, nz), F32)
    for x in range(nx):
        face = outward[0, x : x + 1, :] * lam[0, 0, x, 0:1, :]
        for j in range(1, nv):
            face = face + outward[j, x : x + 1, :] * lam[0, j, x, 0:1, :]
        share = share + modes[x] * face
    row = lax.broadcasted_iota(jnp.int32, (modes_k, modes_k), 0)
    lane = lax.broadcasted_iota(jnp.int32, (modes_k, modes_k), 1)
    stiff = jnp.sum(jnp.where(row == lane, inv_stiff[...], 0.0), axis=1, keepdims=True)
    column = jnp.sum(share, axis=1, keepdims=True) * stiff
    tile_lane = lax.broadcasted_iota(jnp.int32, (8, nz), 1)
    tile = jnp.zeros((8, nz), F32)
    for group in range(modes_k // 8):
        tile = jnp.where(tile_lane == group, column[8 * group : 8 * group + 8], tile)
    packed[...] = tile
    near[nv * ny :, :] = tile
    wrap[nv * ny :, :] = tile
    for slot, (minus, out) in enumerate(zip(sides, (near, wrap))):
        copies[5 + slot].wait()
        cells = lam[0, :, (nx - 1) * (1 - minus)]
        for j in range(nv):
            total = block[slot, 0, j] * cells[0]
            for i in range(1, nv):
                total = total + block[slot, i, j] * cells[i]
            out[j * ny : (j + 1) * ny, :] = total
    for copy in copies[7:]:
        copy.wait()


def share_kernel(masks, *refs):
    held, out = refs[:-1], refs[-1]
    count = lax.axis_size("inst")
    me = lax.axis_index("inst")
    total = None
    for mask, block in zip(masks, held):
        term = weight_of(count, me ^ mask, me ^ 1) * block[0]
        total = term if total is None else total + term
    out[0] = total


def own_kernel(masks, partial, volume, *refs):
    held, out = refs[:-1], refs[-1]
    count = lax.axis_size("inst")
    me = lax.axis_index("inst")
    total = None
    for mask, block in zip(masks, held):
        term = weight_of(count, me ^ mask, me) * block[0]
        total = term if total is None else total + term
    out[0] = volume[...][None] * total + partial[0]


def flux_kernel(lam, source, jac, out):
    nv, nx, ny, nz = lam.shape[1:]
    y = lax.broadcasted_iota(jnp.int32, (ny, nz), 0)
    z = lax.broadcasted_iota(jnp.int32, (ny, nz), 1)

    def product(d, j, x):
        total = jac[0, d, 0, j, x] * lam[0, 0, x]
        for i in range(1, nv):
            total = total + jac[0, d, i, j, x] * lam[0, i, x]
        return total

    for j in range(nv):
        for x in range(nx):
            total = product(0, j, x) - source[0, j, x]
            if x > 0:
                total = total + product(1, j, x - 1)
            if x < nx - 1:
                total = total + product(2, j, x + 1)
            total = total + jnp.where(y == 0, 0.0, pltpu.roll(product(3, j, x), 1, 0))
            total = total + jnp.where(y == ny - 1, 0.0, pltpu.roll(product(4, j, x), ny - 1, 0))
            total = total + jnp.where(z == 0, 0.0, pltpu.roll(product(5, j, x), 1, 1))
            total = total + jnp.where(z == nz - 1, 0.0, pltpu.roll(product(6, j, x), nz - 1, 1))
            out[0, j, x] = total


def final_kernel(partial, volume, mix, near, wrap, modal_tile, modes, surface_in, out, modal):
    nv, nx, ny, nz = partial.shape[1:]
    groups = modal.shape[1] // 8
    odd = lax.rem(lax.axis_index("space"), 2)
    tile = modal_tile[...]
    columns = [tile[:, group : group + 1] for group in range(groups)]
    for group, column in enumerate(columns):
        row = lax.broadcasted_iota(jnp.int32, (8, 8 * groups), 0)
        lane = lax.broadcasted_iota(jnp.int32, (8, 8 * groups), 1)
        piece = jnp.sum(jnp.where(lane == row + 8 * group, column, 0.0), axis=0, keepdims=True)
        line = piece if group == 0 else line + piece
    modal[...] = line
    low = lax.broadcasted_iota(jnp.int32, (ny, nz), 0) == 0
    is_odd = odd == 1
    for x in range(nx):
        back = jnp.zeros((8, nz), F32)
        for group, column in enumerate(columns):
            back = back + modes[x, 8 * group : 8 * group + 8, :] * column
        back = jnp.sum(back, axis=0, keepdims=True)
        for j in range(nv):
            value = partial[0, j, x] + volume[x] * mix[0, j, x]
            rows = pl.ds(j * ny, ny)
            if x == 0:
                value = value + jnp.where(is_odd, near[rows, :], wrap[rows, :])
            if x == nx - 1:
                value = value + jnp.where(is_odd, wrap[rows, :], near[rows, :])
            out[0, j, x] = value + jnp.where(low, surface_in[j, x : x + 1, :] * back, 0.0)


def body(adjoint, jacobian, volume, source, surface_out, surface_in, station, phi, inv_stiff):
    count, slabs = lax.axis_size("inst"), lax.axis_size("space")
    nv, nx, ny, nz = adjoint.shape[1:]
    modes_k = phi.shape[0]

    def swap(value, axis, mask):
        size = lax.axis_size(axis)
        return lax.ppermute(value, axis, [(i, i ^ mask) for i in range(size)])

    def like(array):
        return jax.ShapeDtypeStruct(array.shape, F32)

    masks = tuple(range(0, count, 2))
    foreign = [swap(adjoint, "inst", mask) for mask in masks[1:]]
    rows = nv * ny + 8
    whole = (adjoint, source, volume, surface_in, surface_out, station, phi, inv_stiff.reshape(1, modes_k), jacobian)
    near, wrap, packed, modes, lam, src, vol, inward = pl.pallas_call(
        prep_kernel,
        out_shape=(
            pltpu.VMEM((rows, nz), F32),
            pltpu.VMEM((rows, nz), F32),
            pltpu.VMEM((8, nz), F32),
            pltpu.VMEM((nx, modes_k, nz), F32),
            pltpu.VMEM(adjoint.shape, F32),
            pltpu.VMEM(source.shape, F32),
            pltpu.VMEM(volume.shape, F32),
            pltpu.VMEM(surface_in.shape, F32),
        ),
        in_specs=[HBM] * 9,
        out_specs=(VMEM,) * 8,
        scratch_shapes=[
            pltpu.VMEM((2, nv, nv, ny, nz), F32),
            pltpu.VMEM(surface_out.shape, F32),
            pltpu.VMEM(station.shape, station.dtype),
            pltpu.VMEM(phi.shape, F32),
            pltpu.VMEM((1, modes_k), F32),
            pltpu.SemaphoreType.DMA((10,)),
        ],
        compiler_params=pltpu.CompilerParams(vmem_limit_bytes=8 * 2**20),
        name="prep",
    )(*(pltpu.with_memory_space_constraint(value, pltpu.HBM) for value in whole))
    wrap_in = lax.ppermute(wrap, "space", [(i, (((i + 1) ^ 1) - 1) % slabs) for i in range(slabs)])
    near_in = swap(near, "space", 1)
    if slabs == 4:
        far_in = swap(packed, "space", 2)
        tile = (packed + near_in[nv * ny :]) + (wrap_in[nv * ny :] + far_in)
    else:
        tile = packed + near_in[nv * ny :]
        step = 2
        while step < slabs:
            tile = tile + swap(tile, "space", step)
            step *= 2
    partial = pl.pallas_call(
        flux_kernel,
        out_shape=like(adjoint),
        in_specs=[VMEM] * 3,
        out_specs=VMEM,
        compiler_params=pltpu.CompilerParams(vmem_limit_bytes=16 * 2**20),
        cost_estimate=pl.CostEstimate(flops=2 * jacobian.size, bytes_accessed=4 * jacobian.size, transcendentals=0),
        name="flux",
    )(lam, src, jacobian)
    held = [lam] + foreign
    share = pl.pallas_call(
        functools.partial(share_kernel, masks),
        out_shape=like(adjoint),
        in_specs=[VMEM] * len(masks),
        out_specs=VMEM,
        compiler_params=pltpu.CompilerParams(vmem_limit_bytes=8 * 2**20),
        name="share",
    )(*held)
    mix = swap(share, "inst", 1)
    partial = pl.pallas_call(
        functools.partial(own_kernel, masks),
        out_shape=like(adjoint),
        in_specs=[VMEM] * (2 + len(masks)),
        out_specs=VMEM,
        compiler_params=pltpu.CompilerParams(vmem_limit_bytes=8 * 2**20),
        name="own",
    )(partial, vol, *held)
    residual, modal = pl.pallas_call(
        final_kernel,
        out_shape=(like(adjoint), jax.ShapeDtypeStruct((1, modes_k), F32)),
        in_specs=[VMEM] * 8,
        out_specs=(VMEM, VMEM),
        compiler_params=pltpu.CompilerParams(vmem_limit_bytes=8 * 2**20),
        name="final",
    )(partial, vol, mix, near_in, wrap_in, tile, modes, inward)
    return residual, modal


def solution(mesh):
    placed = (
        P("inst", None, "space", None, None),
        P("inst", None, None, None, "space", None, None),
        P("space", None, None),
        P("inst", None, "space", None, None),
        P(None, "space", None),
        P(None, "space", None),
        P("space", None),
        P(),
        P(),
    )
    return jax.shard_map(
        body,
        mesh=mesh,
        in_specs=placed,
        out_specs=(P("inst", None, "space", None, None), P("inst", None)),
        check_vma=False,
    )
```

time: 48.9 us -> 16.7 us (0.34)
  between operations: 14.3 us -> 0.68 us
  blocking collectives: 10.3 us -> 0 us
  starting transfers between devices: 5.2 us -> 10.1 us
  waiting for transfers between devices: 7.54 us -> 3.07 us
  matrix products: 4.33 us -> 0 us
  other arithmetic: 4.09 us -> 0.01 us
  local copies, waits for them, and re-layouts: 2.89 us -> 0.01 us
  Pallas kernels: 0 us -> 2.66 us
    psum x1 -> x0, blocking collectives: 10.3 us -> none  [body(): loads = lax.psum(local_loads, 'space')]
    all_gather x1 -> x0, waiting for transfers between devices: 6.86 us -> none  [body(): lax.all_gather(adjoint, 'inst', axis=0, tiled=True)]
    ppermute x2 -> x7, starting transfers between devices: 5.17 us -> 10.1 us  [the longest x6 7.63 us: swap(): return lax.ppermute(value, axis, [(i, i ^ mask) for i in range(size)])]
    dot_general x5 -> x0, matrix products: 4.33 us -> none  [the longest x1 3.14 us: body(): jnp.einsum('m,mjxyz->jxyz', column, lax.all_gather(adjoint, 'inst', axis=...]
    unnamed x1 -> x0, other arithmetic: 3.53 us -> none
    ppermute x2 -> x7, waiting for transfers between devices: 0.01 us -> 3.07 us  [the longest x6 3.07 us: swap(): return lax.ppermute(value, axis, [(i, i ^ mask) for i in range(size)])]
    pallas_call x0 -> x5, Pallas kernels: none -> 2.66 us  [the longest x1 1.36 us: body(): pl.pallas_call(prep_kernel, out_shape=(pltpu.VMEM((rows, nz), F32), pltpu...]
    unnamed x21 -> x2, local copies, waits for them, and re-layouts: 2.1 us -> 0.01 us
  transfers between devices with their start and end apart: 3 -> 7, of which waited for: 1 -> 3; matrix products, arithmetic and copies ran while one was open for 14% -> 0% of each run, Pallas kernels for 0% -> 11%
where the time goes in v1:
time: 16.7 us; the launch traced here: 16.5 us
  starting transfers between devices  10.1 us (60%)
  waiting for transfers between devices  3.07 us (18%)
  Pallas kernels  2.66 us (16%)
  between operations  0.68 us (4%)
    ppermute x6, starting transfers between devices, swap(): return lax.ppermute(value, axis, [(i, i ^ mask) for i in range(size)])  7.63 us
    ppermute x6, waiting for transfers between devices, swap(): return lax.ppermute(value, axis, [(i, i ^ mask) for i in range(size)])  3.07 us
    ppermute x1, starting transfers between devices, body(): lax.ppermute(wrap, 'space', [(i, ((i + 1 ^ 1) - 1) % slabs) for i in rang...  2.47 us
    pallas_call x1, Pallas kernels, body(): pl.pallas_call(prep_kernel, out_shape=(pltpu.VMEM((rows, nz), F32), pltpu...  1.36 us
    pallas_call x1, Pallas kernels, body(): pl.pallas_call(final_kernel, out_shape=(like(adjoint), jax.ShapeDtypeStru...  0.77 us
    pallas_call x1, Pallas kernels, body(): pl.pallas_call(flux_kernel, out_shape=like(adjoint), in_specs=[VMEM] * 3,...  0.42 us
  transfers between devices with their start and end apart: 7, of which 3 were waited for; matrix products, arithmetic and copies ran while one was open for 0% of the time, Pallas kernels for 11%

profile of v1, /device:TPU:0, one launch (start us, length us, event | category | flops | bytes accessed | tf_op | source)
XLA Modules:
  0.0 16.5 jit_solution(5937156951530602586)
XLA Ops:
  0.6 0.0 copy-start
  0.6 3.0 %collective-permute-start = (f32[1,5,4,16,128]{4,3,2,1,0:T(8,128)}, f32[1,5,4,16,128]{4,3,2,1,0:T(8,128)S(1)}, u32[]{:S(2)}, u32[]{:S(2)}) collective-permute-start(f32[1,5,4,16,128]{4,3,2,1,0:T(8,128)} %lam_in.1), channel_id=1, source_target_pairs={{0,8},{4,12},{8,0},{12,4},{16,24},{20,28},{24,16},{28,20},{1,9},{5... | collective-permute-start | bytes 491528 | tf_op jit(solution)/shard_map/ppermute | solution.py:184
  3.6 1.5 %collective-permute-start.2 = (f32[1,5,4,16,128]{4,3,2,1,0:T(8,128)}, f32[1,5,4,16,128]{4,3,2,1,0:T(8,128)S(1)}, u32[]{:S(2)}, u32[]{:S(2)}) collective-permute-start(f32[1,5,4,16,128]{4,3,2,1,0:T(8,128)} %lam_in.1), channel_id=1, source_target_pairs={{0,24},{4,28},{8,16},{12,20},{16,8},{20,12},{24,0},{28,4},{1,25},{... | collective-permute-start | bytes 491528 | tf_op jit(solution)/shard_map/ppermute | solution.py:184
  5.1 0.0 collective-permute-start.1
  5.2 1.4 %prep.1 = (f32[88,128]{1,0:T(8,128)S(1)}, f32[88,128]{1,0:T(8,128)S(1)}, f32[8,128]{1,0:T(8,128)S(1)}, f32[4,40,128]{2,1,0:T(8,128)S(1)}, f32[1,5,4,16,128]{4,3,...) custom-call(f32[1,5,4,16,128]{4,3,2,1,0:T(8,128)} %lam_in.1, ...), custom_call_target="tpu_custom_call" | custom-call | tf_op jit(solution)/shard_map/prep/pallas_call | solution.py:193
  6.6 2.1 %collective-permute-start.4 = (f32[88,128]{1,0:T(8,128)S(1)}, f32[88,128]{1,0:T(8,128)S(1)}, u32[]{:S(2)}, u32[]{:S(2)}) collective-permute-start(f32[88,128]{1,0:T(8,128)S(1)} %get-tuple-element.13), channel_id=1, source_target_pairs={{0,1},{1,0},{2,3},{3,2},{4,5},{5,4},{6,7},{7,6},{8,9},{9,8},{10,11... | collective-permute-start | bytes 135176 | tf_op jit(solution)/shard_map/ppermute | solution.py:184
  8.7 2.5 %collective-permute-start.5 = (f32[88,128]{1,0:T(8,128)S(1)}, f32[88,128]{1,0:T(8,128)S(1)}, u32[]{:S(2)}, u32[]{:S(2)}) collective-permute-start(f32[88,128]{1,0:T(8,128)S(1)} %get-tuple-element.14), channel_id=1, source_target_pairs={{0,3},{1,2},{2,1},{3,0},{4,7},{5,6},{6,5},{7,4},{8,11},{9,10},{10,... | collective-permute-start | bytes 135176 | tf_op jit(solution)/shard_map/ppermute | solution.py:218
  11.1 0.0 collective-permute-done.refs_1_
  11.1 0.9 %collective-permute-start.6 = (f32[8,128]{1,0:T(8,128)S(1)}, f32[8,128]{1,0:T(8,128)S(1)}, u32[]{:S(2)}, u32[]{:S(2)}) collective-permute-start(f32[8,128]{1,0:T(8,128)S(1)} %get-tuple-element.15), channel_id=1, source_target_pairs={{0,2},{1,3},{2,0},{3,1},{4,6},{5,7},{6,4},{7,5},{8,10},{9,11},{10,... | collective-permute-start | bytes 12296 | tf_op jit(solution)/shard_map/ppermute | solution.py:184
  12.0 0.0 copy-done
  12.0 0.4 %flux.1.partial = f32[1,5,4,16,128]{4,3,2,1,0:T(8,128)S(1)} custom-call(f32[1,5,4,16,128]{4,3,2,1,0:T(8,128)S(1)} %get-tuple-element.10.lam.refs_0_, f32[1,5,4,16,128]{4,3,2,1,0:T(8,128)S(1)} %get-tuple-element.11.source, f32[1,7,5,5,4,16,128]{6,5,4,3,2,1,0:T(8,128)S(1)} %copy-done), custom_call_target="tpu_custom_call" | custom-call | flops 2867200 | bytes 5734400 | tf_op jit(solution)/shard_map/flux/pallas_call | solution.py:229
  12.5 0.4 %collective-permute-done.2.refs_3_ = f32[1,5,4,16,128]{4,3,2,1,0:T(8,128)S(1)} collective-permute-done((f32[1,5,4,16,128]{4,3,2,1,0:T(8,128)}, f32[1,5,4,16,128]{4,3,2,1,0:T(8,128)S(1)}, u32[]{:S(2)}, u32[]{:S(2)}) %collective-permute-start.2) | collective-permute-done | bytes 163872 | tf_op jit(solution)/shard_map/ppermute | solution.py:184
  12.9 1.4 %collective-permute-done.1.refs_2_ = f32[1,5,4,16,128]{4,3,2,1,0:T(8,128)S(1)} collective-permute-done((f32[1,5,4,16,128]{4,3,2,1,0:T(8,128)}, f32[1,5,4,16,128]{4,3,2,1,0:T(8,128)S(1)}, u32[]{:S(2)}, u32[]{:S(2)}) %collective-permute-start.1) | collective-permute-done | bytes 163872 | tf_op jit(solution)/shard_map/ppermute | solution.py:184
  14.3 0.1 collective-permute-start.3
  14.4 1.3 %collective-permute-done.6 = f32[8,128]{1,0:T(8,128)S(1)} collective-permute-done((f32[8,128]{1,0:T(8,128)S(1)}, f32[8,128]{1,0:T(8,128)S(1)}, u32[]{:S(2)}, u32[]{:S(2)}) %collective-permute-start.6) | collective-permute-done | bytes 4128 | tf_op jit(solution)/shard_map/ppermute | solution.py:184
  15.6 0.0 collective-permute-done.4.near
  15.6 0.0 collective-permute-done.5.wrap
  15.6 0.1 own.1.partial
  15.7 0.0 collective-permute-done.3.mix
  15.8 0.8 %final.1 = (f32[1,5,4,16,128]{4,3,2,1,0:T(8,128)}, f32[1,40]{1,0:T(1,128)}) custom-call(f32[1,5,4,16,128]{4,3,2,1,0:T(8,128)S(1)} %own.1.partial, f32[4,16,128]{2,1,0:T(8,128)S(1)} %get-tuple-element.12.volume, f32[1,5,4,16,128]{4,3,2,1,0:T(8,128)S(1)} %collective-permute-done.3.mix, f32[88,128]{1,0:T(8,128)S(1)} %collective-permute-done.4.near, ...), custom_call_target="tpu_custom_call" | custom-call | tf_op jit(solution)/shard_map/final/pallas_call | solution.py:256
  (2 shorter events, 0.1 us)
Async XLA Ops:
  0.6 11.4 %copy-start = (f32[1,7,5,5,4,16,128]{6,5,4,3,2,1,0:T(8,128)S(1)}, f32[1,7,5,5,4,16,128]{6,5,4,3,2,1,0:T(8,128)}, u32[]{:S(2)}) copy-start(f32[1,7,5,5,4,16,128]{6,5,4,3,2,1,0:T(8,128)} %jac.3) | copy-start | bytes 17203204
  0.6 10.5 %collective-permute-start = (f32[1,5,4,16,128]{4,3,2,1,0:T(8,128)}, f32[1,5,4,16,128]{4,3,2,1,0:T(8,128)S(1)}, u32[]{:S(2)}, u32[]{:S(2)}) collective-permute-start(f32[1,5,4,16,128]{4,3,2,1,0:T(8,128)} %lam_in.1), channel_id=1, source_target_pairs={{0,8},{4,12},{8,0},{12,4},{16,24},{20,28},{24,16},{28,20},{1,9},{5... | collective-permute-start | bytes 491528 | tf_op jit(solution)/shard_map/ppermute | solution.py:184
  3.6 9.2 %collective-permute-start.2 = (f32[1,5,4,16,128]{4,3,2,1,0:T(8,128)}, f32[1,5,4,16,128]{4,3,2,1,0:T(8,128)S(1)}, u32[]{:S(2)}, u32[]{:S(2)}) collective-permute-start(f32[1,5,4,16,128]{4,3,2,1,0:T(8,128)} %lam_in.1), channel_id=1, source_target_pairs={{0,24},{4,28},{8,16},{12,20},{16,8},{20,12},{24,0},{28,4},{1,25},{... | collective-permute-start | bytes 491528 | tf_op jit(solution)/shard_map/ppermute | solution.py:184
  5.1 9.1 %collective-permute-start.1 = (f32[1,5,4,16,128]{4,3,2,1,0:T(8,128)}, f32[1,5,4,16,128]{4,3,2,1,0:T(8,128)S(1)}, u32[]{:S(2)}, u32[]{:S(2)}) collective-permute-start(f32[1,5,4,16,128]{4,3,2,1,0:T(8,128)} %lam_in.1), channel_id=1, source_target_pairs={{0,16},{4,20},{8,24},{12,28},{16,0},{20,4},{24,8},{28,12},{1,17},{... | collective-permute-start | bytes 491528 | tf_op jit(solution)/shard_map/ppermute | solution.py:184
  6.6 9.1 %collective-permute-start.4 = (f32[88,128]{1,0:T(8,128)S(1)}, f32[88,128]{1,0:T(8,128)S(1)}, u32[]{:S(2)}, u32[]{:S(2)}) collective-permute-start(f32[88,128]{1,0:T(8,128)S(1)} %get-tuple-element.13), channel_id=1, source_target_pairs={{0,1},{1,0},{2,3},{3,2},{4,5},{5,4},{6,7},{7,6},{8,9},{9,8},{10,11... | collective-permute-start | bytes 135176 | tf_op jit(solution)/shard_map/ppermute | solution.py:184
  8.7 7.0 %collective-permute-start.5 = (f32[88,128]{1,0:T(8,128)S(1)}, f32[88,128]{1,0:T(8,128)S(1)}, u32[]{:S(2)}, u32[]{:S(2)}) collective-permute-start(f32[88,128]{1,0:T(8,128)S(1)} %get-tuple-element.14), channel_id=1, source_target_pairs={{0,3},{1,2},{2,1},{3,0},{4,7},{5,6},{6,5},{7,4},{8,11},{9,10},{10,... | collective-permute-start | bytes 135176 | tf_op jit(solution)/shard_map/ppermute | solution.py:218
  11.1 4.5 %collective-permute-start.6 = (f32[8,128]{1,0:T(8,128)S(1)}, f32[8,128]{1,0:T(8,128)S(1)}, u32[]{:S(2)}, u32[]{:S(2)}) collective-permute-start(f32[8,128]{1,0:T(8,128)S(1)} %get-tuple-element.15), channel_id=1, source_target_pairs={{0,2},{1,3},{2,0},{3,1},{4,6},{5,7},{6,4},{7,5},{8,10},{9,11},{10,... | collective-permute-start | bytes 12296 | tf_op jit(solution)/shard_map/ppermute | solution.py:184
  14.3 1.5 %collective-permute-start.3 = (f32[1,5,4,16,128]{4,3,2,1,0:T(8,128)S(1)}, f32[1,5,4,16,128]{4,3,2,1,0:T(8,128)S(1)}, u32[]{:S(2)}, u32[]{:S(2)}) collective-permute-start(f32[1,5,4,16,128]{4,3,2,1,0:T(8,128)S(1)} %share.1), channel_id=1, source_target_pairs={{0,4},{4,0},{8,12},{12,8},{16,20},{20,16},{24,28},{28,24},{1,5},{5... | collective-permute-start | bytes 491528 | tf_op jit(solution)/shard_map/ppermute | solution.py:184

commit v2 on v1

--- a/solution.py
+++ b/solution.py
@@ -36,18 +36,16 @@
     return value
 
 
-def prep_kernel(
-    lam_in, source_in, volume_in, inward_in, outward_in, station_in, phi_in, stiff_in, jac,
-    near, wrap, packed, modes, lam, source, volume, inward,
-    block, outward, station, phi, inv_stiff, sem,
-):
+def prep_kernel(targets, sibling, lam_in, outward_in, station_in, phi_in, stiff_in, jac, near, wrap, packed, modes, lam, *refs):
+    blends, (planes, outward, station, phi, inv_stiff, sem) = refs[: len(targets)], refs[len(targets) :]
     nv, nx, ny, nz = lam.shape[1:]
+    count = lax.axis_size("inst")
+    me = lax.axis_index("inst")
     odd = lax.rem(lax.axis_index("space"), 2)
-    sides = (odd, 1 - odd)
-    moves = [(station_in, station), (phi_in, phi), (stiff_in, inv_stiff), (outward_in, outward), (lam_in, lam)]
+    sides = (1 - odd, odd)
+    moves = [(station_in, station), (phi_in, phi), (lam_in, lam), (outward_in, outward), (stiff_in, inv_stiff)]
     for slot, minus in enumerate(sides):
-        moves.append((jac.at[0, 1 + minus, :, :, (nx - 1) * (1 - minus)], block.at[slot]))
-    moves += [(source_in, source), (volume_in, volume), (inward_in, inward)]
+        moves.append((jac.at[0, 1 + minus, :, :, (nx - 1) * (1 - minus)], planes.at[slot]))
     copies = [pltpu.make_async_copy(src, dst, sem.at[i]) for i, (src, dst) in enumerate(moves)]
     for copy in copies:
         copy.start()
@@ -86,38 +84,36 @@
     packed[...] = tile
     near[nv * ny :, :] = tile
     wrap[nv * ny :, :] = tile
-    for slot, (minus, out) in enumerate(zip(sides, (near, wrap))):
+    for mask, blend in zip(targets, blends):
+        own = weight_of(count, me, me ^ mask)
+        other = weight_of(count, me ^ 1, me ^ mask)
+        blend[0] = own * lam[0] + other * sibling[0]
+    for slot, (minus, out) in enumerate(zip(sides, (wrap, near))):
         copies[5 + slot].wait()
         cells = lam[0, :, (nx - 1) * (1 - minus)]
         for j in range(nv):
-            total = block[slot, 0, j] * cells[0]
+            total = planes[slot, 0, j] * cells[0]
             for i in range(1, nv):
-                total = total + block[slot, i, j] * cells[i]
+                total = total + planes[slot, i, j] * cells[i]
             out[j * ny : (j + 1) * ny, :] = total
-    for copy in copies[7:]:
-        copy.wait()
-
-
-def share_kernel(masks, *refs):
-    held, out = refs[:-1], refs[-1]
+
+
+def mix_of(masks, blocks, target):
     count = lax.axis_size("inst")
     me = lax.axis_index("inst")
     total = None
-    for mask, block in zip(masks, held):
-        term = weight_of(count, me ^ mask, me ^ 1) * block[0]
+    for mask, block in zip(masks, blocks):
+        term = weight_of(count, me ^ mask, me ^ target) * block[0]
         total = term if total is None else total + term
-    out[0] = total
+    return total
+
+
+def share_kernel(masks, *refs):
+    refs[-1][0] = mix_of(masks, refs[:-1], 1)
 
 
 def own_kernel(masks, partial, volume, *refs):
-    held, out = refs[:-1], refs[-1]
-    count = lax.axis_size("inst")
-    me = lax.axis_index("inst")
-    total = None
-    for mask, block in zip(masks, held):
-        term = weight_of(count, me ^ mask, me) * block[0]
-        total = term if total is None else total + term
-    out[0] = volume[...][None] * total + partial[0]
+    refs[-1][0] = volume[...][None] * mix_of(masks, refs[:-1], 0) + partial[0]
 
 
 def flux_kernel(lam, source, jac, out):
@@ -145,7 +141,8 @@
             out[0, j, x] = total
 
 
-def final_kernel(partial, volume, mix, near, wrap, modal_tile, modes, surface_in, out, modal):
+def final_kernel(partial, volume, near, wrap, modal_tile, modes, surface_in, *refs):
+    mixes, (out, modal) = refs[:-2], refs[-2:]
     nv, nx, ny, nz = partial.shape[1:]
     groups = modal.shape[1] // 8
     odd = lax.rem(lax.axis_index("space"), 2)
@@ -165,7 +162,10 @@
             back = back + modes[x, 8 * group : 8 * group + 8, :] * column
         back = jnp.sum(back, axis=0, keepdims=True)
         for j in range(nv):
-            value = partial[0, j, x] + volume[x] * mix[0, j, x]
+            mixed = mixes[0][0, j, x]
+            for mix in mixes[1:]:
+                mixed = mixed + mix[0, j, x]
+            value = partial[0, j, x] + volume[x] * mixed
             rows = pl.ds(j * ny, ny)
             if x == 0:
                 value = value + jnp.where(is_odd, near[rows, :], wrap[rows, :])
@@ -186,35 +186,39 @@
     def like(array):
         return jax.ShapeDtypeStruct(array.shape, F32)
 
-    masks = tuple(range(0, count, 2))
-    foreign = [swap(adjoint, "inst", mask) for mask in masks[1:]]
+    def fast(array):
+        return pltpu.with_memory_space_constraint(array, pltpu.VMEM)
+
+    masks = [mask for mask in range(2, count, 2) if mask & (mask - 1) == 0]
+    targets = [mask for mask in range(2, count, 2) if mask & (mask - 1)]
+    sibling = swap(adjoint, "inst", 1)
+    foreign = [swap(adjoint, "inst", mask) for mask in masks]
     rows = nv * ny + 8
-    whole = (adjoint, source, volume, surface_in, surface_out, station, phi, inv_stiff.reshape(1, modes_k), jacobian)
-    near, wrap, packed, modes, lam, src, vol, inward = pl.pallas_call(
-        prep_kernel,
+    whole = (adjoint, surface_out, station, phi, inv_stiff.reshape(1, modes_k), jacobian)
+    near, wrap, packed, modes, lam, *blends = pl.pallas_call(
+        functools.partial(prep_kernel, targets),
         out_shape=(
             pltpu.VMEM((rows, nz), F32),
             pltpu.VMEM((rows, nz), F32),
             pltpu.VMEM((8, nz), F32),
             pltpu.VMEM((nx, modes_k, nz), F32),
             pltpu.VMEM(adjoint.shape, F32),
-            pltpu.VMEM(source.shape, F32),
-            pltpu.VMEM(volume.shape, F32),
-            pltpu.VMEM(surface_in.shape, F32),
-        ),
-        in_specs=[HBM] * 9,
-        out_specs=(VMEM,) * 8,
+        )
+        + (pltpu.VMEM(adjoint.shape, F32),) * len(targets),
+        in_specs=[VMEM] + [HBM] * len(whole),
+        out_specs=(VMEM,) * (5 + len(targets)),
         scratch_shapes=[
             pltpu.VMEM((2, nv, nv, ny, nz), F32),
             pltpu.VMEM(surface_out.shape, F32),
             pltpu.VMEM(station.shape, station.dtype),
             pltpu.VMEM(phi.shape, F32),
             pltpu.VMEM((1, modes_k), F32),
-            pltpu.SemaphoreType.DMA((10,)),
+            pltpu.SemaphoreType.DMA((7,)),
         ],
         compiler_params=pltpu.CompilerParams(vmem_limit_bytes=8 * 2**20),
         name="prep",
-    )(*(pltpu.with_memory_space_constraint(value, pltpu.HBM) for value in whole))
+    )(sibling, *(pltpu.with_memory_space_constraint(value, pltpu.HBM) for value in whole))
+    blends = [swap(blend, "inst", mask) for mask, blend in zip(targets, blends)]
     wrap_in = lax.ppermute(wrap, "space", [(i, (((i + 1) ^ 1) - 1) % slabs) for i in range(slabs)])
     near_in = swap(near, "space", 1)
     if slabs == 4:
@@ -234,8 +238,7 @@
         compiler_params=pltpu.CompilerParams(vmem_limit_bytes=16 * 2**20),
         cost_estimate=pl.CostEstimate(flops=2 * jacobian.size, bytes_accessed=4 * jacobian.size, transcendentals=0),
         name="flux",
-    )(lam, src, jacobian)
-    held = [lam] + foreign
+    )(lam, fast(source), fast(jacobian))
     share = pl.pallas_call(
         functools.partial(share_kernel, masks),
         out_shape=like(adjoint),
@@ -243,12 +246,14 @@
         out_specs=VMEM,
         compiler_params=pltpu.CompilerParams(vmem_limit_bytes=8 * 2**20),
         name="share",
-    )(*held)
-    mix = swap(share, "inst", 1)
+    )(*foreign)
+    mixes = [swap(share, "inst", 1)] + blends
+    vol = fast(volume)
+    held = [lam, sibling] + foreign
     partial = pl.pallas_call(
-        functools.partial(own_kernel, masks),
+        functools.partial(own_kernel, [0, 1] + masks),
         out_shape=like(adjoint),
-        in_specs=[VMEM] * (2 + len(masks)),
+        in_specs=[VMEM] * (2 + len(held)),
         out_specs=VMEM,
         compiler_params=pltpu.CompilerParams(vmem_limit_bytes=8 * 2**20),
         name="own",
@@ -256,11 +261,11 @@
     residual, modal = pl.pallas_call(
         final_kernel,
         out_shape=(like(adjoint), jax.ShapeDtypeStruct((1, modes_k), F32)),
-        in_specs=[VMEM] * 8,
+        in_specs=[VMEM] * (7 + len(mixes)),
         out_specs=(VMEM, VMEM),
         compiler_params=pltpu.CompilerParams(vmem_limit_bytes=8 * 2**20),
         name="final",
-    )(partial, vol, mix, near_in, wrap_in, tile, modes, inward)
+    )(partial, vol, near_in, wrap_in, tile, modes, fast(surface_in), *mixes)
     return residual, modal
 
 

time: 16.7 us -> 18.1 us (1.084)
  waiting for transfers between devices: 3.07 us -> 4.68 us
  starting transfers between devices: 10.1 us -> 9.9 us
    ppermute x6 -> x7, waiting for transfers between devices: 3.07 us -> 4.67 us  [swap(): return lax.ppermute(value, axis, [(i, i ^ mask) for i in range(size)])]
    ppermute x6 -> x7, starting transfers between devices: 7.63 us -> 7.43 us  [swap(): return lax.ppermute(value, axis, [(i, i ^ mask) for i in range(size)])]
  transfers between devices with their start and end apart: 7 -> 8, of which waited for: 3 -> 2; matrix products, arithmetic and copies ran while one was open for 0% -> 0% of each run, Pallas kernels for 11% -> 10%
where the time goes in v2:
time: 18.1 us; the launch traced here: 17.9 us
  starting transfers between devices  9.9 us (55%)
  waiting for transfers between devices  4.68 us (26%)
  Pallas kernels  2.62 us (14%)
  between operations  0.72 us (4%)
    ppermute x7, starting transfers between devices, swap(): return lax.ppermute(value, axis, [(i, i ^ mask) for i in range(size)])  7.43 us
    ppermute x7, waiting for transfers between devices, swap(): return lax.ppermute(value, axis, [(i, i ^ mask) for i in range(size)])  4.67 us
    ppermute x1, starting transfers between devices, body(): lax.ppermute(wrap, 'space', [(i, ((i + 1 ^ 1) - 1) % slabs) for i in rang...  2.48 us
    pallas_call x1, Pallas kernels, body(): pl.pallas_call(functools.partial(prep_kernel, targets), out_shape=(pltpu....  1.32 us
    pallas_call x1, Pallas kernels, body(): pl.pallas_call(final_kernel, out_shape=(like(adjoint), jax.ShapeDtypeStru...  0.77 us
    pallas_call x1, Pallas kernels, body(): pl.pallas_call(flux_kernel, out_shape=like(adjoint), in_specs=[VMEM] * 3,...  0.42 us
  transfers between devices with their start and end apart: 8, of which 2 were waited for; matrix products, arithmetic and copies ran while one was open for 0% of the time, Pallas kernels for 10%

profile of v2, /device:TPU:0, one launch (start us, length us, event | category | flops | bytes accessed | tf_op | source)
XLA Modules:
  0.0 17.9 jit_solution(434110378907452398)
XLA Ops:
  0.6 0.0 copy-start
  0.6 0.0 copy-start.1
  0.7 0.5 %collective-permute-start = (f32[1,5,4,16,128]{4,3,2,1,0:T(8,128)}, f32[1,5,4,16,128]{4,3,2,1,0:T(8,128)S(1)}, u32[]{:S(2)}, u32[]{:S(2)}) collective-permute-start(f32[1,5,4,16,128]{4,3,2,1,0:T(8,128)} %lam_in.1), channel_id=1, source_target_pairs={{0,4},{4,0},{8,12},{12,8},{16,20},{20,16},{24,28},{28,24},{1,5},{5... | collective-permute-start | bytes 491528 | tf_op jit(solution)/shard_map/ppermute | solution.py:184
  1.2 2.6 %collective-permute-start.1 = (f32[1,5,4,16,128]{4,3,2,1,0:T(8,128)}, f32[1,5,4,16,128]{4,3,2,1,0:T(8,128)S(1)}, u32[]{:S(2)}, u32[]{:S(2)}) collective-permute-start(f32[1,5,4,16,128]{4,3,2,1,0:T(8,128)} %lam_in.1), channel_id=1, source_target_pairs={{0,8},{4,12},{8,0},{12,4},{16,24},{20,28},{24,16},{28,20},{1,9},{5... | collective-permute-start | bytes 491528 | tf_op jit(solution)/shard_map/ppermute | solution.py:184
  3.7 1.5 %collective-permute-start.2 = (f32[1,5,4,16,128]{4,3,2,1,0:T(8,128)}, f32[1,5,4,16,128]{4,3,2,1,0:T(8,128)S(1)}, u32[]{:S(2)}, u32[]{:S(2)}) collective-permute-start(f32[1,5,4,16,128]{4,3,2,1,0:T(8,128)} %lam_in.1), channel_id=1, source_target_pairs={{0,16},{4,20},{8,24},{12,28},{16,0},{20,4},{24,8},{28,12},{1,17},{... | collective-permute-start | bytes 491528 | tf_op jit(solution)/shard_map/ppermute | solution.py:184
  5.3 0.0 collective-permute-done.sibling.refs_1_
  5.3 0.0 copy-start.2
  5.3 0.0 copy-start.3
  5.3 1.3 %prep.1 = (f32[88,128]{1,0:T(8,128)S(1)}, f32[88,128]{1,0:T(8,128)S(1)}, f32[8,128]{1,0:T(8,128)S(1)}, f32[4,40,128]{2,1,0:T(8,128)S(1)}, f32[1,5,4,16,128]{4,3,...) custom-call(f32[1,5,4,16,128]{4,3,2,1,0:T(8,128)S(1)} %collective-permute-done.sibling.refs_1_, ...), custom_call_target="tpu_custom_call" | custom-call | tf_op jit(solution)/shard_map/prep/pallas_call | solution.py:198
  6.6 1.6 %collective-permute-start.3 = (f32[88,128]{1,0:T(8,128)S(1)}, f32[88,128]{1,0:T(8,128)S(1)}, u32[]{:S(2)}, u32[]{:S(2)}) collective-permute-start(f32[88,128]{1,0:T(8,128)S(1)} %get-tuple-element.9), channel_id=1, source_target_pairs={{0,1},{1,0},{2,3},{3,2},{4,5},{5,4},{6,7},{7,6},{8,9},{9,8},{10,11... | collective-permute-start | bytes 135176 | tf_op jit(solution)/shard_map/ppermute | solution.py:184
  8.2 2.5 %collective-permute-start.4 = (f32[88,128]{1,0:T(8,128)S(1)}, f32[88,128]{1,0:T(8,128)S(1)}, u32[]{:S(2)}, u32[]{:S(2)}) collective-permute-start(f32[88,128]{1,0:T(8,128)S(1)} %get-tuple-element.10), channel_id=1, source_target_pairs={{0,3},{1,2},{2,1},{3,0},{4,7},{5,6},{6,5},{7,4},{8,11},{9,10},{10,... | collective-permute-start | bytes 135176 | tf_op jit(solution)/shard_map/ppermute | solution.py:222
  10.7 0.1 collective-permute-start.5
  10.8 0.0 collective-permute-done.1.refs_2_.refs_0_
  10.8 1.0 %collective-permute-start.7 = (f32[1,5,4,16,128]{4,3,2,1,0:T(8,128)S(1)}, f32[1,5,4,16,128]{4,3,2,1,0:T(8,128)S(1)}, u32[]{:S(2)}, u32[]{:S(2)}) collective-permute-start(f32[1,5,4,16,128]{4,3,2,1,0:T(8,128)S(1)} %get-tuple-element.13), channel_id=1, source_target_pairs={{0,24},{4,28},{8,16},{12,20},{16,8},{20,12},{24,0},{28,4},{1,25},{... | collective-permute-start | bytes 491528 | tf_op jit(solution)/shard_map/ppermute | solution.py:184
  11.8 0.0 collective-permute-done.2.refs_3_.refs_1_
  11.9 0.1 collective-permute-start.6
  12.0 0.0 copy-done
  12.0 0.0 copy-done.1
  12.0 0.4 %flux.1.partial = f32[1,5,4,16,128]{4,3,2,1,0:T(8,128)S(1)} custom-call(f32[1,5,4,16,128]{4,3,2,1,0:T(8,128)S(1)} %get-tuple-element.8.lam.refs_0_, f32[1,5,4,16,128]{4,3,2,1,0:T(8,128)S(1)} %copy-done.1, f32[1,7,5,5,4,16,128]{6,5,4,3,2,1,0:T(8,128)S(1)} %copy-done), custom_call_target="tpu_custom_call" | custom-call | flops 2867200 | bytes 5734400 | tf_op jit(solution)/shard_map/flux/pallas_call | solution.py:233
  12.4 0.0 copy-done.2
  12.4 0.1 own.1.partial
  12.5 2.7 %collective-permute-done.5 = f32[8,128]{1,0:T(8,128)S(1)} collective-permute-done((f32[8,128]{1,0:T(8,128)S(1)}, f32[8,128]{1,0:T(8,128)S(1)}, u32[]{:S(2)}, u32[]{:S(2)}) %collective-permute-start.5) | collective-permute-done | bytes 4128 | tf_op jit(solution)/shard_map/ppermute | solution.py:184
  15.2 0.0 collective-permute-done.3.near
  15.2 0.0 collective-permute-done.4.wrap
  15.2 1.9 %collective-permute-done.7.refs_1_ = f32[1,5,4,16,128]{4,3,2,1,0:T(8,128)S(1)} collective-permute-done((f32[1,5,4,16,128]{4,3,2,1,0:T(8,128)S(1)}, f32[1,5,4,16,128]{4,3,2,1,0:T(8,128)S(1)}, u32[]{:S(2)}, u32[]{:S(2)}) %collective-permute-start.7) | collective-permute-done | bytes 163872 | tf_op jit(solution)/shard_map/ppermute | solution.py:184
  17.2 0.0 collective-permute-done.6.refs_0_
  17.2 0.0 copy-done.3
  17.2 0.8 %final.1 = (f32[1,5,4,16,128]{4,3,2,1,0:T(8,128)}, f32[1,40]{1,0:T(1,128)}) custom-call(f32[1,5,4,16,128]{4,3,2,1,0:T(8,128)S(1)} %own.1.partial, f32[4,16,128]{2,1,0:T(8,128)S(1)} %copy-done.2, f32[88,128]{1,0:T(8,128)S(1)} %collective-permute-done.3.near, f32[88,128]{1,0:T(8,128)S(1)} %collective-permute-done.4.wrap, f32[8,128]{1,0:T(8,128)S(1)} %fusion.modal_tile, ...), custom_call_target="tpu_custom_call" | custom-call | tf_op jit(solution)/shard_map/final/pallas_call | solution.py:261
  (2 shorter events, 0.0 us)
Async XLA Ops:
  0.6 11.3 %copy-start = (f32[1,7,5,5,4,16,128]{6,5,4,3,2,1,0:T(8,128)S(1)}, f32[1,7,5,5,4,16,128]{6,5,4,3,2,1,0:T(8,128)}, u32[]{:S(2)}) copy-start(f32[1,7,5,5,4,16,128]{6,5,4,3,2,1,0:T(8,128)} %jac.3) | copy-start | bytes 17203204
  0.6 11.3 %copy-start.1 = (f32[1,5,4,16,128]{4,3,2,1,0:T(8,128)S(1)}, f32[1,5,4,16,128]{4,3,2,1,0:T(8,128)}, u32[]{:S(2)}) copy-start(f32[1,5,4,16,128]{4,3,2,1,0:T(8,128)} %source.1) | copy-start | bytes 491524
  0.7 4.6 %collective-permute-start = (f32[1,5,4,16,128]{4,3,2,1,0:T(8,128)}, f32[1,5,4,16,128]{4,3,2,1,0:T(8,128)S(1)}, u32[]{:S(2)}, u32[]{:S(2)}) collective-permute-start(f32[1,5,4,16,128]{4,3,2,1,0:T(8,128)} %lam_in.1), channel_id=1, source_target_pairs={{0,4},{4,0},{8,12},{12,8},{16,20},{20,16},{24,28},{28,24},{1,5},{5... | collective-permute-start | bytes 491528 | tf_op jit(solution)/shard_map/ppermute | solution.py:184
  1.2 9.7 %collective-permute-start.1 = (f32[1,5,4,16,128]{4,3,2,1,0:T(8,128)}, f32[1,5,4,16,128]{4,3,2,1,0:T(8,128)S(1)}, u32[]{:S(2)}, u32[]{:S(2)}) collective-permute-start(f32[1,5,4,16,128]{4,3,2,1,0:T(8,128)} %lam_in.1), channel_id=1, source_target_pairs={{0,8},{4,12},{8,0},{12,4},{16,24},{20,28},{24,16},{28,20},{1,9},{5... | collective-permute-start | bytes 491528 | tf_op jit(solution)/shard_map/ppermute | solution.py:184
  3.7 8.1 %collective-permute-start.2 = (f32[1,5,4,16,128]{4,3,2,1,0:T(8,128)}, f32[1,5,4,16,128]{4,3,2,1,0:T(8,128)S(1)}, u32[]{:S(2)}, u32[]{:S(2)}) collective-permute-start(f32[1,5,4,16,128]{4,3,2,1,0:T(8,128)} %lam_in.1), channel_id=1, source_target_pairs={{0,16},{4,20},{8,24},{12,28},{16,0},{20,4},{24,8},{28,12},{1,17},{... | collective-permute-start | bytes 491528 | tf_op jit(solution)/shard_map/ppermute | solution.py:184
  5.3 7.1 %copy-start.2 = (f32[4,16,128]{2,1,0:T(8,128)S(1)}, f32[4,16,128]{2,1,0:T(8,128)}, u32[]{:S(2)}) copy-start(f32[4,16,128]{2,1,0:T(8,128)} %volume.3) | copy-start | bytes 98308
  5.3 11.9 %copy-start.3 = (f32[5,4,128]{2,1,0:T(4,128)S(1)}, f32[5,4,128]{2,1,0:T(4,128)}, u32[]{:S(2)}) copy-start(f32[5,4,128]{2,1,0:T(4,128)} %surface_in.1) | copy-start | bytes 30724
  6.6 8.6 %collective-permute-start.3 = (f32[88,128]{1,0:T(8,128)S(1)}, f32[88,128]{1,0:T(8,128)S(1)}, u32[]{:S(2)}, u32[]{:S(2)}) collective-permute-start(f32[88,128]{1,0:T(8,128)S(1)} %get-tuple-element.9), channel_id=1, source_target_pairs={{0,1},{1,0},{2,3},{3,2},{4,5},{5,4},{6,7},{7,6},{8,9},{9,8},{10,11... | collective-permute-start | bytes 135176 | tf_op jit(solution)/shard_map/ppermute | solution.py:184
  8.2 7.0 %collective-permute-start.4 = (f32[88,128]{1,0:T(8,128)S(1)}, f32[88,128]{1,0:T(8,128)S(1)}, u32[]{:S(2)}, u32[]{:S(2)}) collective-permute-start(f32[88,128]{1,0:T(8,128)S(1)} %get-tuple-element.10), channel_id=1, source_target_pairs={{0,3},{1,2},{2,1},{3,0},{4,7},{5,6},{6,5},{7,4},{8,11},{9,10},{10,... | collective-permute-start | bytes 135176 | tf_op jit(solution)/shard_map/ppermute | solution.py:222
  10.7 4.5 %collective-permute-start.5 = (f32[8,128]{1,0:T(8,128)S(1)}, f32[8,128]{1,0:T(8,128)S(1)}, u32[]{:S(2)}, u32[]{:S(2)}) collective-permute-start(f32[8,128]{1,0:T(8,128)S(1)} %get-tuple-element.11), channel_id=1, source_target_pairs={{0,2},{1,3},{2,0},{3,1},{4,6},{5,7},{6,4},{7,5},{8,10},{9,11},{10,... | collective-permute-start | bytes 12296 | tf_op jit(solution)/shard_map/ppermute | solution.py:184
  10.8 6.3 %collective-permute-start.7 = (f32[1,5,4,16,128]{4,3,2,1,0:T(8,128)S(1)}, f32[1,5,4,16,128]{4,3,2,1,0:T(8,128)S(1)}, u32[]{:S(2)}, u32[]{:S(2)}) collective-permute-start(f32[1,5,4,16,128]{4,3,2,1,0:T(8,128)S(1)} %get-tuple-element.13), channel_id=1, source_target_pairs={{0,24},{4,28},{8,16},{12,20},{16,8},{20,12},{24,0},{28,4},{1,25},{... | collective-permute-start | bytes 491528 | tf_op jit(solution)/shard_map/ppermute | solution.py:184
  11.9 5.3 %collective-permute-start.6 = (f32[1,5,4,16,128]{4,3,2,1,0:T(8,128)S(1)}, f32[1,5,4,16,128]{4,3,2,1,0:T(8,128)S(1)}, u32[]{:S(2)}, u32[]{:S(2)}) collective-permute-start(f32[1,5,4,16,128]{4,3,2,1,0:T(8,128)S(1)} %share.1), channel_id=1, source_target_pairs={{0,4},{4,0},{8,12},{12,8},{16,20},{20,16},{24,28},{28,24},{1,5},{5... | collective-permute-start | bytes 491528 | tf_op jit(solution)/shard_map/ppermute | solution.py:184

commit v3 on v2

v3 whole, which is shorter than its diff:
```python
import functools
import math

import jax
import jax.numpy as jnp
import numpy as np
from jax import lax
from jax.experimental import pallas as pl
from jax.experimental.pallas import tpu as pltpu
from jax.sharding import PartitionSpec as P

VMEM = pl.BlockSpec(memory_space=pltpu.VMEM)
SMEM = pl.BlockSpec(memory_space=pltpu.SMEM)
F32 = jnp.float32
SMALL = pl.CostEstimate(flops=0, bytes_accessed=0, transcendentals=0)


def weight_table(count):
    table = []
    for k in range(count):
        if k == 0:
            first, second = 0.0, -(count * count + 2) / 12.0
        else:
            sign = 1.0 - 2.0 * (k % 2)
            sine = math.sin(math.pi * k / count)
            first = 0.5 * sign * math.cos(math.pi * k / count) / sine
            second = -0.5 * sign / (sine * sine)
        table.append(first - 0.25 * second)
    return np.asarray(table, np.float32)


def weight_of(count, source, target):
    gap = lax.rem(source - target + count, count)
    value = jnp.float32(0.0)
    for k, entry in enumerate(weight_table(count)):
        value = jnp.where(gap == k, jnp.float32(entry), value)
    return value


def table_kernel(out):
    count = lax.axis_size("inst")
    me = lax.axis_index("inst")
    for target in range(2):
        for mask in range(count):
            out[target, mask] = weight_of(count, me ^ mask, me ^ target)


def prep_kernel(targets, token, sibling, lam, outward, station, phi, inv_stiff, jac, near, wrap, packed, modes, *blends):
    nv, nx, ny, nz = lam.shape[1:]
    count = lax.axis_size("inst")
    me = lax.axis_index("inst")
    odd = lax.rem(lax.axis_index("space"), 2)
    for mask, blend in zip(targets, blends):
        own = weight_of(count, me, me ^ mask)
        other = weight_of(count, me ^ 1, me ^ mask)
        blend[0] = own * lam[0] + other * sibling[0]
    for minus, out in ((1 - odd, wrap), (odd, near)):
        plane = (nx - 1) * (1 - minus)
        for j in range(nv):
            total = jac[0, 1 + minus, 0, j, plane] * lam[0, 0, plane]
            for i in range(1, nv):
                total = total + jac[0, 1 + minus, i, j, plane] * lam[0, i, plane]
            out[j * ny : (j + 1) * ny, :] = total
    modes_k, stations = phi.shape
    full = phi[...]
    high = full.astype(jnp.bfloat16)
    rest = full - high.astype(F32)
    mid = rest.astype(jnp.bfloat16)
    low = (rest - mid.astype(F32)).astype(jnp.bfloat16)
    rows = lax.broadcasted_iota(jnp.int32, (stations, nz), 0)
    share = jnp.zeros((modes_k, nz), F32)
    for x in range(nx):
        hot = (rows == station[x : x + 1, :]).astype(F32).astype(jnp.bfloat16)
        at_face = (
            jnp.dot(low, hot, preferred_element_type=F32)
            + jnp.dot(mid, hot, preferred_element_type=F32)
            + jnp.dot(high, hot, preferred_element_type=F32)
        )
        modes[x] = at_face
        face = outward[0, x : x + 1, :] * lam[0, 0, x, 0:1, :]
        for j in range(1, nv):
            face = face + outward[j, x : x + 1, :] * lam[0, j, x, 0:1, :]
        share = share + at_face * face
    row = lax.broadcasted_iota(jnp.int32, (modes_k, modes_k), 0)
    lane = lax.broadcasted_iota(jnp.int32, (modes_k, modes_k), 1)
    stiff = jnp.sum(jnp.where(row == lane, inv_stiff[...], 0.0), axis=1, keepdims=True)
    column = jnp.sum(share, axis=1, keepdims=True) * stiff
    tile_lane = lax.broadcasted_iota(jnp.int32, (8, nz), 1)
    tile = jnp.zeros((8, nz), F32)
    for group in range(modes_k // 8):
        tile = jnp.where(tile_lane == group, column[8 * group : 8 * group + 8], tile)
    packed[...] = tile
    near[nv * ny :, :] = tile
    wrap[nv * ny :, :] = tile


def mix_of(masks, blocks, target):
    count = lax.axis_size("inst")
    me = lax.axis_index("inst")
    total = None
    for mask, block in zip(masks, blocks):
        term = weight_of(count, me ^ mask, me ^ target) * block[0]
        total = term if total is None else total + term
    return total


def share_kernel(masks, after, *refs):
    refs[-1][0] = mix_of(masks, refs[:-1], 1)


def own_kernel(masks, partial, volume, wrap, *refs):
    nv, nx, ny, nz = partial.shape[1:]
    held, blends, out = refs[: len(masks)], refs[len(masks) : -1], refs[-1]
    total = mix_of(masks, held, 0)
    for blend in blends:
        total = total + blend[0]
    out[0] = volume[...][None] * total + partial[0]
    plane = (nx - 1) * lax.rem(lax.axis_index("space"), 2)
    for j in range(nv):
        out[0, j, plane] = out[0, j, plane] + wrap[j * ny : (j + 1) * ny, :]


def flux_kernel(lam, source, jac, out):
    nv, nx, ny, nz = lam.shape[1:]
    y = lax.broadcasted_iota(jnp.int32, (ny, nz), 0)
    z = lax.broadcasted_iota(jnp.int32, (ny, nz), 1)

    def product(d, j, x):
        total = jac[0, d, 0, j, x] * lam[0, 0, x]
        for i in range(1, nv):
            total = total + jac[0, d, i, j, x] * lam[0, i, x]
        return total

    for j in range(nv):
        for x in range(nx):
            total = product(0, j, x) - source[0, j, x]
            if x > 0:
                total = total + product(1, j, x - 1)
            if x < nx - 1:
                total = total + product(2, j, x + 1)
            total = total + jnp.where(y == 0, 0.0, pltpu.roll(product(3, j, x), 1, 0))
            total = total + jnp.where(y == ny - 1, 0.0, pltpu.roll(product(4, j, x), ny - 1, 0))
            total = total + jnp.where(z == 0, 0.0, pltpu.roll(product(5, j, x), 1, 1))
            total = total + jnp.where(z == nz - 1, 0.0, pltpu.roll(product(6, j, x), nz - 1, 1))
            out[0, j, x] = total


def final_kernel(partial, volume, near, modes, surface_in, mix, *refs):
    tiles, (out, modal) = refs[:-2], refs[-2:]
    nv, nx, ny, nz = partial.shape[1:]
    groups = modal.shape[1] // 8
    even = lax.rem(lax.axis_index("space"), 2) == 0
    tile = sum(ref[ref.shape[0] - 8 :, :] for ref in tiles)
    columns = [tile[:, group : group + 1] for group in range(groups)]
    line = None
    for group, column in enumerate(columns):
        row = lax.broadcasted_iota(jnp.int32, (8, 8 * groups), 0)
        lane = lax.broadcasted_iota(jnp.int32, (8, 8 * groups), 1)
        piece = jnp.sum(jnp.where(lane == row + 8 * group, column, 0.0), axis=0, keepdims=True)
        line = piece if line is None else line + piece
    modal[...] = line
    low = lax.broadcasted_iota(jnp.int32, (ny, nz), 0) == 0
    for x in range(nx):
        back = jnp.zeros((8, nz), F32)
        for group, column in enumerate(columns):
            back = back + modes[x, 8 * group : 8 * group + 8, :] * column
        back = jnp.sum(back, axis=0, keepdims=True)
        for j in range(nv):
            value = partial[0, j, x] + volume[x] * mix[0, j, x]
            if x == 0 or x == nx - 1:
                border = near[j * ny : (j + 1) * ny, :]
                value = value + jnp.where(even if x else jnp.logical_not(even), border, 0.0)
            out[0, j, x] = value + jnp.where(low, surface_in[j, x : x + 1, :] * back, 0.0)


def body(adjoint, jacobian, volume, source, surface_out, surface_in, station, phi, inv_stiff):
    count, slabs = lax.axis_size("inst"), lax.axis_size("space")
    nv, nx, ny, nz = adjoint.shape[1:]
    modes_k = phi.shape[0]

    def swap(value, axis, mask):
        size = lax.axis_size(axis)
        return lax.ppermute(value, axis, [(i, i ^ mask) for i in range(size)])

    def like(array):
        return jax.ShapeDtypeStruct(array.shape, F32)

    def fast(array):
        return pltpu.with_memory_space_constraint(array, pltpu.VMEM)

    masks = [mask for mask in range(2, count, 2) if mask & (mask - 1) == 0]
    targets = [mask for mask in range(2, count, 2) if mask & (mask - 1)]
    sibling = swap(adjoint, "inst", 1)
    foreign = [swap(adjoint, "inst", mask) for mask in masks]
    rows = nv * ny + 8
    lam, jac = fast(adjoint), fast(jacobian)
    weights = pl.pallas_call(
        table_kernel,
        out_shape=pltpu.SMEM((2, count), F32),
        out_specs=SMEM,
        cost_estimate=pl.CostEstimate(flops=2**31, bytes_accessed=0, transcendentals=0),
        name="table",
    )()
    near, wrap, packed, modes, *blends = pl.pallas_call(
        functools.partial(prep_kernel, targets),
        out_shape=(
            pltpu.VMEM((rows, nz), F32),
            pltpu.VMEM((rows, nz), F32),
            pltpu.VMEM((8, nz), F32),
            pltpu.VMEM((nx, modes_k, nz), F32),
        )
        + (pltpu.VMEM(adjoint.shape, F32),) * len(targets),
        in_specs=[SMEM] + [VMEM] * 7,
        out_specs=(VMEM,) * (4 + len(targets)),
        compiler_params=pltpu.CompilerParams(vmem_limit_bytes=8 * 2**20),
        name="prep",
    )(weights, sibling, lam, fast(surface_out), fast(station), fast(phi), fast(inv_stiff.reshape(1, modes_k)), jac)
    blends = [swap(blend, "inst", mask) for mask, blend in zip(targets, blends)]
    wrap_in = lax.ppermute(wrap, "space", [(i, (((i + 1) ^ 1) - 1) % slabs) for i in range(slabs)])
    near_in = swap(near, "space", 1)
    if slabs == 4:
        tiles = [packed, near_in, wrap_in, swap(packed, "space", 2)]
    else:
        tile = packed + near_in[nv * ny :]
        step = 2
        while step < slabs:
            tile = tile + swap(tile, "space", step)
            step *= 2
        tiles = [tile]
    partial = pl.pallas_call(
        flux_kernel,
        out_shape=like(adjoint),
        in_specs=[VMEM] * 3,
        out_specs=VMEM,
        compiler_params=pltpu.CompilerParams(vmem_limit_bytes=16 * 2**20),
        cost_estimate=pl.CostEstimate(flops=2 * jacobian.size, bytes_accessed=4 * jacobian.size, transcendentals=0),
        name="flux",
    )(lam, fast(source), jac)
    share = pl.pallas_call(
        functools.partial(share_kernel, masks),
        out_shape=like(adjoint),
        in_specs=[pl.BlockSpec(memory_space=pl.ANY)] + [VMEM] * len(masks),
        out_specs=VMEM,
        compiler_params=pltpu.CompilerParams(vmem_limit_bytes=8 * 2**20),
        cost_estimate=SMALL,
        name="share",
    )(partial, *foreign)
    mix = swap(share, "inst", 1)
    vol = fast(volume)
    held = [lam, sibling] + foreign
    partial = pl.pallas_call(
        functools.partial(own_kernel, [0, 1] + masks),
        out_shape=like(adjoint),
        in_specs=[VMEM] * (3 + len(held) + len(blends)),
        out_specs=VMEM,
        compiler_params=pltpu.CompilerParams(vmem_limit_bytes=8 * 2**20),
        cost_estimate=pl.CostEstimate(flops=2**31, bytes_accessed=0, transcendentals=0),
        name="own",
    )(partial, vol, wrap_in, *held, *blends)
    residual, modal = pl.pallas_call(
        final_kernel,
        out_shape=(like(adjoint), jax.ShapeDtypeStruct((1, modes_k), F32)),
        in_specs=[VMEM] * (6 + len(tiles)),
        out_specs=(VMEM, VMEM),
        compiler_params=pltpu.CompilerParams(vmem_limit_bytes=8 * 2**20),
        name="final",
    )(partial, vol, near_in, modes, fast(surface_in), mix, *tiles)
    return residual, modal


def solution(mesh):
    placed = (
        P("inst", None, "space", None, None),
        P("inst", None, None, None, "space", None, None),
        P("space", None, None),
        P("inst", None, "space", None, None),
        P(None, "space", None),
        P(None, "space", None),
        P("space", None),
        P(),
        P(),
    )
    return jax.shard_map(
        body,
        mesh=mesh,
        in_specs=placed,
        out_specs=(P("inst", None, "space", None, None), P("inst", None)),
        check_vma=False,
    )
```

time: 18.1 us -> 18.9 us (1.044)
  local copies, waits for them, and re-layouts: 0.02 us -> 2.66 us
  waiting for transfers between devices: 4.68 us -> 2.45 us
  starting transfers between devices: 9.9 us -> 11.1 us
  Pallas kernels: 2.62 us -> 1.7 us
    unnamed x8 -> x20, local copies, waits for them, and re-layouts: 0.02 us -> 2.66 us
    ppermute x7, waiting for transfers between devices: 4.67 us -> 2.45 us  [swap(): return lax.ppermute(value, axis, [(i, i ^ mask) for i in range(size)])]
    ppermute x1, starting transfers between devices: 2.48 us -> 3.6 us  [body(): lax.ppermute(wrap, 'space', [(i, ((i + 1 ^ 1) - 1) % slabs) for i in rang...]
    pallas_call x1, Pallas kernels: 1.32 us -> 0.37 us  [body(): pl.pallas_call(functools.partial(prep_kernel, targets), out_shape=(pltpu....]
  transfers between devices with their start and end apart: 8 -> 8, of which waited for: 2 -> 1; matrix products, arithmetic and copies ran while one was open for 0% -> 0% of each run, Pallas kernels for 10% -> 5%
where the time goes in v3:
time: 18.9 us; the launch traced here: 18.7 us
  starting transfers between devices  11.1 us (59%)
  local copies, waits for them, and re-layouts  2.66 us (14%)
  waiting for transfers between devices  2.45 us (13%)
  Pallas kernels  1.7 us (9%)
  between operations  0.79 us (4%)
    ppermute x7, starting transfers between devices, swap(): return lax.ppermute(value, axis, [(i, i ^ mask) for i in range(size)])  7.54 us
    ppermute x1, starting transfers between devices, body(): lax.ppermute(wrap, 'space', [(i, ((i + 1 ^ 1) - 1) % slabs) for i in rang...  3.6 us
    unnamed x20, local copies, waits for them, and re-layouts  2.66 us
    ppermute x7, waiting for transfers between devices, swap(): return lax.ppermute(value, axis, [(i, i ^ mask) for i in range(size)])  2.45 us
    pallas_call x1, Pallas kernels, body(): pl.pallas_call(final_kernel, out_shape=(like(adjoint), jax.ShapeDtypeStru...  0.77 us
    pallas_call x1, Pallas kernels, body(): pl.pallas_call(flux_kernel, out_shape=like(adjoint), in_specs=[VMEM] * 3,...  0.42 us
  transfers between devices with their start and end apart: 8, of which 1 were waited for; matrix products, arithmetic and copies ran while one was open for 0% of the time, Pallas kernels for 5%

profile of v3, /device:TPU:0, one launch (start us, length us, event | category | flops | bytes accessed | tf_op | source)
XLA Modules:
  0.0 18.7 jit_solution(8394019382576452983)
XLA Ops:
  0.6 0.0 copy-start.2
  0.6 0.0 copy-start.9
  0.7 0.0 copy-start.6
  0.7 0.0 copy-start.8
  0.7 0.0 copy-start.4
  0.7 0.0 copy-start.3
  0.7 0.5 %collective-permute-start = (f32[1,5,4,16,128]{4,3,2,1,0:T(8,128)}, f32[1,5,4,16,128]{4,3,2,1,0:T(8,128)S(1)}, u32[]{:S(2)}, u32[]{:S(2)}) collective-permute-start(f32[1,5,4,16,128]{4,3,2,1,0:T(8,128)} %refs_0_.1), channel_id=1, source_target_pairs={{0,4},{4,0},{8,12},{12,8},{16,20},{20,16},{24,28},{28,24},{1,5},{5... | collective-permute-start | bytes 491528 | tf_op jit(solution)/shard_map/ppermute | solution.py:183
  1.2 2.6 %collective-permute-start.2 = (f32[1,5,4,16,128]{4,3,2,1,0:T(8,128)}, f32[1,5,4,16,128]{4,3,2,1,0:T(8,128)S(1)}, u32[]{:S(2)}, u32[]{:S(2)}) collective-permute-start(f32[1,5,4,16,128]{4,3,2,1,0:T(8,128)} %refs_0_.1), channel_id=1, source_target_pairs={{0,8},{4,12},{8,0},{12,4},{16,24},{20,28},{24,16},{28,20},{1,9},{5... | collective-permute-start | bytes 491528 | tf_op jit(solution)/shard_map/ppermute | solution.py:183
  3.8 1.5 %collective-permute-start.3 = (f32[1,5,4,16,128]{4,3,2,1,0:T(8,128)}, f32[1,5,4,16,128]{4,3,2,1,0:T(8,128)S(1)}, u32[]{:S(2)}, u32[]{:S(2)}) collective-permute-start(f32[1,5,4,16,128]{4,3,2,1,0:T(8,128)} %refs_0_.1), channel_id=1, source_target_pairs={{0,16},{4,20},{8,24},{12,28},{16,0},{20,4},{24,8},{28,12},{1,17},{... | collective-permute-start | bytes 491528 | tf_op jit(solution)/shard_map/ppermute | solution.py:183
  5.3 0.0 collective-permute-done.sibling.refs_1_
  5.3 0.0 copy-done.2
  5.3 0.0 copy-done.9
  5.3 0.0 copy-start
  5.3 2.6 %copy-done = f32[1,7,5,5,4,16,128]{6,5,4,3,2,1,0:T(8,128)S(1)} copy-done((f32[1,7,5,5,4,16,128]{6,5,4,3,2,1,0:T(8,128)S(1)}, f32[1,7,5,5,4,16,128]{6,5,4,3,2,1,0:T(8,128)}, u32[]{:S(2)}) %copy-start) | copy-done | bytes 5734424
  8.0 0.4 %prep.1 = (f32[88,128]{1,0:T(8,128)S(1)}, f32[88,128]{1,0:T(8,128)S(1)}, f32[8,128]{1,0:T(8,128)S(1)}, f32[4,40,128]{2,1,0:T(8,128)S(1)}, f32[1,5,4,16,128]{4,3,2,1,0:T(8,128)S(1)}) custom-call(f32[2,8]{1,0:T(2,128)S(4)} %table.1.token, f32[1,5,4,16,128]{4,3,2,1,0:T(8,128)S(1)} %collective-permute-done.sibling.refs_1_, f32[1,5,4,16,128]{4,3,2,1,0:T(8,128)S(1)} %copy-done.2, ...), custom_call_target="tpu_custom_call" | custom-call | tf_op jit(solution)/shard_map/prep/pallas_call | solution.py:204
  8.3 1.0 %collective-permute-start.4 = (f32[1,5,4,16,128]{4,3,2,1,0:T(8,128)S(1)}, f32[1,5,4,16,128]{4,3,2,1,0:T(8,128)S(1)}, u32[]{:S(2)}, u32[]{:S(2)}) collective-permute-start(f32[1,5,4,16,128]{4,3,2,1,0:T(8,128)S(1)} %get-tuple-element.8), channel_id=1, source_target_pairs={{0,24},{4,28},{8,16},{12,20},{16,8},{20,12},{24,0},{28,4},{1,25},{... | collective-permute-start | bytes 491528 | tf_op jit(solution)/shard_map/ppermute | solution.py:183
  9.3 3.6 %collective-permute-start.1 = (f32[88,128]{1,0:T(8,128)S(1)}, f32[88,128]{1,0:T(8,128)S(1)}, u32[]{:S(2)}, u32[]{:S(2)}) collective-permute-start(f32[88,128]{1,0:T(8,128)S(1)} %get-tuple-element.7), channel_id=1, source_target_pairs={{0,3},{1,2},{2,1},{3,0},{4,7},{5,6},{6,5},{7,4},{8,11},{9,10},{10,... | collective-permute-start | bytes 135176 | tf_op jit(solution)/shard_map/ppermute | solution.py:219
  13.0 0.4 %flux.1.partial.after = f32[1,5,4,16,128]{4,3,2,1,0:T(8,128)S(1)} custom-call(f32[1,5,4,16,128]{4,3,2,1,0:T(8,128)S(1)} %copy-done.2, f32[1,5,4,16,128]{4,3,2,1,0:T(8,128)S(1)} %copy-done.3, f32[1,7,5,5,4,16,128]{6,5,4,3,2,1,0:T(8,128)S(1)} %copy-done.1), custom_call_target="tpu_custom_call" | custom-call | flops 2867200 | bytes 5734400 | tf_op jit(solution)/shard_map/flux/pallas_call | solution.py:230
  13.4 0.0 copy-start.7
  13.4 0.3 %collective-permute-start.7 = (f32[8,128]{1,0:T(8,128)S(1)}, f32[8,128]{1,0:T(8,128)S(1)}, u32[]{:S(2)}, u32[]{:S(2)}) collective-permute-start(f32[8,128]{1,0:T(8,128)S(1)} %get-tuple-element.11.refs_0_), channel_id=1, source_target_pairs={{0,2},{1,3},{2,0},{3,1},{4,6},{5,7},{6,4},{7,5},{8,10},{9,11},{10,... | collective-permute-start | bytes 12296 | tf_op jit(solution)/shard_map/ppermute | solution.py:183
  13.7 0.0 collective-permute-done.2.refs_2_.refs_0_
  13.7 1.6 %collective-permute-start.5 = (f32[88,128]{1,0:T(8,128)S(1)}, f32[88,128]{1,0:T(8,128)S(1)}, u32[]{:S(2)}, u32[]{:S(2)}) collective-permute-start(f32[88,128]{1,0:T(8,128)S(1)} %get-tuple-element.9), channel_id=1, source_target_pairs={{0,1},{1,0},{2,3},{3,2},{4,5},{5,4},{6,7},{7,6},{8,9},{9,8},{10,11... | collective-permute-start | bytes 135176 | tf_op jit(solution)/shard_map/ppermute | solution.py:183
  15.3 0.0 collective-permute-done.3.refs_3_.refs_1_
  15.3 0.1 collective-permute-start.6
  15.4 0.0 collective-permute-done.1.wrap.refs_2_
  15.4 0.0 collective-permute-done.4.refs_4_
  15.4 0.0 copy-done.5
  15.4 0.1 own.1.partial
  15.5 2.4 %collective-permute-done.7.refs_3_ = f32[8,128]{1,0:T(8,128)S(1)} collective-permute-done((f32[8,128]{1,0:T(8,128)S(1)}, f32[8,128]{1,0:T(8,128)S(1)}, u32[]{:S(2)}, u32[]{:S(2)}) %collective-permute-start.7) | collective-permute-done | bytes 4128 | tf_op jit(solution)/shard_map/ppermute | solution.py:183
  18.0 0.0 collective-permute-done.5.near.refs_1_
  18.0 0.0 collective-permute-done.6.mix
  18.0 0.8 %final.1 = (f32[1,5,4,16,128]{4,3,2,1,0:T(8,128)}, f32[1,40]{1,0:T(1,128)}) custom-call(f32[1,5,4,16,128]{4,3,2,1,0:T(8,128)S(1)} %own.1.partial, f32[4,16,128]{2,1,0:T(8,128)S(1)} %copy-done.5, f32[88,128]{1,0:T(8,128)S(1)} %collective-permute-done.5.near.refs_1_, f32[4,40,128]{2,1,0:T(8,128)S(1)} %get-tuple-element.10.modes, f32[5,4,128]{2,1,0:T(4,128)S(1)} %copy-done.7, ...), custom_call_target="tpu_custom_call" | custom-call | tf_op jit(solution)/shard_map/final/pallas_call | solution.py:260
  (10 shorter events, 0.1 us)
Async XLA Ops:
  0.6 4.7 %copy-start.2 = (f32[1,5,4,16,128]{4,3,2,1,0:T(8,128)S(1)}, f32[1,5,4,16,128]{4,3,2,1,0:T(8,128)}, u32[]{:S(2)}) copy-start(f32[1,5,4,16,128]{4,3,2,1,0:T(8,128)} %refs_0_.1) | copy-start | bytes 491524
  0.6 4.7 %copy-start.9 = (f32[40]{0:T(128)S(1)}, f32[40]{0:T(128)}, u32[]{:S(2)}) copy-start(f32[40]{0:T(128)} %param.17) | copy-start | bytes 484
  0.7 4.7 %copy-start.6 = (f32[5,4,128]{2,1,0:T(4,128)S(1)}, f32[5,4,128]{2,1,0:T(4,128)}, u32[]{:S(2)}) copy-start(f32[5,4,128]{2,1,0:T(4,128)} %outward.1) | copy-start | bytes 30724
  0.7 4.7 %copy-start.8 = (s32[4,128]{1,0:T(4,128)S(1)}, s32[4,128]{1,0:T(4,128)}, u32[]{:S(2)}) copy-start(s32[4,128]{1,0:T(4,128)} %station.1) | copy-start | bytes 6148
  0.7 4.7 %copy-start.4 = (f32[40,256]{1,0:T(8,128)S(1)}, f32[40,256]{1,0:T(8,128)}, u32[]{:S(2)}) copy-start(f32[40,256]{1,0:T(8,128)} %phi.1) | copy-start | bytes 122884
  0.7 12.3 %copy-start.3 = (f32[1,5,4,16,128]{4,3,2,1,0:T(8,128)S(1)}, f32[1,5,4,16,128]{4,3,2,1,0:T(8,128)}, u32[]{:S(2)}) copy-start(f32[1,5,4,16,128]{4,3,2,1,0:T(8,128)} %source.1) | copy-start | bytes 491524
  0.7 4.6 %collective-permute-start = (f32[1,5,4,16,128]{4,3,2,1,0:T(8,128)}, f32[1,5,4,16,128]{4,3,2,1,0:T(8,128)S(1)}, u32[]{:S(2)}, u32[]{:S(2)}) collective-permute-start(f32[1,5,4,16,128]{4,3,2,1,0:T(8,128)} %refs_0_.1), channel_id=1, source_target_pairs={{0,4},{4,0},{8,12},{12,8},{16,20},{20,16},{24,28},{28,24},{1,5},{5... | collective-permute-start | bytes 491528 | tf_op jit(solution)/shard_map/ppermute | solution.py:183
  1.2 12.5 %collective-permute-start.2 = (f32[1,5,4,16,128]{4,3,2,1,0:T(8,128)}, f32[1,5,4,16,128]{4,3,2,1,0:T(8,128)S(1)}, u32[]{:S(2)}, u32[]{:S(2)}) collective-permute-start(f32[1,5,4,16,128]{4,3,2,1,0:T(8,128)} %refs_0_.1), channel_id=1, source_target_pairs={{0,8},{4,12},{8,0},{12,4},{16,24},{20,28},{24,16},{28,20},{1,9},{5... | collective-permute-start | bytes 491528 | tf_op jit(solution)/shard_map/ppermute | solution.py:183
  3.8 11.5 %collective-permute-start.3 = (f32[1,5,4,16,128]{4,3,2,1,0:T(8,128)}, f32[1,5,4,16,128]{4,3,2,1,0:T(8,128)S(1)}, u32[]{:S(2)}, u32[]{:S(2)}) collective-permute-start(f32[1,5,4,16,128]{4,3,2,1,0:T(8,128)} %refs_0_.1), channel_id=1, source_target_pairs={{0,16},{4,20},{8,24},{12,28},{16,0},{20,4},{24,8},{28,12},{1,17},{... | collective-permute-start | bytes 491528 | tf_op jit(solution)/shard_map/ppermute | solution.py:183
  5.3 2.6 %copy-start = (f32[1,7,5,5,4,16,128]{6,5,4,3,2,1,0:T(8,128)S(1)}, f32[1,7,5,5,4,16,128]{6,5,4,3,2,1,0:T(8,128)}, u32[]{:S(2)}) copy-start(f32[1,7,5,5,4,16,128]{6,5,4,3,2,1,0:T(8,128)} %jac.3) | copy-start | bytes 17203204
  8.0 5.0 %copy-start.1 = (f32[1,7,5,5,4,16,128]{6,5,4,3,2,1,0:T(8,128)S(1)}, f32[1,7,5,5,4,16,128]{6,5,4,3,2,1,0:T(8,128)}, u32[]{:S(2)}) copy-start(f32[1,7,5,5,4,16,128]{6,5,4,3,2,1,0:T(8,128)} %jac.3) | copy-start | bytes 17203204
  8.0 7.4 %copy-start.5 = (f32[4,16,128]{2,1,0:T(8,128)S(1)}, f32[4,16,128]{2,1,0:T(8,128)}, u32[]{:S(2)}) copy-start(f32[4,16,128]{2,1,0:T(8,128)} %volume.3) | copy-start | bytes 98308
  8.3 7.1 %collective-permute-start.4 = (f32[1,5,4,16,128]{4,3,2,1,0:T(8,128)S(1)}, f32[1,5,4,16,128]{4,3,2,1,0:T(8,128)S(1)}, u32[]{:S(2)}, u32[]{:S(2)}) collective-permute-start(f32[1,5,4,16,128]{4,3,2,1,0:T(8,128)S(1)} %get-tuple-element.8), channel_id=1, source_target_pairs={{0,24},{4,28},{8,16},{12,20},{16,8},{20,12},{24,0},{28,4},{1,25},{... | collective-permute-start | bytes 491528 | tf_op jit(solution)/shard_map/ppermute | solution.py:183
  9.3 6.0 %collective-permute-start.1 = (f32[88,128]{1,0:T(8,128)S(1)}, f32[88,128]{1,0:T(8,128)S(1)}, u32[]{:S(2)}, u32[]{:S(2)}) collective-permute-start(f32[88,128]{1,0:T(8,128)S(1)} %get-tuple-element.7), channel_id=1, source_target_pairs={{0,3},{1,2},{2,1},{3,0},{4,7},{5,6},{6,5},{7,4},{8,11},{9,10},{10,... | collective-permute-start | bytes 135176 | tf_op jit(solution)/shard_map/ppermute | solution.py:219
  13.4 4.6 %copy-start.7 = (f32[5,4,128]{2,1,0:T(4,128)S(1)}, f32[5,4,128]{2,1,0:T(4,128)}, u32[]{:S(2)}) copy-start(f32[5,4,128]{2,1,0:T(4,128)} %surface_in.1) | copy-start | bytes 30724
  13.4 4.6 %collective-permute-start.7 = (f32[8,128]{1,0:T(8,128)S(1)}, f32[8,128]{1,0:T(8,128)S(1)}, u32[]{:S(2)}, u32[]{:S(2)}) collective-permute-start(f32[8,128]{1,0:T(8,128)S(1)} %get-tuple-element.11.refs_0_), channel_id=1, source_target_pairs={{0,2},{1,3},{2,0},{3,1},{4,6},{5,7},{6,4},{7,5},{8,10},{9,11},{10,... | collective-permute-start | bytes 12296 | tf_op jit(solution)/shard_map/ppermute | solution.py:183
  13.7 4.3 %collective-permute-start.5 = (f32[88,128]{1,0:T(8,128)S(1)}, f32[88,128]{1,0:T(8,128)S(1)}, u32[]{:S(2)}, u32[]{:S(2)}) collective-permute-start(f32[88,128]{1,0:T(8,128)S(1)} %get-tuple-element.9), channel_id=1, source_target_pairs={{0,1},{1,0},{2,3},{3,2},{4,5},{5,4},{6,7},{7,6},{8,9},{9,8},{10,11... | collective-permute-start | bytes 135176 | tf_op jit(solution)/shard_map/ppermute | solution.py:183
  15.3 2.7 %collective-permute-start.6 = (f32[1,5,4,16,128]{4,3,2,1,0:T(8,128)S(1)}, f32[1,5,4,16,128]{4,3,2,1,0:T(8,128)S(1)}, u32[]{:S(2)}, u32[]{:S(2)}) collective-permute-start(f32[1,5,4,16,128]{4,3,2,1,0:T(8,128)S(1)} %share.1), channel_id=1, source_target_pairs={{0,4},{4,0},{8,12},{12,8},{16,20},{20,16},{24,28},{28,24},{1,5},{5... | collective-permute-start | bytes 491528 | tf_op jit(solution)/shard_map/ppermute | solution.py:183

commit v4 on v3

v4 whole, which is shorter than its diff:
```python
import functools
import math

import jax
import jax.numpy as jnp
import numpy as np
from jax import lax
from jax.experimental import pallas as pl
from jax.experimental.pallas import tpu as pltpu
from jax.sharding import PartitionSpec as P

VMEM = pl.BlockSpec(memory_space=pltpu.VMEM)
SMEM = pl.BlockSpec(memory_space=pltpu.SMEM)
ANY = pl.BlockSpec(memory_space=pl.ANY)
F32 = jnp.float32


def weight_values(count):
    table = []
    for k in range(count):
        if k == 0:
            first, second = 0.0, -(count * count + 2) / 12.0
        else:
            sign = 1.0 - 2.0 * (k % 2)
            sine = math.sin(math.pi * k / count)
            first = 0.5 * sign * math.cos(math.pi * k / count) / sine
            second = -0.5 * sign / (sine * sine)
        table.append(first - 0.25 * second)
    return np.asarray(table, np.float32)


def weight_of(count, source, target):
    gap = lax.rem(source - target + count, count)
    value = jnp.float32(0.0)
    for k, entry in enumerate(weight_values(count)):
        value = jnp.where(gap == k, jnp.float32(entry), value)
    return value


def raw_masks(count):
    steps = [mask for mask in range(2, count, 2) if mask & (mask - 1) == 0]
    others = [mask for mask in range(2, count, 2) if mask & (mask - 1)]
    return [(steps[k], steps[(k + 1) % len(steps)]) for k in range(len(steps))] + [(mask, mask) for mask in others]


def held_masks(me):
    pairs = raw_masks(lax.axis_size("inst"))
    core = lax.rem(me, 2)
    return [0] + [a if a == b else jnp.where(core == 0, a, b) for a, b in pairs]


def table_kernel(out):
    me = lax.axis_index("inst")
    out[0, 0] = weight_of(lax.axis_size("inst"), me, me)


def prep_kernel(token, lam, outward, station, phi, inv_stiff, jac, near, wrap, packed, modes):
    nv, nx, ny, nz = lam.shape[1:]
    odd = lax.rem(lax.axis_index("space"), 2)

    def columns(j, carry):
        for minus, out in ((1 - odd, wrap), (odd, near)):
            plane = (nx - 1) * (1 - minus)
            total = jac[0, 1 + minus, 0, j, plane] * lam[0, 0, plane]
            for i in range(1, nv):
                total = total + jac[0, 1 + minus, i, j, plane] * lam[0, i, plane]
            out[pl.ds(pl.multiple_of(j * ny, ny), ny), :] = total
        return carry

    modes_k, stations = phi.shape
    full = phi[...]
    high = full.astype(jnp.bfloat16)
    rest = full - high.astype(F32)
    mid = rest.astype(jnp.bfloat16)
    low = (rest - mid.astype(F32)).astype(jnp.bfloat16)
    pieces = jnp.concatenate([low, mid, high], axis=0)
    rows = lax.broadcasted_iota(jnp.int32, (stations, nz), 0)
    share = jnp.zeros((modes_k, nz), F32)
    for x in range(nx):
        hot = (rows == station[x : x + 1, :]).astype(F32).astype(jnp.bfloat16)
        parts = jnp.dot(pieces, hot, preferred_element_type=F32)
        at_face = parts[:modes_k] + parts[modes_k : 2 * modes_k] + parts[2 * modes_k :]
        modes[x] = at_face
        face = outward[0, x : x + 1, :] * lam[0, 0, x, 0:1, :]
        for j in range(1, nv):
            face = face + outward[j, x : x + 1, :] * lam[0, j, x, 0:1, :]
        share = share + at_face * face
    lax.fori_loop(0, nv, columns, 0)
    row = lax.broadcasted_iota(jnp.int32, (modes_k, modes_k), 0)
    lane = lax.broadcasted_iota(jnp.int32, (modes_k, modes_k), 1)
    stiff = jnp.sum(jnp.where(row == lane, inv_stiff[...], 0.0), axis=1, keepdims=True)
    column = jnp.sum(share, axis=1, keepdims=True) * stiff
    tile_lane = lax.broadcasted_iota(jnp.int32, (8, nz), 1)
    tile = jnp.zeros((8, nz), F32)
    for group in range(modes_k // 8):
        tile = jnp.where(tile_lane == group, column[8 * group : 8 * group + 8], tile)
    packed[...] = tile
    near[nv * ny :, :] = tile
    wrap[nv * ny :, :] = tile


def share_kernel(*refs):
    held, out = refs[:-1], refs[-1]
    count = lax.axis_size("inst")
    me = lax.axis_index("inst")
    weights = [weight_of(count, me ^ mask, me ^ 1) for mask in held_masks(me)]

    def columns(j, carry):
        out[0, j] = sum(weight * block[0, j] for weight, block in zip(weights, held))
        return carry

    lax.fori_loop(0, out.shape[1], columns, 0)


def flux_kernel(lam, source, jac, out):
    nv, nx, ny, nz = lam.shape[1:]
    y = lax.broadcasted_iota(jnp.int32, (ny, nz), 0)
    z = lax.broadcasted_iota(jnp.int32, (ny, nz), 1)

    def product(d, j, x):
        total = jac[0, d, 0, j, x] * lam[0, 0, x]
        for i in range(1, nv):
            total = total + jac[0, d, i, j, x] * lam[0, i, x]
        return total

    def columns(j, carry):
        for x in range(nx):
            total = product(0, j, x) - source[0, j, x]
            if x > 0:
                total = total + product(1, j, x - 1)
            if x < nx - 1:
                total = total + product(2, j, x + 1)
            total = total + jnp.where(y == 0, 0.0, pltpu.roll(product(3, j, x), 1, 0))
            total = total + jnp.where(y == ny - 1, 0.0, pltpu.roll(product(4, j, x), ny - 1, 0))
            total = total + jnp.where(z == 0, 0.0, pltpu.roll(product(5, j, x), 1, 1))
            total = total + jnp.where(z == nz - 1, 0.0, pltpu.roll(product(6, j, x), nz - 1, 1))
            out[0, j, x] = total
        return carry

    lax.fori_loop(0, nv, columns, 0)


def own_kernel(partial, volume, packed, wrap, *refs):
    far, refs = (refs[0], refs[1:]) if len(refs) - 3 > len(raw_masks(lax.axis_size("inst"))) else (None, refs)
    held, (out, tile) = refs[:-2], refs[-2:]
    nv, nx, ny, nz = partial.shape[1:]
    count = lax.axis_size("inst")
    me = lax.axis_index("inst")
    weights = [weight_of(count, me ^ mask, me) for mask in held_masks(me)]
    plane = (nx - 1) * lax.rem(lax.axis_index("space"), 2)

    def columns(j, carry):
        total = sum(weight * block[0, j] for weight, block in zip(weights, held))
        out[0, j] = volume[...] * total + partial[0, j]
        out[0, j, plane] = out[0, j, plane] + wrap[pl.ds(pl.multiple_of(j * ny, ny), ny), :]
        return carry

    lax.fori_loop(0, nv, columns, 0)
    tile[...] = packed[...]
    if far is not None:
        tile[...] = packed[...] + wrap[nv * ny :, :] + far[...]


def final_kernel(partial, volume, modes, surface_in, mix, near, tile_in, out, modal):
    nv, nx, ny, nz = partial.shape[1:]
    groups = modal.shape[1] // 8
    tile = near[nv * ny :, :] + tile_in[...]
    even = lax.rem(lax.axis_index("space"), 2) == 0
    columns = [tile[:, group : group + 1] for group in range(groups)]
    line = None
    for group, column in enumerate(columns):
        row = lax.broadcasted_iota(jnp.int32, (8, 8 * groups), 0)
        lane = lax.broadcasted_iota(jnp.int32, (8, 8 * groups), 1)
        piece = jnp.sum(jnp.where(lane == row + 8 * group, column, 0.0), axis=0, keepdims=True)
        line = piece if line is None else line + piece
    modal[...] = line
    low = lax.broadcasted_iota(jnp.int32, (ny, nz), 0) == 0
    backs = []
    for x in range(nx):
        back = jnp.zeros((8, nz), F32)
        for group, column in enumerate(columns):
            back = back + modes[x, 8 * group : 8 * group + 8, :] * column
        backs.append(jnp.sum(back, axis=0, keepdims=True))

    def step(j, carry):
        inward = surface_in[j]
        border = near[pl.ds(pl.multiple_of(j * ny, ny), ny), :]
        for x in range(nx):
            value = partial[0, j, x] + volume[x] * mix[0, j, x]
            if x == 0:
                value = value + jnp.where(even, 0.0, border)
            if x == nx - 1:
                value = value + jnp.where(even, border, 0.0)
            out[0, j, x] = value + jnp.where(low, inward[x : x + 1, :] * backs[x], 0.0)
        return carry

    lax.fori_loop(0, nv, step, 0)


def body(adjoint, jacobian, volume, source, surface_out, surface_in, station, phi, inv_stiff):
    count, slabs = lax.axis_size("inst"), lax.axis_size("space")
    nv, nx, ny, nz = adjoint.shape[1:]
    modes_k = phi.shape[0]

    def swap(value, axis, mask):
        size = lax.axis_size(axis)
        return lax.ppermute(value, axis, [(i, i ^ mask) for i in range(size)])

    def fast(array):
        return pltpu.with_memory_space_constraint(array, pltpu.VMEM)

    def call(kernel, name, out_shape, flops, *operands, specs=None):
        return pl.pallas_call(
            kernel,
            out_shape=out_shape,
            in_specs=[VMEM] * len(operands) if specs is None else specs,
            out_specs=jax.tree.map(lambda shape: SMEM if name == "table" else VMEM, out_shape),
            compiler_params=pltpu.CompilerParams(vmem_limit_bytes=4 * 2**20),
            cost_estimate=pl.CostEstimate(flops=flops, bytes_accessed=0, transcendentals=0),
            name=name,
        )(*operands)

    block = pltpu.VMEM(adjoint.shape, F32)
    raws = [
        lax.ppermute(adjoint, "inst", [(i, i ^ pair[i % 2]) for i in range(count)]) for pair in raw_masks(count)
    ]
    rows = nv * ny + 8
    lam, jac = fast(adjoint), fast(jacobian)
    weights = call(table_kernel, "table", pltpu.SMEM((1, 1), F32), 2**31)
    near, wrap, packed, modes = call(
        prep_kernel,
        "prep",
        (
            pltpu.VMEM((rows, nz), F32),
            pltpu.VMEM((rows, nz), F32),
            pltpu.VMEM((8, nz), F32),
            pltpu.VMEM((nx, modes_k, nz), F32),
        ),
        0,
        weights,
        lam,
        fast(surface_out),
        fast(station),
        fast(phi),
        fast(inv_stiff.reshape(1, modes_k)),
        jac,
        specs=[SMEM] + [VMEM] * 6,
    )
    wrap_in = lax.ppermute(wrap, "space", [(i, (((i + 1) ^ 1) - 1) % slabs) for i in range(slabs)])
    near_in = swap(near, "space", 1)
    far_in = [swap(packed, "space", 2)] if slabs == 4 else []
    partial = call(flux_kernel, "flux", block, 2 * jacobian.size, lam, fast(source), jac)
    share = call(share_kernel, "share", block, 0, lam, *raws)
    mix = swap(share, "inst", 1)
    vol = fast(volume)
    partial, tile = call(
        own_kernel,
        "own",
        (block, pltpu.VMEM((8, nz), F32)),
        2**31,
        partial,
        vol,
        packed,
        wrap_in,
        *far_in,
        lam,
        *raws,
    )
    if slabs != 4:
        tile = tile + near_in[nv * ny :]
        step = 2
        while step < slabs:
            tile = tile + swap(tile, "space", step)
            step *= 2
        near_in = near_in.at[nv * ny :].set(0.0)
    residual, modal = call(
        final_kernel,
        "final",
        (jax.ShapeDtypeStruct(adjoint.shape, F32), jax.ShapeDtypeStruct((1, modes_k), F32)),
        0,
        partial,
        vol,
        modes,
        fast(surface_in),
        mix,
        near_in,
        tile,
    )
    return residual, modal


def solution(mesh):
    placed = (
        P("inst", None, "space", None, None),
        P("inst", None, None, None, "space", None, None),
        P("space", None, None),
        P("inst", None, "space", None, None),
        P(None, "space", None),
        P(None, "space", None),
        P("space", None),
        P(),
        P(),
    )
    return jax.shard_map(
        body,
        mesh=mesh,
        in_specs=placed,
        out_specs=(P("inst", None, "space", None, None), P("inst", None)),
        check_vma=False,
    )
```

time: 18.9 us -> 15.5 us (0.82)
  local copies, waits for them, and re-layouts: 2.66 us -> 0.04 us
  starting transfers between devices: 11.1 us -> 9.41 us
  waiting for transfers between devices: 2.45 us -> 3.2 us
  Pallas kernels: 1.7 us -> 1.94 us
    ppermute x7 -> x3, starting transfers between devices: 7.54 us -> 0.78 us  [swap(): return lax.ppermute(value, axis, [(i, i ^ mask) for i in range(size)])]
    ppermute x0 -> x3, starting transfers between devices: none -> 4.54 us  [body(): lax.ppermute(adjoint, 'inst', [(i, i ^ pair[i % 2]) for i in range(count)])]
    unnamed x20 -> x18, local copies, waits for them, and re-layouts: 2.66 us -> 0.04 us
    ppermute x0 -> x3, waiting for transfers between devices: none -> 1.82 us  [body(): lax.ppermute(adjoint, 'inst', [(i, i ^ pair[i % 2]) for i in range(count)])]
    ppermute x7 -> x3, waiting for transfers between devices: 2.45 us -> 1.37 us  [swap(): return lax.ppermute(value, axis, [(i, i ^ mask) for i in range(size)])]
    ppermute x1, starting transfers between devices: 3.6 us -> 4.09 us  [body(): lax.ppermute(wrap, 'space', [(i, ((i + 1 ^ 1) - 1) % slabs) for i in rang...]
    pallas_call x6, Pallas kernels: 1.7 us -> 1.94 us  [call(): pl.pallas_call(kernel, out_shape=out_shape, in_specs=[VMEM] * len(operand...]
  transfers between devices with their start and end apart: 8 -> 7, of which waited for: 1 -> 4; matrix products, arithmetic and copies ran while one was open for 0% -> 0% of each run, Pallas kernels for 5% -> 7%
where the time goes in v4:
time: 15.5 us; the launch traced here: 15.4 us
  starting transfers between devices  9.41 us (61%)
  waiting for transfers between devices  3.2 us (21%)
  Pallas kernels  1.94 us (13%)
  between operations  0.77 us (5%)
    ppermute x3, starting transfers between devices, body(): lax.ppermute(adjoint, 'inst', [(i, i ^ pair[i % 2]) for i in range(count)])  4.54 us
    ppermute x1, starting transfers between devices, body(): lax.ppermute(wrap, 'space', [(i, ((i + 1 ^ 1) - 1) % slabs) for i in rang...  4.09 us
    pallas_call x6, Pallas kernels, call(): pl.pallas_call(kernel, out_shape=out_shape, in_specs=[VMEM] * len(operand...  1.94 us
    ppermute x3, waiting for transfers between devices, body(): lax.ppermute(adjoint, 'inst', [(i, i ^ pair[i % 2]) for i in range(count)])  1.82 us
    ppermute x3, waiting for transfers between devices, swap(): return lax.ppermute(value, axis, [(i, i ^ mask) for i in range(size)])  1.37 us
    ppermute x3, starting transfers between devices, swap(): return lax.ppermute(value, axis, [(i, i ^ mask) for i in range(size)])  0.78 us
  transfers between devices with their start and end apart: 7, of which 4 were waited for; matrix products, arithmetic and copies ran while one was open for 0% of the time, Pallas kernels for 7%

profile of v4, /device:TPU:0, one launch (start us, length us, event | category | flops | bytes accessed | tf_op | source)
XLA Modules:
  0.0 15.4 jit_solution(9664270775587868760)
XLA Ops:
  0.6 0.0 copy-start.1
  0.6 0.0 copy-start.8
  0.7 0.0 copy-start
  0.7 0.0 copy-start.5
  0.7 0.0 copy-start.7
  0.7 0.0 copy-start.3
  0.7 0.0 copy-start.2
  0.7 3.0 %collective-permute-start.2 = (f32[1,5,4,16,128]{4,3,2,1,0:T(8,128)}, f32[1,5,4,16,128]{4,3,2,1,0:T(8,128)S(1)}, u32[]{:S(2)}, u32[]{:S(2)}) collective-permute-start(f32[1,5,4,16,128]{4,3,2,1,0:T(8,128)} %refs_0_.1), channel_id=1, source_target_pairs={{0,8},{4,20},{8,0},{12,28},{16,24},{20,4},{24,16},{28,12},{1,9},{5... | collective-permute-start | bytes 491528 | tf_op jit(solution)/shard_map/ppermute | solution.py:225
  3.7 1.5 %collective-permute-start.3 = (f32[1,5,4,16,128]{4,3,2,1,0:T(8,128)}, f32[1,5,4,16,128]{4,3,2,1,0:T(8,128)S(1)}, u32[]{:S(2)}, u32[]{:S(2)}) collective-permute-start(f32[1,5,4,16,128]{4,3,2,1,0:T(8,128)} %refs_0_.1), channel_id=1, source_target_pairs={{0,16},{4,12},{8,24},{12,4},{16,0},{20,28},{24,8},{28,20},{1,17},{... | collective-permute-start | bytes 491528 | tf_op jit(solution)/shard_map/ppermute | solution.py:225
  5.2 0.0 collective-permute-start.4
  5.2 0.0 copy-done.1
  5.3 0.0 copy-done.8
  5.3 0.0 copy-done
  5.3 0.0 copy-done.5
  5.3 0.0 copy-start.4
  5.3 0.4 %prep.1 = (f32[88,128]{1,0:T(8,128)S(1)}, f32[88,128]{1,0:T(8,128)S(1)}, f32[8,128]{1,0:T(8,128)S(1)}, f32[4,40,128]{2,1,0:T(8,128)S(1)}) custom-call(f32[1,1]{1,0:T(1,128)S(4)} %table.1.token, f32[1,5,4,16,128]{4,3,2,1,0:T(8,128)S(1)} %copy-done.1, f32[5,4,128]{2,1,0:T(4,128)S(1)} %copy-done.5, s32[4,128]{1,0:T(4,128)S(1)} %copy-done.7, ...), custom_call_target="tpu_custom_call" | custom-call | tf_op jit(solution)/shard_map/prep/pallas_call | solution.py:213
  5.7 4.1 %collective-permute-start = (f32[88,128]{1,0:T(8,128)S(1)}, f32[88,128]{1,0:T(8,128)S(1)}, u32[]{:S(2)}, u32[]{:S(2)}) collective-permute-start(f32[88,128]{1,0:T(8,128)S(1)} %get-tuple-element.9), channel_id=1, source_target_pairs={{0,3},{1,2},{2,1},{3,0},{4,7},{5,6},{6,5},{7,4},{8,11},{9,10},{10,... | collective-permute-start | bytes 135176 | tf_op jit(solution)/shard_map/ppermute | solution.py:249
  9.8 0.0 collective-permute-start.1
  9.8 0.6 %flux.1.partial = f32[1,5,4,16,128]{4,3,2,1,0:T(8,128)S(1)} custom-call(f32[1,5,4,16,128]{4,3,2,1,0:T(8,128)S(1)} %copy-done.1, f32[1,5,4,16,128]{4,3,2,1,0:T(8,128)S(1)} %copy-done.2, f32[1,7,5,5,4,16,128]{6,5,4,3,2,1,0:T(8,128)S(1)} %copy-done), custom_call_target="tpu_custom_call" | custom-call | flops 2867200 | tf_op jit(solution)/shard_map/flux/pallas_call | solution.py:213
  10.4 0.0 copy-start.6
  10.4 0.0 collective-permute-done.2.refs_2_.refs_1_
  10.4 0.7 %collective-permute-start.6 = (f32[88,128]{1,0:T(8,128)S(1)}, f32[88,128]{1,0:T(8,128)S(1)}, u32[]{:S(2)}, u32[]{:S(2)}) collective-permute-start(f32[88,128]{1,0:T(8,128)S(1)} %get-tuple-element.12), channel_id=1, source_target_pairs={{0,1},{1,0},{2,3},{3,2},{4,5},{5,4},{6,7},{7,6},{8,9},{9,8},{10,11... | collective-permute-start | bytes 135176 | tf_op jit(solution)/shard_map/ppermute | solution.py:207
  11.1 0.8 %collective-permute-done.3.refs_3_.refs_2_ = f32[1,5,4,16,128]{4,3,2,1,0:T(8,128)S(1)} collective-permute-done((f32[1,5,4,16,128]{4,3,2,1,0:T(8,128)}, f32[1,5,4,16,128]{4,3,2,1,0:T(8,128)S(1)}, u32[]{:S(2)}, u32[]{:S(2)}) %collective-permute-start.3) | collective-permute-done | bytes 163872 | tf_op jit(solution)/shard_map/ppermute | solution.py:225
  11.9 1.0 %collective-permute-done.4.refs_4_.refs_3_ = f32[1,5,4,16,128]{4,3,2,1,0:T(8,128)S(1)} collective-permute-done((f32[1,5,4,16,128]{4,3,2,1,0:T(8,128)}, f32[1,5,4,16,128]{4,3,2,1,0:T(8,128)S(1)}, u32[]{:S(2)}, u32[]{:S(2)}) %collective-permute-start.4) | collective-permute-done | bytes 163872 | tf_op jit(solution)/shard_map/ppermute | solution.py:225
  12.9 0.1 share.1
  13.0 0.1 collective-permute-start.5
  13.1 1.3 %collective-permute-done.1.refs_0_ = f32[8,128]{1,0:T(8,128)S(1)} collective-permute-done((f32[8,128]{1,0:T(8,128)S(1)}, f32[8,128]{1,0:T(8,128)S(1)}, u32[]{:S(2)}, u32[]{:S(2)}) %collective-permute-start.1) | collective-permute-done | bytes 4128 | tf_op jit(solution)/shard_map/ppermute | solution.py:207
  14.4 0.0 collective-permute-done.wrap
  14.4 0.1 own.1
  14.5 0.1 collective-permute-done.6.near
  14.5 0.0 collective-permute-done.5.mix
  14.5 0.8 %final.1 = (f32[1,5,4,16,128]{4,3,2,1,0:T(8,128)}, f32[1,40]{1,0:T(1,128)}) custom-call(f32[1,5,4,16,128]{4,3,2,1,0:T(8,128)S(1)} %get-tuple-element.10.partial, f32[4,16,128]{2,1,0:T(8,128)S(1)} %copy-done.4, f32[4,40,128]{2,1,0:T(8,128)S(1)} %get-tuple-element.11.modes, f32[5,4,128]{2,1,0:T(4,128)S(1)} %copy-done.6, ...), custom_call_target="tpu_custom_call" | custom-call | tf_op jit(solution)/shard_map/final/pallas_call | solution.py:213
  (6 shorter events, 0.0 us)
Async XLA Ops:
  0.6 4.6 %copy-start.1 = (f32[1,5,4,16,128]{4,3,2,1,0:T(8,128)S(1)}, f32[1,5,4,16,128]{4,3,2,1,0:T(8,128)}, u32[]{:S(2)}) copy-start(f32[1,5,4,16,128]{4,3,2,1,0:T(8,128)} %refs_0_.1) | copy-start | bytes 491524
  0.6 4.6 %copy-start.8 = (f32[40]{0:T(128)S(1)}, f32[40]{0:T(128)}, u32[]{:S(2)}) copy-start(f32[40]{0:T(128)} %param.17) | copy-start | bytes 484
  0.7 4.6 %copy-start = (f32[1,7,5,5,4,16,128]{6,5,4,3,2,1,0:T(8,128)S(1)}, f32[1,7,5,5,4,16,128]{6,5,4,3,2,1,0:T(8,128)}, u32[]{:S(2)}) copy-start(f32[1,7,5,5,4,16,128]{6,5,4,3,2,1,0:T(8,128)} %jac.3) | copy-start | bytes 17203204
  0.7 4.6 %copy-start.5 = (f32[5,4,128]{2,1,0:T(4,128)S(1)}, f32[5,4,128]{2,1,0:T(4,128)}, u32[]{:S(2)}) copy-start(f32[5,4,128]{2,1,0:T(4,128)} %outward.1) | copy-start | bytes 30724
  0.7 4.6 %copy-start.7 = (s32[4,128]{1,0:T(4,128)S(1)}, s32[4,128]{1,0:T(4,128)}, u32[]{:S(2)}) copy-start(s32[4,128]{1,0:T(4,128)} %station.1) | copy-start | bytes 6148
  0.7 4.6 %copy-start.3 = (f32[40,256]{1,0:T(8,128)S(1)}, f32[40,256]{1,0:T(8,128)}, u32[]{:S(2)}) copy-start(f32[40,256]{1,0:T(8,128)} %phi.1) | copy-start | bytes 122884
  0.7 9.1 %copy-start.2 = (f32[1,5,4,16,128]{4,3,2,1,0:T(8,128)S(1)}, f32[1,5,4,16,128]{4,3,2,1,0:T(8,128)}, u32[]{:S(2)}) copy-start(f32[1,5,4,16,128]{4,3,2,1,0:T(8,128)} %source.1) | copy-start | bytes 491524
  0.7 9.7 %collective-permute-start.2 = (f32[1,5,4,16,128]{4,3,2,1,0:T(8,128)}, f32[1,5,4,16,128]{4,3,2,1,0:T(8,128)S(1)}, u32[]{:S(2)}, u32[]{:S(2)}) collective-permute-start(f32[1,5,4,16,128]{4,3,2,1,0:T(8,128)} %refs_0_.1), channel_id=1, source_target_pairs={{0,8},{4,20},{8,0},{12,28},{16,24},{20,4},{24,16},{28,12},{1,9},{5... | collective-permute-start | bytes 491528 | tf_op jit(solution)/shard_map/ppermute | solution.py:225
  3.7 8.2 %collective-permute-start.3 = (f32[1,5,4,16,128]{4,3,2,1,0:T(8,128)}, f32[1,5,4,16,128]{4,3,2,1,0:T(8,128)S(1)}, u32[]{:S(2)}, u32[]{:S(2)}) collective-permute-start(f32[1,5,4,16,128]{4,3,2,1,0:T(8,128)} %refs_0_.1), channel_id=1, source_target_pairs={{0,16},{4,12},{8,24},{12,4},{16,0},{20,28},{24,8},{28,20},{1,17},{... | collective-permute-start | bytes 491528 | tf_op jit(solution)/shard_map/ppermute | solution.py:225
  5.2 7.7 %collective-permute-start.4 = (f32[1,5,4,16,128]{4,3,2,1,0:T(8,128)}, f32[1,5,4,16,128]{4,3,2,1,0:T(8,128)S(1)}, u32[]{:S(2)}, u32[]{:S(2)}) collective-permute-start(f32[1,5,4,16,128]{4,3,2,1,0:T(8,128)} %refs_0_.1), channel_id=1, source_target_pairs={{0,24},{4,28},{8,16},{12,20},{16,8},{20,12},{24,0},{28,4},{1,25},{... | collective-permute-start | bytes 491528 | tf_op jit(solution)/shard_map/ppermute | solution.py:225
  5.3 9.1 %copy-start.4 = (f32[4,16,128]{2,1,0:T(8,128)S(1)}, f32[4,16,128]{2,1,0:T(8,128)}, u32[]{:S(2)}) copy-start(f32[4,16,128]{2,1,0:T(8,128)} %volume.3) | copy-start | bytes 98308
  5.7 8.7 %collective-permute-start = (f32[88,128]{1,0:T(8,128)S(1)}, f32[88,128]{1,0:T(8,128)S(1)}, u32[]{:S(2)}, u32[]{:S(2)}) collective-permute-start(f32[88,128]{1,0:T(8,128)S(1)} %get-tuple-element.9), channel_id=1, source_target_pairs={{0,3},{1,2},{2,1},{3,0},{4,7},{5,6},{6,5},{7,4},{8,11},{9,10},{10,... | collective-permute-start | bytes 135176 | tf_op jit(solution)/shard_map/ppermute | solution.py:249
  9.8 4.6 %collective-permute-start.1 = (f32[8,128]{1,0:T(8,128)S(1)}, f32[8,128]{1,0:T(8,128)S(1)}, u32[]{:S(2)}, u32[]{:S(2)}) collective-permute-start(f32[8,128]{1,0:T(8,128)S(1)} %get-tuple-element.8.packed), channel_id=1, source_target_pairs={{0,2},{1,3},{2,0},{3,1},{4,6},{5,7},{6,4},{7,5},{8,10},{9,11},{10,... | collective-permute-start | bytes 12296 | tf_op jit(solution)/shard_map/ppermute | solution.py:207
  10.4 4.2 %copy-start.6 = (f32[5,4,128]{2,1,0:T(4,128)S(1)}, f32[5,4,128]{2,1,0:T(4,128)}, u32[]{:S(2)}) copy-start(f32[5,4,128]{2,1,0:T(4,128)} %surface_in.1) | copy-start | bytes 30724
  10.4 4.2 %collective-permute-start.6 = (f32[88,128]{1,0:T(8,128)S(1)}, f32[88,128]{1,0:T(8,128)S(1)}, u32[]{:S(2)}, u32[]{:S(2)}) collective-permute-start(f32[88,128]{1,0:T(8,128)S(1)} %get-tuple-element.12), channel_id=1, source_target_pairs={{0,1},{1,0},{2,3},{3,2},{4,5},{5,4},{6,7},{7,6},{8,9},{9,8},{10,11... | collective-permute-start | bytes 135176 | tf_op jit(solution)/shard_map/ppermute | solution.py:207
  13.0 1.6 %collective-permute-start.5 = (f32[1,5,4,16,128]{4,3,2,1,0:T(8,128)S(1)}, f32[1,5,4,16,128]{4,3,2,1,0:T(8,128)S(1)}, u32[]{:S(2)}, u32[]{:S(2)}) collective-permute-start(f32[1,5,4,16,128]{4,3,2,1,0:T(8,128)S(1)} %share.1), channel_id=1, source_target_pairs={{0,4},{4,0},{8,12},{12,8},{16,20},{20,16},{24,28},{28,24},{1,5},{5... | collective-permute-start | bytes 491528 | tf_op jit(solution)/shard_map/ppermute | solution.py:207

commit v5 on v4

--- a/solution.py
+++ b/solution.py
@@ -40,13 +40,14 @@
 def raw_masks(count):
     steps = [mask for mask in range(2, count, 2) if mask & (mask - 1) == 0]
     others = [mask for mask in range(2, count, 2) if mask & (mask - 1)]
-    return [(steps[k], steps[(k + 1) % len(steps)]) for k in range(len(steps))] + [(mask, mask) for mask in others]
+    first = [(steps[k] + 0, steps[(k + 1) % len(steps)] + 0) for k in range(len(steps))]
+    return first + [(mask + 1, mask + 1) for mask in others]
 
 
 def held_masks(me):
     pairs = raw_masks(lax.axis_size("inst"))
     core = lax.rem(me, 2)
-    return [0] + [a if a == b else jnp.where(core == 0, a, b) for a, b in pairs]
+    return [0] + [jnp.where(core == a % 2, a, b) for a, b in pairs]
 
 
 def table_kernel(out):
@@ -99,17 +100,21 @@
     wrap[nv * ny :, :] = tile
 
 
-def share_kernel(*refs):
-    held, out = refs[:-1], refs[-1]
+def mix_kernel(partial, volume, *refs):
+    held, (share, out) = refs[:-2], refs[-2:]
     count = lax.axis_size("inst")
     me = lax.axis_index("inst")
-    weights = [weight_of(count, me ^ mask, me ^ 1) for mask in held_masks(me)]
+    masks = held_masks(me)
+    there = [weight_of(count, me ^ mask, me ^ 1) for mask in masks]
+    here = [weight_of(count, me ^ mask, me) for mask in masks]
 
     def columns(j, carry):
-        out[0, j] = sum(weight * block[0, j] for weight, block in zip(weights, held))
-        return carry
-
-    lax.fori_loop(0, out.shape[1], columns, 0)
+        share[0, j] = sum(weight * block[0, j] for weight, block in zip(there, held))
+        total = sum(weight * block[0, j] for weight, block in zip(here, held))
+        out[0, j] = volume[...] * total + partial[0, j]
+        return carry
+
+    lax.fori_loop(0, partial.shape[1], columns, 0)
 
 
 def flux_kernel(lam, source, jac, out):
@@ -140,31 +145,17 @@
     lax.fori_loop(0, nv, columns, 0)
 
 
-def own_kernel(partial, volume, packed, wrap, *refs):
-    far, refs = (refs[0], refs[1:]) if len(refs) - 3 > len(raw_masks(lax.axis_size("inst"))) else (None, refs)
-    held, (out, tile) = refs[:-2], refs[-2:]
-    nv, nx, ny, nz = partial.shape[1:]
-    count = lax.axis_size("inst")
-    me = lax.axis_index("inst")
-    weights = [weight_of(count, me ^ mask, me) for mask in held_masks(me)]
-    plane = (nx - 1) * lax.rem(lax.axis_index("space"), 2)
-
-    def columns(j, carry):
-        total = sum(weight * block[0, j] for weight, block in zip(weights, held))
-        out[0, j] = volume[...] * total + partial[0, j]
-        out[0, j, plane] = out[0, j, plane] + wrap[pl.ds(pl.multiple_of(j * ny, ny), ny), :]
-        return carry
-
-    lax.fori_loop(0, nv, columns, 0)
-    tile[...] = packed[...]
-    if far is not None:
-        tile[...] = packed[...] + wrap[nv * ny :, :] + far[...]
-
-
-def final_kernel(partial, volume, modes, surface_in, mix, near, tile_in, out, modal):
+def pick_kernel(packed, first, second, out):
+    lower = lax.axis_index("space") < 2
+    split = out.shape[0] - 8
+    out[:split, :] = jnp.where(lower, first[:split, :], second[:split, :])
+    out[split:, :] = packed[...] + first[split:, :] + second[split:, :]
+
+
+def final_kernel(partial, volume, modes, surface_in, mix, near, wrap, out, modal):
     nv, nx, ny, nz = partial.shape[1:]
     groups = modal.shape[1] // 8
-    tile = near[nv * ny :, :] + tile_in[...]
+    tile = near[nv * ny :, :] + wrap[nv * ny :, :]
     even = lax.rem(lax.axis_index("space"), 2) == 0
     columns = [tile[:, group : group + 1] for group in range(groups)]
     line = None
@@ -184,13 +175,15 @@
 
     def step(j, carry):
         inward = surface_in[j]
-        border = near[pl.ds(pl.multiple_of(j * ny, ny), ny), :]
+        rows = pl.ds(pl.multiple_of(j * ny, ny), ny)
+        first = jnp.where(even, wrap[rows, :], near[rows, :])
+        last = jnp.where(even, near[rows, :], wrap[rows, :])
         for x in range(nx):
             value = partial[0, j, x] + volume[x] * mix[0, j, x]
             if x == 0:
-                value = value + jnp.where(even, 0.0, border)
+                value = value + first
             if x == nx - 1:
-                value = value + jnp.where(even, border, 0.0)
+                value = value + last
             out[0, j, x] = value + jnp.where(low, inward[x : x + 1, :] * backs[x], 0.0)
         return carry
 
@@ -246,33 +239,25 @@
         jac,
         specs=[SMEM] + [VMEM] * 6,
     )
-    wrap_in = lax.ppermute(wrap, "space", [(i, (((i + 1) ^ 1) - 1) % slabs) for i in range(slabs)])
-    near_in = swap(near, "space", 1)
-    far_in = [swap(packed, "space", 2)] if slabs == 4 else []
-    partial = call(flux_kernel, "flux", block, 2 * jacobian.size, lam, fast(source), jac)
-    share = call(share_kernel, "share", block, 0, lam, *raws)
-    mix = swap(share, "inst", 1)
-    vol = fast(volume)
-    partial, tile = call(
-        own_kernel,
-        "own",
-        (block, pltpu.VMEM((8, nz), F32)),
-        2**31,
-        partial,
-        vol,
-        packed,
-        wrap_in,
-        *far_in,
-        lam,
-        *raws,
-    )
-    if slabs != 4:
-        tile = tile + near_in[nv * ny :]
+    if slabs == 4:
+        first = lax.ppermute(wrap, "space", [(3, 0), (2, 1), (0, 2), (1, 3)])
+        second = lax.ppermute(wrap, "space", [(0, 3), (1, 2), (2, 0), (3, 1)])
+        near_in = swap(near, "space", 1)
+        wrap_in = call(pick_kernel, "pick", pltpu.VMEM((rows, nz), F32), 2**31, packed, first, second)
+    else:
+        wrap_in = lax.ppermute(wrap, "space", [(i, (((i + 1) ^ 1) - 1) % slabs) for i in range(slabs)])
+        near_in = swap(near, "space", 1)
+        tile = packed + near_in[nv * ny :]
         step = 2
         while step < slabs:
             tile = tile + swap(tile, "space", step)
             step *= 2
+        wrap_in = wrap_in.at[nv * ny :].set(tile)
         near_in = near_in.at[nv * ny :].set(0.0)
+    partial = call(flux_kernel, "flux", block, 2 * jacobian.size, lam, fast(source), jac)
+    vol = fast(volume)
+    share, partial = call(mix_kernel, "mix", (block, block), 0, partial, vol, lam, *raws)
+    mix = swap(share, "inst", 1)
     residual, modal = call(
         final_kernel,
         "final",
@@ -284,7 +269,7 @@
         fast(surface_in),
         mix,
         near_in,
-        tile,
+        wrap_in,
     )
     return residual, modal
 

time: 15.5 us -> 15.5 us (level)
    ppermute x3 -> x2, waiting for transfers between devices: 1.37 us -> 0.78 us  [swap(): return lax.ppermute(value, axis, [(i, i ^ mask) for i in range(size)])]
    ppermute x1 -> x2, waiting for transfers between devices: 0.01 us -> 0.48 us  [the longest x1 0.47 us: body(): second = lax.ppermute(wrap, 'space', [(0, 3), (1, 2), (2, 0), (3, 1)])]
    ppermute x3 -> x2, starting transfers between devices: 0.78 us -> 1.11 us  [swap(): return lax.ppermute(value, axis, [(i, i ^ mask) for i in range(size)])]
    ppermute x1 -> x2, starting transfers between devices: 4.09 us -> 3.84 us  [the longest x1 2.6 us: body(): first = lax.ppermute(wrap, 'space', [(3, 0), (2, 1), (0, 2), (1, 3)])]
  transfers between devices with their start and end apart: 7 -> 7, of which waited for: 4 -> 5; matrix products, arithmetic and copies ran while one was open for 0% -> 0% of each run, Pallas kernels for 7% -> 7%
where the time goes in v5:
time: 15.5 us; the launch traced here: 15.3 us
  starting transfers between devices  9.47 us (61%)
  waiting for transfers between devices  3.19 us (21%)
  Pallas kernels  1.83 us (12%)
  between operations  0.76 us (5%)
    ppermute x3, starting transfers between devices, body(): lax.ppermute(adjoint, 'inst', [(i, i ^ pair[i % 2]) for i in range(count)])  4.53 us
    ppermute x1, starting transfers between devices, body(): first = lax.ppermute(wrap, 'space', [(3, 0), (2, 1), (0, 2), (1, 3)])  2.6 us
    ppermute x3, waiting for transfers between devices, body(): lax.ppermute(adjoint, 'inst', [(i, i ^ pair[i % 2]) for i in range(count)])  1.93 us
    pallas_call x6, Pallas kernels, call(): pl.pallas_call(kernel, out_shape=out_shape, in_specs=[VMEM] * len(operand...  1.83 us
    ppermute x1, starting transfers between devices, body(): second = lax.ppermute(wrap, 'space', [(0, 3), (1, 2), (2, 0), (3, 1)])  1.24 us
    ppermute x2, starting transfers between devices, swap(): return lax.ppermute(value, axis, [(i, i ^ mask) for i in range(size)])  1.11 us
    ppermute x2, waiting for transfers between devices, swap(): return lax.ppermute(value, axis, [(i, i ^ mask) for i in range(size)])  0.78 us
    ppermute x1, waiting for transfers between devices, body(): second = lax.ppermute(wrap, 'space', [(0, 3), (1, 2), (2, 0), (3, 1)])  0.47 us
  transfers between devices with their start and end apart: 7, of which 5 were waited for; matrix products, arithmetic and copies ran while one was open for 0% of the time, Pallas kernels for 7%

profile of v5, /device:TPU:0, one launch (start us, length us, event | category | flops | bytes accessed | tf_op | source)
XLA Modules:
  0.0 15.3 jit_solution(12029433222643526532)
XLA Ops:
  0.6 0.0 copy-start.1
  0.6 0.0 copy-start
  0.7 0.0 copy-start.5
  0.7 0.0 copy-start.7
  0.7 0.0 copy-start.4
  0.7 0.0 copy-start.8
  0.7 0.0 copy-start.2
  0.7 3.0 %collective-permute-start = (f32[1,5,4,16,128]{4,3,2,1,0:T(8,128)}, f32[1,5,4,16,128]{4,3,2,1,0:T(8,128)S(1)}, u32[]{:S(2)}, u32[]{:S(2)}) collective-permute-start(f32[1,5,4,16,128]{4,3,2,1,0:T(8,128)} %lam.3), channel_id=1, source_target_pairs={{0,8},{4,20},{8,0},{12,28},{16,24},{20,4},{24,16},{28,12},{1,9},{5... | collective-permute-start | bytes 491528 | tf_op jit(solution)/shard_map/ppermute | solution.py:218
  3.7 1.5 %collective-permute-start.1 = (f32[1,5,4,16,128]{4,3,2,1,0:T(8,128)}, f32[1,5,4,16,128]{4,3,2,1,0:T(8,128)S(1)}, u32[]{:S(2)}, u32[]{:S(2)}) collective-permute-start(f32[1,5,4,16,128]{4,3,2,1,0:T(8,128)} %lam.3), channel_id=1, source_target_pairs={{0,16},{4,12},{8,24},{12,4},{16,0},{20,28},{24,8},{28,20},{1,17},{... | collective-permute-start | bytes 491528 | tf_op jit(solution)/shard_map/ppermute | solution.py:218
  5.2 0.0 collective-permute-start.2
  5.2 0.0 copy-done.1
  5.2 0.0 copy-done
  5.2 0.0 copy-done.5
  5.2 0.0 copy-done.7
  5.3 0.0 copy-start.3
  5.3 0.4 %prep.1 = (f32[88,128]{1,0:T(8,128)S(1)}, f32[88,128]{1,0:T(8,128)S(1)}, f32[8,128]{1,0:T(8,128)S(1)}, f32[4,40,128]{2,1,0:T(8,128)S(1)}) custom-call(f32[1,1]{1,0:T(1,128)S(4)} %table.1.token, f32[1,5,4,16,128]{4,3,2,1,0:T(8,128)S(1)} %copy-done.1, f32[5,4,128]{2,1,0:T(4,128)S(1)} %copy-done.5, s32[4,128]{1,0:T(4,128)S(1)} %copy-done.7, ...), custom_call_target="tpu_custom_call" | custom-call | tf_op jit(solution)/shard_map/prep/pallas_call | solution.py:206
  5.7 2.6 %collective-permute-start.5 = (f32[88,128]{1,0:T(8,128)S(1)}, f32[88,128]{1,0:T(8,128)S(1)}, u32[]{:S(2)}, u32[]{:S(2)}) collective-permute-start(f32[88,128]{1,0:T(8,128)S(1)} %get-tuple-element.13), channel_id=1, source_target_pairs={{3,0},{2,1},{0,2},{1,3},{7,4},{6,5},{4,6},{5,7},{11,8},{10,9},{8,1... | collective-permute-start | bytes 135176 | tf_op jit(solution)/shard_map/ppermute | solution.py:243
  8.3 1.2 %collective-permute-start.6 = (f32[88,128]{1,0:T(8,128)S(1)}, f32[88,128]{1,0:T(8,128)S(1)}, u32[]{:S(2)}, u32[]{:S(2)}) collective-permute-start(f32[88,128]{1,0:T(8,128)S(1)} %get-tuple-element.13), channel_id=1, source_target_pairs={{0,3},{1,2},{2,0},{3,1},{4,7},{5,6},{6,4},{7,5},{8,11},{9,10},{10,... | collective-permute-start | bytes 135176 | tf_op jit(solution)/shard_map/ppermute | solution.py:244
  9.5 0.5 %flux.1.partial = f32[1,5,4,16,128]{4,3,2,1,0:T(8,128)S(1)} custom-call(f32[1,5,4,16,128]{4,3,2,1,0:T(8,128)S(1)} %copy-done.1, f32[1,5,4,16,128]{4,3,2,1,0:T(8,128)S(1)} %copy-done.2, f32[1,7,5,5,4,16,128]{6,5,4,3,2,1,0:T(8,128)S(1)} %copy-done), custom_call_target="tpu_custom_call" | custom-call | flops 2867200 | tf_op jit(solution)/shard_map/flux/pallas_call | solution.py:206
  10.0 0.0 copy-start.6
  10.0 0.0 collective-permute-done.refs_1_
  10.0 0.9 %collective-permute-start.4 = (f32[88,128]{1,0:T(8,128)S(1)}, f32[88,128]{1,0:T(8,128)S(1)}, u32[]{:S(2)}, u32[]{:S(2)}) collective-permute-start(f32[88,128]{1,0:T(8,128)S(1)} %get-tuple-element.11), channel_id=1, source_target_pairs={{0,1},{1,0},{2,3},{3,2},{4,5},{5,4},{6,7},{7,6},{8,9},{9,8},{10,11... | collective-permute-start | bytes 135176 | tf_op jit(solution)/shard_map/ppermute | solution.py:200
  11.0 1.0 %collective-permute-done.1.refs_2_ = f32[1,5,4,16,128]{4,3,2,1,0:T(8,128)S(1)} collective-permute-done((f32[1,5,4,16,128]{4,3,2,1,0:T(8,128)}, f32[1,5,4,16,128]{4,3,2,1,0:T(8,128)S(1)}, u32[]{:S(2)}, u32[]{:S(2)}) %collective-permute-start.1) | collective-permute-done | bytes 163872 | tf_op jit(solution)/shard_map/ppermute | solution.py:218
  11.9 1.0 %collective-permute-done.2.refs_3_ = f32[1,5,4,16,128]{4,3,2,1,0:T(8,128)S(1)} collective-permute-done((f32[1,5,4,16,128]{4,3,2,1,0:T(8,128)}, f32[1,5,4,16,128]{4,3,2,1,0:T(8,128)S(1)}, u32[]{:S(2)}, u32[]{:S(2)}) %collective-permute-start.2) | collective-permute-done | bytes 163872 | tf_op jit(solution)/shard_map/ppermute | solution.py:218
  12.9 0.0 copy-done.3
  12.9 0.1 mix.1
  13.0 0.2 %collective-permute-start.3 = (f32[1,5,4,16,128]{4,3,2,1,0:T(8,128)S(1)}, f32[1,5,4,16,128]{4,3,2,1,0:T(8,128)S(1)}, u32[]{:S(2)}, u32[]{:S(2)}) collective-permute-start(f32[1,5,4,16,128]{4,3,2,1,0:T(8,128)S(1)} %get-tuple-element.10), channel_id=1, source_target_pairs={{0,4},{4,0},{8,12},{12,8},{16,20},{20,16},{24,28},{28,24},{1,5},{5... | collective-permute-start | bytes 491528 | tf_op jit(solution)/shard_map/ppermute | solution.py:200
  13.2 0.0 collective-permute-done.5.first
  13.2 0.5 %collective-permute-done.6.second = f32[88,128]{1,0:T(8,128)S(1)} collective-permute-done((f32[88,128]{1,0:T(8,128)S(1)}, f32[88,128]{1,0:T(8,128)S(1)}, u32[]{:S(2)}, u32[]{:S(2)}) %collective-permute-start.6) | collective-permute-done | bytes 45088 | tf_op jit(solution)/shard_map/ppermute | solution.py:244
  13.7 0.5 %collective-permute-done.4.near = f32[88,128]{1,0:T(8,128)S(1)} collective-permute-done((f32[88,128]{1,0:T(8,128)S(1)}, f32[88,128]{1,0:T(8,128)S(1)}, u32[]{:S(2)}, u32[]{:S(2)}) %collective-permute-start.4) | collective-permute-done | bytes 45088 | tf_op jit(solution)/shard_map/ppermute | solution.py:200
  14.2 0.3 %collective-permute-done.3.mix = f32[1,5,4,16,128]{4,3,2,1,0:T(8,128)S(1)} collective-permute-done((f32[1,5,4,16,128]{4,3,2,1,0:T(8,128)S(1)}, f32[1,5,4,16,128]{4,3,2,1,0:T(8,128)S(1)}, u32[]{:S(2)}, u32[]{:S(2)}) %collective-permute-start.3) | collective-permute-done | bytes 163872 | tf_op jit(solution)/shard_map/ppermute | solution.py:200
  14.5 0.8 %final.1 = (f32[1,5,4,16,128]{4,3,2,1,0:T(8,128)}, f32[1,40]{1,0:T(1,128)}) custom-call(f32[1,5,4,16,128]{4,3,2,1,0:T(8,128)S(1)} %get-tuple-element.8.partial, f32[4,16,128]{2,1,0:T(8,128)S(1)} %copy-done.3, f32[4,40,128]{2,1,0:T(8,128)S(1)} %get-tuple-element.9.modes, f32[5,4,128]{2,1,0:T(4,128)S(1)} %copy-done.6, ...), custom_call_target="tpu_custom_call" | custom-call | tf_op jit(solution)/shard_map/final/pallas_call | solution.py:206
  (6 shorter events, 0.0 us)
Async XLA Ops:
  0.6 4.6 %copy-start.1 = (f32[1,5,4,16,128]{4,3,2,1,0:T(8,128)S(1)}, f32[1,5,4,16,128]{4,3,2,1,0:T(8,128)}, u32[]{:S(2)}) copy-start(f32[1,5,4,16,128]{4,3,2,1,0:T(8,128)} %lam.3) | copy-start | bytes 491524
  0.6 4.6 %copy-start = (f32[1,7,5,5,4,16,128]{6,5,4,3,2,1,0:T(8,128)S(1)}, f32[1,7,5,5,4,16,128]{6,5,4,3,2,1,0:T(8,128)}, u32[]{:S(2)}) copy-start(f32[1,7,5,5,4,16,128]{6,5,4,3,2,1,0:T(8,128)} %jac.3) | copy-start | bytes 17203204
  0.7 4.6 %copy-start.5 = (f32[5,4,128]{2,1,0:T(4,128)S(1)}, f32[5,4,128]{2,1,0:T(4,128)}, u32[]{:S(2)}) copy-start(f32[5,4,128]{2,1,0:T(4,128)} %outward.1) | copy-start | bytes 30724
  0.7 4.6 %copy-start.7 = (s32[4,128]{1,0:T(4,128)S(1)}, s32[4,128]{1,0:T(4,128)}, u32[]{:S(2)}) copy-start(s32[4,128]{1,0:T(4,128)} %station.1) | copy-start | bytes 6148
  0.7 4.6 %copy-start.4 = (f32[40,256]{1,0:T(8,128)S(1)}, f32[40,256]{1,0:T(8,128)}, u32[]{:S(2)}) copy-start(f32[40,256]{1,0:T(8,128)} %phi.1) | copy-start | bytes 122884
  0.7 4.6 %copy-start.8 = (f32[40]{0:T(128)S(1)}, f32[40]{0:T(128)}, u32[]{:S(2)}) copy-start(f32[40]{0:T(128)} %param.17) | copy-start | bytes 484
  0.7 8.8 %copy-start.2 = (f32[1,5,4,16,128]{4,3,2,1,0:T(8,128)S(1)}, f32[1,5,4,16,128]{4,3,2,1,0:T(8,128)}, u32[]{:S(2)}) copy-start(f32[1,5,4,16,128]{4,3,2,1,0:T(8,128)} %source.1) | copy-start | bytes 491524
  0.7 9.3 %collective-permute-start = (f32[1,5,4,16,128]{4,3,2,1,0:T(8,128)}, f32[1,5,4,16,128]{4,3,2,1,0:T(8,128)S(1)}, u32[]{:S(2)}, u32[]{:S(2)}) collective-permute-start(f32[1,5,4,16,128]{4,3,2,1,0:T(8,128)} %lam.3), channel_id=1, source_target_pairs={{0,8},{4,20},{8,0},{12,28},{16,24},{20,4},{24,16},{28,12},{1,9},{5... | collective-permute-start | bytes 491528 | tf_op jit(solution)/shard_map/ppermute | solution.py:218
  3.7 8.2 %collective-permute-start.1 = (f32[1,5,4,16,128]{4,3,2,1,0:T(8,128)}, f32[1,5,4,16,128]{4,3,2,1,0:T(8,128)S(1)}, u32[]{:S(2)}, u32[]{:S(2)}) collective-permute-start(f32[1,5,4,16,128]{4,3,2,1,0:T(8,128)} %lam.3), channel_id=1, source_target_pairs={{0,16},{4,12},{8,24},{12,4},{16,0},{20,28},{24,8},{28,20},{1,17},{... | collective-permute-start | bytes 491528 | tf_op jit(solution)/shard_map/ppermute | solution.py:218
  5.2 7.7 %collective-permute-start.2 = (f32[1,5,4,16,128]{4,3,2,1,0:T(8,128)}, f32[1,5,4,16,128]{4,3,2,1,0:T(8,128)S(1)}, u32[]{:S(2)}, u32[]{:S(2)}) collective-permute-start(f32[1,5,4,16,128]{4,3,2,1,0:T(8,128)} %lam.3), channel_id=1, source_target_pairs={{0,28},{4,24},{8,20},{12,16},{16,12},{20,8},{24,4},{28,0},{1,29},{... | collective-permute-start | bytes 491528 | tf_op jit(solution)/shard_map/ppermute | solution.py:218
  5.3 7.6 %copy-start.3 = (f32[4,16,128]{2,1,0:T(8,128)S(1)}, f32[4,16,128]{2,1,0:T(8,128)}, u32[]{:S(2)}) copy-start(f32[4,16,128]{2,1,0:T(8,128)} %volume.3) | copy-start | bytes 98308
  5.7 7.6 %collective-permute-start.5 = (f32[88,128]{1,0:T(8,128)S(1)}, f32[88,128]{1,0:T(8,128)S(1)}, u32[]{:S(2)}, u32[]{:S(2)}) collective-permute-start(f32[88,128]{1,0:T(8,128)S(1)} %get-tuple-element.13), channel_id=1, source_target_pairs={{3,0},{2,1},{0,2},{1,3},{7,4},{6,5},{4,6},{5,7},{11,8},{10,9},{8,1... | collective-permute-start | bytes 135176 | tf_op jit(solution)/shard_map/ppermute | solution.py:243
  8.3 5.4 %collective-permute-start.6 = (f32[88,128]{1,0:T(8,128)S(1)}, f32[88,128]{1,0:T(8,128)S(1)}, u32[]{:S(2)}, u32[]{:S(2)}) collective-permute-start(f32[88,128]{1,0:T(8,128)S(1)} %get-tuple-element.13), channel_id=1, source_target_pairs={{0,3},{1,2},{2,0},{3,1},{4,7},{5,6},{6,4},{7,5},{8,11},{9,10},{10,... | collective-permute-start | bytes 135176 | tf_op jit(solution)/shard_map/ppermute | solution.py:244
  10.0 4.5 %copy-start.6 = (f32[5,4,128]{2,1,0:T(4,128)S(1)}, f32[5,4,128]{2,1,0:T(4,128)}, u32[]{:S(2)}) copy-start(f32[5,4,128]{2,1,0:T(4,128)} %surface_in.1) | copy-start | bytes 30724
  10.0 4.1 %collective-permute-start.4 = (f32[88,128]{1,0:T(8,128)S(1)}, f32[88,128]{1,0:T(8,128)S(1)}, u32[]{:S(2)}, u32[]{:S(2)}) collective-permute-start(f32[88,128]{1,0:T(8,128)S(1)} %get-tuple-element.11), channel_id=1, source_target_pairs={{0,1},{1,0},{2,3},{3,2},{4,5},{5,4},{6,7},{7,6},{8,9},{9,8},{10,11... | collective-permute-start | bytes 135176 | tf_op jit(solution)/shard_map/ppermute | solution.py:200
  13.0 1.5 %collective-permute-start.3 = (f32[1,5,4,16,128]{4,3,2,1,0:T(8,128)S(1)}, f32[1,5,4,16,128]{4,3,2,1,0:T(8,128)S(1)}, u32[]{:S(2)}, u32[]{:S(2)}) collective-permute-start(f32[1,5,4,16,128]{4,3,2,1,0:T(8,128)S(1)} %get-tuple-element.10), channel_id=1, source_target_pairs={{0,4},{4,0},{8,12},{12,8},{16,20},{20,16},{24,28},{28,24},{1,5},{5... | collective-permute-start | bytes 491528 | tf_op jit(solution)/shard_map/ppermute | solution.py:200

commit v6 on v5

--- a/solution.py
+++ b/solution.py
@@ -40,7 +40,7 @@
 def raw_masks(count):
     steps = [mask for mask in range(2, count, 2) if mask & (mask - 1) == 0]
     others = [mask for mask in range(2, count, 2) if mask & (mask - 1)]
-    first = [(steps[k] + 0, steps[(k + 1) % len(steps)] + 0) for k in range(len(steps))]
+    first = [(steps[k], steps[(k + 1) % len(steps)]) for k in range(len(steps))]
     return first + [(mask + 1, mask + 1) for mask in others]
 
 
@@ -100,24 +100,25 @@
     wrap[nv * ny :, :] = tile
 
 
-def mix_kernel(partial, volume, *refs):
-    held, (share, out) = refs[:-2], refs[-2:]
+def mix_of(held, target):
     count = lax.axis_size("inst")
     me = lax.axis_index("inst")
-    masks = held_masks(me)
-    there = [weight_of(count, me ^ mask, me ^ 1) for mask in masks]
-    here = [weight_of(count, me ^ mask, me) for mask in masks]
+    weights = [weight_of(count, me ^ mask, me ^ target) for mask in held_masks(me)]
+    return lambda j: sum(weight * block[0, j] for weight, block in zip(weights, held))
+
+
+def share_kernel(after, *refs):
+    held, out = refs[:-1], refs[-1]
+    share = mix_of(held, 1)
 
     def columns(j, carry):
-        share[0, j] = sum(weight * block[0, j] for weight, block in zip(there, held))
-        total = sum(weight * block[0, j] for weight, block in zip(here, held))
-        out[0, j] = volume[...] * total + partial[0, j]
-        return carry
-
-    lax.fori_loop(0, partial.shape[1], columns, 0)
-
-
-def flux_kernel(lam, source, jac, out):
+        out[0, j] = share(j)
+        return carry
+
+    lax.fori_loop(0, out.shape[1], columns, 0)
+
+
+def flux_kernel(after, lam, source, jac, out):
     nv, nx, ny, nz = lam.shape[1:]
     y = lax.broadcasted_iota(jnp.int32, (ny, nz), 0)
     z = lax.broadcasted_iota(jnp.int32, (ny, nz), 1)
@@ -152,11 +153,13 @@
     out[split:, :] = packed[...] + first[split:, :] + second[split:, :]
 
 
-def final_kernel(partial, volume, modes, surface_in, mix, near, wrap, out, modal):
+def beam_kernel(partial, volume, modes, surface_in, near, wrap, *refs):
+    held, (out, modal) = refs[:-2], refs[-2:]
     nv, nx, ny, nz = partial.shape[1:]
     groups = modal.shape[1] // 8
+    own = mix_of(held, 0)
+    even = lax.rem(lax.axis_index("space"), 2) == 0
     tile = near[nv * ny :, :] + wrap[nv * ny :, :]
-    even = lax.rem(lax.axis_index("space"), 2) == 0
     columns = [tile[:, group : group + 1] for group in range(groups)]
     line = None
     for group, column in enumerate(columns):
@@ -174,12 +177,13 @@
         backs.append(jnp.sum(back, axis=0, keepdims=True))
 
     def step(j, carry):
+        mixed = own(j)
         inward = surface_in[j]
         rows = pl.ds(pl.multiple_of(j * ny, ny), ny)
         first = jnp.where(even, wrap[rows, :], near[rows, :])
         last = jnp.where(even, near[rows, :], wrap[rows, :])
         for x in range(nx):
-            value = partial[0, j, x] + volume[x] * mix[0, j, x]
+            value = partial[0, j, x] + volume[x] * mixed[x]
             if x == 0:
                 value = value + first
             if x == nx - 1:
@@ -188,6 +192,16 @@
         return carry
 
     lax.fori_loop(0, nv, step, 0)
+
+
+def final_kernel(partial, volume, line, mix, out, modal):
+    modal[...] = line[...]
+
+    def columns(j, carry):
+        out[0, j] = partial[0, j] + volume[...] * mix[0, j]
+        return carry
+
+    lax.fori_loop(0, out.shape[1], columns, 0)
 
 
 def body(adjoint, jacobian, volume, source, surface_out, surface_in, station, phi, inv_stiff):
@@ -254,23 +268,26 @@
             step *= 2
         wrap_in = wrap_in.at[nv * ny :].set(tile)
         near_in = near_in.at[nv * ny :].set(0.0)
-    partial = call(flux_kernel, "flux", block, 2 * jacobian.size, lam, fast(source), jac)
+    partial = call(flux_kernel, "flux", block, 2 * jacobian.size, raws[0], lam, fast(source), jac, specs=[ANY] + [VMEM] * 3)
     vol = fast(volume)
-    share, partial = call(mix_kernel, "mix", (block, block), 0, partial, vol, lam, *raws)
+    share = call(share_kernel, "share", block, 0, partial, lam, *raws, specs=[ANY] + [VMEM] * (1 + len(raws)))
     mix = swap(share, "inst", 1)
-    residual, modal = call(
-        final_kernel,
-        "final",
-        (jax.ShapeDtypeStruct(adjoint.shape, F32), jax.ShapeDtypeStruct((1, modes_k), F32)),
+    partial, line = call(
+        beam_kernel,
+        "beam",
+        (block, pltpu.VMEM((1, modes_k), F32)),
         0,
         partial,
         vol,
         modes,
         fast(surface_in),
-        mix,
         near_in,
         wrap_in,
+        lam,
+        *raws,
     )
+    shapes = (jax.ShapeDtypeStruct(adjoint.shape, F32), jax.ShapeDtypeStruct((1, modes_k), F32))
+    residual, modal = call(final_kernel, "final", shapes, 0, partial, vol, line, mix)
     return residual, modal
 
 

time: 15.5 us -> 15.3 us (0.987)
  waiting for transfers between devices: 3.19 us -> 2.36 us
  starting transfers between devices: 9.47 us -> 10 us
    ppermute x3, waiting for transfers between devices: 1.93 us -> 1.32 us  [body(): lax.ppermute(adjoint, 'inst', [(i, i ^ pair[i % 2]) for i in range(count)])]
    ppermute x2, starting transfers between devices: 1.11 us -> 1.67 us  [swap(): return lax.ppermute(value, axis, [(i, i ^ mask) for i in range(size)])]
    ppermute x2, waiting for transfers between devices: 0.78 us -> 0.52 us  [swap(): return lax.ppermute(value, axis, [(i, i ^ mask) for i in range(size)])]
    pallas_call x6 -> x7, Pallas kernels: 1.83 us -> 1.95 us  [call(): pl.pallas_call(kernel, out_shape=out_shape, in_specs=[VMEM] * len(operand...]
  transfers between devices with their start and end apart: 7 -> 7, of which waited for: 5 -> 5; matrix products, arithmetic and copies ran while one was open for 0% -> 0% of each run, Pallas kernels for 7% -> 8%
where the time goes in v6:
time: 15.3 us; the launch traced here: 15.1 us
  starting transfers between devices  10 us (65%)
  waiting for transfers between devices  2.36 us (15%)
  Pallas kernels  1.95 us (13%)
  between operations  0.77 us (5%)
    ppermute x3, starting transfers between devices, body(): lax.ppermute(adjoint, 'inst', [(i, i ^ pair[i % 2]) for i in range(count)])  4.53 us
    ppermute x1, starting transfers between devices, body(): first = lax.ppermute(wrap, 'space', [(3, 0), (2, 1), (0, 2), (1, 3)])  2.6 us
    pallas_call x7, Pallas kernels, call(): pl.pallas_call(kernel, out_shape=out_shape, in_specs=[VMEM] * len(operand...  1.95 us
    ppermute x2, starting transfers between devices, swap(): return lax.ppermute(value, axis, [(i, i ^ mask) for i in range(size)])  1.67 us
    ppermute x3, waiting for transfers between devices, body(): lax.ppermute(adjoint, 'inst', [(i, i ^ pair[i % 2]) for i in range(count)])  1.32 us
    ppermute x1, starting transfers between devices, body(): second = lax.ppermute(wrap, 'space', [(0, 3), (1, 2), (2, 0), (3, 1)])  1.23 us
    ppermute x1, waiting for transfers between devices, body(): second = lax.ppermute(wrap, 'space', [(0, 3), (1, 2), (2, 0), (3, 1)])  0.53 us
    ppermute x2, waiting for transfers between devices, swap(): return lax.ppermute(value, axis, [(i, i ^ mask) for i in range(size)])  0.52 us
  transfers between devices with their start and end apart: 7, of which 5 were waited for; matrix products, arithmetic and copies ran while one was open for 0% of the time, Pallas kernels for 8%

profile of v6, /device:TPU:0, one launch (start us, length us, event | category | flops | bytes accessed | tf_op | source)
XLA Modules:
  0.0 15.1 jit_solution(6426981290048136927)
XLA Ops:
  0.6 0.0 copy-start.1
  0.6 0.0 copy-start.8
  0.7 0.0 copy-start
  0.7 0.0 copy-start.5
  0.7 0.0 copy-start.7
  0.7 0.0 copy-start.4
  0.7 0.0 copy-start.2
  0.7 3.0 %collective-permute-start = (f32[1,5,4,16,128]{4,3,2,1,0:T(8,128)}, f32[1,5,4,16,128]{4,3,2,1,0:T(8,128)S(1)}, u32[]{:S(2)}, u32[]{:S(2)}) collective-permute-start(f32[1,5,4,16,128]{4,3,2,1,0:T(8,128)} %refs_0_.3), channel_id=1, source_target_pairs={{0,8},{4,20},{8,0},{12,28},{16,24},{20,4},{24,16},{28,12},{1,9},{5... | collective-permute-start | bytes 491528 | tf_op jit(solution)/shard_map/ppermute | solution.py:232
  3.7 1.5 %collective-permute-start.4 = (f32[1,5,4,16,128]{4,3,2,1,0:T(8,128)}, f32[1,5,4,16,128]{4,3,2,1,0:T(8,128)S(1)}, u32[]{:S(2)}, u32[]{:S(2)}) collective-permute-start(f32[1,5,4,16,128]{4,3,2,1,0:T(8,128)} %refs_0_.3), channel_id=1, source_target_pairs={{0,16},{4,12},{8,24},{12,4},{16,0},{20,28},{24,8},{28,20},{1,17},{... | collective-permute-start | bytes 491528 | tf_op jit(solution)/shard_map/ppermute | solution.py:232
  5.2 0.0 collective-permute-start.5
  5.2 0.0 copy-done.1
  5.2 0.0 copy-done.8
  5.2 0.0 copy-done
  5.3 0.4 %prep.1 = (f32[88,128]{1,0:T(8,128)S(1)}, f32[88,128]{1,0:T(8,128)S(1)}, f32[8,128]{1,0:T(8,128)S(1)}, f32[4,40,128]{2,1,0:T(8,128)S(1)}) custom-call(f32[1,1]{1,0:T(1,128)S(4)} %table.1.token, f32[1,5,4,16,128]{4,3,2,1,0:T(8,128)S(1)} %copy-done.1, f32[5,4,128]{2,1,0:T(4,128)S(1)} %copy-done.5, s32[4,128]{1,0:T(4,128)S(1)} %copy-done.7, ...), custom_call_target="tpu_custom_call" | custom-call | tf_op jit(solution)/shard_map/prep/pallas_call | solution.py:220
  5.7 2.6 %collective-permute-start.2 = (f32[88,128]{1,0:T(8,128)S(1)}, f32[88,128]{1,0:T(8,128)S(1)}, u32[]{:S(2)}, u32[]{:S(2)}) collective-permute-start(f32[88,128]{1,0:T(8,128)S(1)} %get-tuple-element.11), channel_id=1, source_target_pairs={{3,0},{2,1},{0,2},{1,3},{7,4},{6,5},{4,6},{5,7},{11,8},{10,9},{8,1... | collective-permute-start | bytes 135176 | tf_op jit(solution)/shard_map/ppermute | solution.py:257
  8.3 1.2 %collective-permute-start.3 = (f32[88,128]{1,0:T(8,128)S(1)}, f32[88,128]{1,0:T(8,128)S(1)}, u32[]{:S(2)}, u32[]{:S(2)}) collective-permute-start(f32[88,128]{1,0:T(8,128)S(1)} %get-tuple-element.11), channel_id=1, source_target_pairs={{0,3},{1,2},{2,0},{3,1},{4,7},{5,6},{6,4},{7,5},{8,11},{9,10},{10,... | collective-permute-start | bytes 135176 | tf_op jit(solution)/shard_map/ppermute | solution.py:258
  9.5 0.0 collective-permute-done.after.refs_1_
  9.5 1.5 %collective-permute-start.1 = (f32[88,128]{1,0:T(8,128)S(1)}, f32[88,128]{1,0:T(8,128)S(1)}, u32[]{:S(2)}, u32[]{:S(2)}) collective-permute-start(f32[88,128]{1,0:T(8,128)S(1)} %get-tuple-element.9), channel_id=1, source_target_pairs={{0,1},{1,0},{2,3},{3,2},{4,5},{5,4},{6,7},{7,6},{8,9},{9,8},{10,11... | collective-permute-start | bytes 135176 | tf_op jit(solution)/shard_map/ppermute | solution.py:214
  11.0 0.6 %flux.1.partial.after = f32[1,5,4,16,128]{4,3,2,1,0:T(8,128)S(1)} custom-call(f32[1,5,4,16,128]{4,3,2,1,0:T(8,128)S(1)} %collective-permute-done.after.refs_1_, f32[1,5,4,16,128]{4,3,2,1,0:T(8,128)S(1)} %copy-done.1, f32[1,5,4,16,128]{4,3,2,1,0:T(8,128)S(1)} %copy-done.2, f32[1,7,5,5,4,16,128]{6,5,4,3,2,1,0:T(8,128)S(1)} %copy-done), custom_call_target="tpu_custom_call" | custom-call | flops 2867200 | tf_op jit(solution)/shard_map/flux/pallas_call | solution.py:220
  11.6 0.0 copy-start.3
  11.6 0.0 copy-start.6
  11.6 0.3 %collective-permute-done.4.refs_2_ = f32[1,5,4,16,128]{4,3,2,1,0:T(8,128)S(1)} collective-permute-done((f32[1,5,4,16,128]{4,3,2,1,0:T(8,128)}, f32[1,5,4,16,128]{4,3,2,1,0:T(8,128)S(1)}, u32[]{:S(2)}, u32[]{:S(2)}) %collective-permute-start.4) | collective-permute-done | bytes 163872 | tf_op jit(solution)/shard_map/ppermute | solution.py:232
  11.9 1.0 %collective-permute-done.5.refs_3_ = f32[1,5,4,16,128]{4,3,2,1,0:T(8,128)S(1)} collective-permute-done((f32[1,5,4,16,128]{4,3,2,1,0:T(8,128)}, f32[1,5,4,16,128]{4,3,2,1,0:T(8,128)S(1)}, u32[]{:S(2)}, u32[]{:S(2)}) %collective-permute-start.5) | collective-permute-done | bytes 163872 | tf_op jit(solution)/shard_map/ppermute | solution.py:232
  12.9 0.1 share.1
  13.0 0.2 %collective-permute-start.6 = (f32[1,5,4,16,128]{4,3,2,1,0:T(8,128)S(1)}, f32[1,5,4,16,128]{4,3,2,1,0:T(8,128)S(1)}, u32[]{:S(2)}, u32[]{:S(2)}) collective-permute-start(f32[1,5,4,16,128]{4,3,2,1,0:T(8,128)S(1)} %share.1), channel_id=1, source_target_pairs={{0,4},{4,0},{8,12},{12,8},{16,20},{20,16},{24,28},{28,24},{1,5},{5... | collective-permute-start | bytes 491528 | tf_op jit(solution)/shard_map/ppermute | solution.py:214
  13.2 0.0 collective-permute-done.2.first
  13.2 0.5 %collective-permute-done.3.second = f32[88,128]{1,0:T(8,128)S(1)} collective-permute-done((f32[88,128]{1,0:T(8,128)S(1)}, f32[88,128]{1,0:T(8,128)S(1)}, u32[]{:S(2)}, u32[]{:S(2)}) %collective-permute-start.3) | collective-permute-done | bytes 45088 | tf_op jit(solution)/shard_map/ppermute | solution.py:258
  13.7 0.3 %collective-permute-done.1.near = f32[88,128]{1,0:T(8,128)S(1)} collective-permute-done((f32[88,128]{1,0:T(8,128)S(1)}, f32[88,128]{1,0:T(8,128)S(1)}, u32[]{:S(2)}, u32[]{:S(2)}) %collective-permute-start.1) | collective-permute-done | bytes 45088 | tf_op jit(solution)/shard_map/ppermute | solution.py:214
  14.0 0.0 copy-done.3
  14.0 0.2 %beam.1 = (f32[1,5,4,16,128]{4,3,2,1,0:T(8,128)S(1)}, f32[1,40]{1,0:T(1,128)S(1)}) custom-call(f32[1,5,4,16,128]{4,3,2,1,0:T(8,128)S(1)} %flux.1.partial.after, f32[4,16,128]{2,1,0:T(8,128)S(1)} %copy-done.3, f32[4,40,128]{2,1,0:T(8,128)S(1)} %get-tuple-element.8.modes, f32[5,4,128]{2,1,0:T(4,128)S(1)} %copy-done.6, ...), custom_call_target="tpu_custom_call" | custom-call | tf_op jit(solution)/shard_map/beam/pallas_call | solution.py:220
  14.2 0.2 %collective-permute-done.6.mix = f32[1,5,4,16,128]{4,3,2,1,0:T(8,128)S(1)} collective-permute-done((f32[1,5,4,16,128]{4,3,2,1,0:T(8,128)S(1)}, f32[1,5,4,16,128]{4,3,2,1,0:T(8,128)S(1)}, u32[]{:S(2)}, u32[]{:S(2)}) %collective-permute-start.6) | collective-permute-done | bytes 163872 | tf_op jit(solution)/shard_map/ppermute | solution.py:214
  14.4 0.7 %final.1 = (f32[1,5,4,16,128]{4,3,2,1,0:T(8,128)}, f32[1,40]{1,0:T(1,128)}) custom-call(f32[1,5,4,16,128]{4,3,2,1,0:T(8,128)S(1)} %get-tuple-element.12.partial, f32[4,16,128]{2,1,0:T(8,128)S(1)} %copy-done.3, f32[1,40]{1,0:T(1,128)S(1)} %get-tuple-element.13.line, f32[1,5,4,16,128]{4,3,2,1,0:T(8,128)S(1)} %collective-permute-done.6.mix), custom_call_target="tpu_custom_call" | custom-call | tf_op jit(solution)/shard_map/final/pallas_call | solution.py:220
  (7 shorter events, 0.0 us)
Async XLA Ops:
  0.6 4.6 %copy-start.1 = (f32[1,5,4,16,128]{4,3,2,1,0:T(8,128)S(1)}, f32[1,5,4,16,128]{4,3,2,1,0:T(8,128)}, u32[]{:S(2)}) copy-start(f32[1,5,4,16,128]{4,3,2,1,0:T(8,128)} %refs_0_.3) | copy-start | bytes 491524
  0.6 4.6 %copy-start.8 = (f32[40]{0:T(128)S(1)}, f32[40]{0:T(128)}, u32[]{:S(2)}) copy-start(f32[40]{0:T(128)} %param.17) | copy-start | bytes 484
  0.7 4.6 %copy-start = (f32[1,7,5,5,4,16,128]{6,5,4,3,2,1,0:T(8,128)S(1)}, f32[1,7,5,5,4,16,128]{6,5,4,3,2,1,0:T(8,128)}, u32[]{:S(2)}) copy-start(f32[1,7,5,5,4,16,128]{6,5,4,3,2,1,0:T(8,128)} %jac.3) | copy-start | bytes 17203204
  0.7 4.6 %copy-start.5 = (f32[5,4,128]{2,1,0:T(4,128)S(1)}, f32[5,4,128]{2,1,0:T(4,128)}, u32[]{:S(2)}) copy-start(f32[5,4,128]{2,1,0:T(4,128)} %outward.1) | copy-start | bytes 30724
  0.7 4.6 %copy-start.7 = (s32[4,128]{1,0:T(4,128)S(1)}, s32[4,128]{1,0:T(4,128)}, u32[]{:S(2)}) copy-start(s32[4,128]{1,0:T(4,128)} %station.1) | copy-start | bytes 6148
  0.7 4.6 %copy-start.4 = (f32[40,256]{1,0:T(8,128)S(1)}, f32[40,256]{1,0:T(8,128)}, u32[]{:S(2)}) copy-start(f32[40,256]{1,0:T(8,128)} %phi.1) | copy-start | bytes 122884
  0.7 10.3 %copy-start.2 = (f32[1,5,4,16,128]{4,3,2,1,0:T(8,128)S(1)}, f32[1,5,4,16,128]{4,3,2,1,0:T(8,128)}, u32[]{:S(2)}) copy-start(f32[1,5,4,16,128]{4,3,2,1,0:T(8,128)} %source.1) | copy-start | bytes 491524
  0.7 8.8 %collective-permute-start = (f32[1,5,4,16,128]{4,3,2,1,0:T(8,128)}, f32[1,5,4,16,128]{4,3,2,1,0:T(8,128)S(1)}, u32[]{:S(2)}, u32[]{:S(2)}) collective-permute-start(f32[1,5,4,16,128]{4,3,2,1,0:T(8,128)} %refs_0_.3), channel_id=1, source_target_pairs={{0,8},{4,20},{8,0},{12,28},{16,24},{20,4},{24,16},{28,12},{1,9},{5... | collective-permute-start | bytes 491528 | tf_op jit(solution)/shard_map/ppermute | solution.py:232
  3.7 8.2 %collective-permute-start.4 = (f32[1,5,4,16,128]{4,3,2,1,0:T(8,128)}, f32[1,5,4,16,128]{4,3,2,1,0:T(8,128)S(1)}, u32[]{:S(2)}, u32[]{:S(2)}) collective-permute-start(f32[1,5,4,16,128]{4,3,2,1,0:T(8,128)} %refs_0_.3), channel_id=1, source_target_pairs={{0,16},{4,12},{8,24},{12,4},{16,0},{20,28},{24,8},{28,20},{1,17},{... | collective-permute-start | bytes 491528 | tf_op jit(solution)/shard_map/ppermute | solution.py:232
  5.2 7.7 %collective-permute-start.5 = (f32[1,5,4,16,128]{4,3,2,1,0:T(8,128)}, f32[1,5,4,16,128]{4,3,2,1,0:T(8,128)S(1)}, u32[]{:S(2)}, u32[]{:S(2)}) collective-permute-start(f32[1,5,4,16,128]{4,3,2,1,0:T(8,128)} %refs_0_.3), channel_id=1, source_target_pairs={{0,28},{4,24},{8,20},{12,16},{16,12},{20,8},{24,4},{28,0},{1,29},{... | collective-permute-start | bytes 491528 | tf_op jit(solution)/shard_map/ppermute | solution.py:232
  5.7 7.5 %collective-permute-start.2 = (f32[88,128]{1,0:T(8,128)S(1)}, f32[88,128]{1,0:T(8,128)S(1)}, u32[]{:S(2)}, u32[]{:S(2)}) collective-permute-start(f32[88,128]{1,0:T(8,128)S(1)} %get-tuple-element.11), channel_id=1, source_target_pairs={{3,0},{2,1},{0,2},{1,3},{7,4},{6,5},{4,6},{5,7},{11,8},{10,9},{8,1... | collective-permute-start | bytes 135176 | tf_op jit(solution)/shard_map/ppermute | solution.py:257
  8.3 5.4 %collective-permute-start.3 = (f32[88,128]{1,0:T(8,128)S(1)}, f32[88,128]{1,0:T(8,128)S(1)}, u32[]{:S(2)}, u32[]{:S(2)}) collective-permute-start(f32[88,128]{1,0:T(8,128)S(1)} %get-tuple-element.11), channel_id=1, source_target_pairs={{0,3},{1,2},{2,0},{3,1},{4,7},{5,6},{6,4},{7,5},{8,11},{9,10},{10,... | collective-permute-start | bytes 135176 | tf_op jit(solution)/shard_map/ppermute | solution.py:258
  9.5 4.5 %collective-permute-start.1 = (f32[88,128]{1,0:T(8,128)S(1)}, f32[88,128]{1,0:T(8,128)S(1)}, u32[]{:S(2)}, u32[]{:S(2)}) collective-permute-start(f32[88,128]{1,0:T(8,128)S(1)} %get-tuple-element.9), channel_id=1, source_target_pairs={{0,1},{1,0},{2,3},{3,2},{4,5},{5,4},{6,7},{7,6},{8,9},{9,8},{10,11... | collective-permute-start | bytes 135176 | tf_op jit(solution)/shard_map/ppermute | solution.py:214
  11.6 2.4 %copy-start.3 = (f32[4,16,128]{2,1,0:T(8,128)S(1)}, f32[4,16,128]{2,1,0:T(8,128)}, u32[]{:S(2)}) copy-start(f32[4,16,128]{2,1,0:T(8,128)} %volume.3) | copy-start | bytes 98308
  11.6 2.4 %copy-start.6 = (f32[5,4,128]{2,1,0:T(4,128)S(1)}, f32[5,4,128]{2,1,0:T(4,128)}, u32[]{:S(2)}) copy-start(f32[5,4,128]{2,1,0:T(4,128)} %surface_in.1) | copy-start | bytes 30724
  13.0 1.5 %collective-permute-start.6 = (f32[1,5,4,16,128]{4,3,2,1,0:T(8,128)S(1)}, f32[1,5,4,16,128]{4,3,2,1,0:T(8,128)S(1)}, u32[]{:S(2)}, u32[]{:S(2)}) collective-permute-start(f32[1,5,4,16,128]{4,3,2,1,0:T(8,128)S(1)} %share.1), channel_id=1, source_target_pairs={{0,4},{4,0},{8,12},{12,8},{16,20},{20,16},{24,28},{28,24},{1,5},{5... | collective-permute-start | bytes 491528 | tf_op jit(solution)/shard_map/ppermute | solution.py:214

commit v7 on v6

--- a/solution.py
+++ b/solution.py
@@ -100,10 +100,11 @@
     wrap[nv * ny :, :] = tile
 
 
-def mix_of(held, target):
+def mix_of(held, target, skip=0, core=0):
     count = lax.axis_size("inst")
     me = lax.axis_index("inst")
-    weights = [weight_of(count, me ^ mask, me ^ target) for mask in held_masks(me)]
+    there = me ^ core
+    weights = [weight_of(count, there ^ mask, me ^ target) for mask in held_masks(there)[skip:]]
     return lambda j: sum(weight * block[0, j] for weight, block in zip(weights, held))
 
 
@@ -194,11 +195,13 @@
     lax.fori_loop(0, nv, step, 0)
 
 
-def final_kernel(partial, volume, line, mix, out, modal):
+def final_kernel(partial, volume, line, mix, *refs):
+    last, (out, modal) = refs[:-2], refs[-2:]
     modal[...] = line[...]
+    rest = mix_of(last, 0, len(held_masks(0)) - len(last), 1)
 
     def columns(j, carry):
-        out[0, j] = partial[0, j] + volume[...] * mix[0, j]
+        out[0, j] = partial[0, j] + volume[...] * (mix[0, j] + rest(j))
         return carry
 
     lax.fori_loop(0, out.shape[1], columns, 0)
@@ -231,6 +234,7 @@
     raws = [
         lax.ppermute(adjoint, "inst", [(i, i ^ pair[i % 2]) for i in range(count)]) for pair in raw_masks(count)
     ]
+    steps = sum(mask & (mask - 1) == 0 for mask in range(2, count, 2))
     rows = nv * ny + 8
     lam, jac = fast(adjoint), fast(jacobian)
     weights = call(table_kernel, "table", pltpu.SMEM((1, 1), F32), 2**31)
@@ -270,8 +274,9 @@
         near_in = near_in.at[nv * ny :].set(0.0)
     partial = call(flux_kernel, "flux", block, 2 * jacobian.size, raws[0], lam, fast(source), jac, specs=[ANY] + [VMEM] * 3)
     vol = fast(volume)
-    share = call(share_kernel, "share", block, 0, partial, lam, *raws, specs=[ANY] + [VMEM] * (1 + len(raws)))
+    share = call(share_kernel, "share", block, 0, partial, lam, *raws[:steps], specs=[ANY] + [VMEM] * (1 + steps))
     mix = swap(share, "inst", 1)
+    last = [swap(block, "inst", 1) for block in raws[steps:]]
     partial, line = call(
         beam_kernel,
         "beam",
@@ -287,7 +292,7 @@
         *raws,
     )
     shapes = (jax.ShapeDtypeStruct(adjoint.shape, F32), jax.ShapeDtypeStruct((1, modes_k), F32))
-    residual, modal = call(final_kernel, "final", shapes, 0, partial, vol, line, mix)
+    residual, modal = call(final_kernel, "final", shapes, 0, partial, vol, line, mix, *last)
     return residual, modal
 
 

time: 15.3 us -> 15.2 us (level)
    ppermute x2 -> x3, waiting for transfers between devices: 0.52 us -> 0.38 us  [swap(): return lax.ppermute(value, axis, [(i, i ^ mask) for i in range(size)])]
    ppermute x2 -> x3, starting transfers between devices: 1.67 us -> 1.67 us  [swap(): return lax.ppermute(value, axis, [(i, i ^ mask) for i in range(size)])]
  transfers between devices with their start and end apart: 7 -> 8, of which waited for: 5 -> 5; matrix products, arithmetic and copies ran while one was open for 0% -> 0% of each run, Pallas kernels for 8% -> 8%
where the time goes in v7:
time: 15.2 us; the launch traced here: 15 us
  starting transfers between devices  10 us (66%)
  waiting for transfers between devices  2.22 us (15%)
  Pallas kernels  1.93 us (13%)
  between operations  0.78 us (5%)
    ppermute x3, starting transfers between devices, body(): lax.ppermute(adjoint, 'inst', [(i, i ^ pair[i % 2]) for i in range(count)])  4.53 us
    ppermute x1, starting transfers between devices, body(): first = lax.ppermute(wrap, 'space', [(3, 0), (2, 1), (0, 2), (1, 3)])  2.6 us
    pallas_call x7, Pallas kernels, call(): pl.pallas_call(kernel, out_shape=out_shape, in_specs=[VMEM] * len(operand...  1.93 us
    ppermute x3, starting transfers between devices, swap(): return lax.ppermute(value, axis, [(i, i ^ mask) for i in range(size)])  1.67 us
    ppermute x1, starting transfers between devices, body(): second = lax.ppermute(wrap, 'space', [(0, 3), (1, 2), (2, 0), (3, 1)])  1.23 us
    ppermute x3, waiting for transfers between devices, body(): lax.ppermute(adjoint, 'inst', [(i, i ^ pair[i % 2]) for i in range(count)])  1.18 us
    ppermute x1, waiting for transfers between devices, body(): second = lax.ppermute(wrap, 'space', [(0, 3), (1, 2), (2, 0), (3, 1)])  0.66 us
    ppermute x3, waiting for transfers between devices, swap(): return lax.ppermute(value, axis, [(i, i ^ mask) for i in range(size)])  0.38 us
  transfers between devices with their start and end apart: 8, of which 5 were waited for; matrix products, arithmetic and copies ran while one was open for 0% of the time, Pallas kernels for 8%

profile of v7, /device:TPU:0, one launch (start us, length us, event | category | flops | bytes accessed | tf_op | source)
XLA Modules:
  0.0 15.0 jit_solution(12134472668582473558)
XLA Ops:
  0.6 0.0 copy-start.1
  0.6 0.0 copy-start.8
  0.7 0.0 copy-start
  0.7 0.0 copy-start.5
  0.7 0.0 copy-start.7
  0.7 0.0 copy-start.4
  0.7 0.0 copy-start.2
  0.7 3.0 %collective-permute-start = (f32[1,5,4,16,128]{4,3,2,1,0:T(8,128)}, f32[1,5,4,16,128]{4,3,2,1,0:T(8,128)S(1)}, u32[]{:S(2)}, u32[]{:S(2)}) collective-permute-start(f32[1,5,4,16,128]{4,3,2,1,0:T(8,128)} %refs_0_.3), channel_id=1, source_target_pairs={{0,8},{4,20},{8,0},{12,28},{16,24},{20,4},{24,16},{28,12},{1,9},{5... | collective-permute-start | bytes 491528 | tf_op jit(solution)/shard_map/ppermute | solution.py:235
  3.7 1.5 %collective-permute-start.4 = (f32[1,5,4,16,128]{4,3,2,1,0:T(8,128)}, f32[1,5,4,16,128]{4,3,2,1,0:T(8,128)S(1)}, u32[]{:S(2)}, u32[]{:S(2)}) collective-permute-start(f32[1,5,4,16,128]{4,3,2,1,0:T(8,128)} %refs_0_.3), channel_id=1, source_target_pairs={{0,16},{4,12},{8,24},{12,4},{16,0},{20,28},{24,8},{28,20},{1,17},{... | collective-permute-start | bytes 491528 | tf_op jit(solution)/shard_map/ppermute | solution.py:235
  5.2 0.0 collective-permute-start.5
  5.2 0.0 copy-done.1
  5.2 0.0 copy-done.8
  5.3 0.4 %prep.1 = (f32[88,128]{1,0:T(8,128)S(1)}, f32[88,128]{1,0:T(8,128)S(1)}, f32[8,128]{1,0:T(8,128)S(1)}, f32[4,40,128]{2,1,0:T(8,128)S(1)}) custom-call(f32[1,1]{1,0:T(1,128)S(4)} %table.1.token, f32[1,5,4,16,128]{4,3,2,1,0:T(8,128)S(1)} %copy-done.1, f32[5,4,128]{2,1,0:T(4,128)S(1)} %copy-done.5, s32[4,128]{1,0:T(4,128)S(1)} %copy-done.7, ...), custom_call_target="tpu_custom_call" | custom-call | tf_op jit(solution)/shard_map/prep/pallas_call | solution.py:223
  5.7 2.6 %collective-permute-start.2 = (f32[88,128]{1,0:T(8,128)S(1)}, f32[88,128]{1,0:T(8,128)S(1)}, u32[]{:S(2)}, u32[]{:S(2)}) collective-permute-start(f32[88,128]{1,0:T(8,128)S(1)} %get-tuple-element.11), channel_id=1, source_target_pairs={{3,0},{2,1},{0,2},{1,3},{7,4},{6,5},{4,6},{5,7},{11,8},{10,9},{8,1... | collective-permute-start | bytes 135176 | tf_op jit(solution)/shard_map/ppermute | solution.py:261
  8.3 1.2 %collective-permute-start.3 = (f32[88,128]{1,0:T(8,128)S(1)}, f32[88,128]{1,0:T(8,128)S(1)}, u32[]{:S(2)}, u32[]{:S(2)}) collective-permute-start(f32[88,128]{1,0:T(8,128)S(1)} %get-tuple-element.11), channel_id=1, source_target_pairs={{0,3},{1,2},{2,0},{3,1},{4,7},{5,6},{6,4},{7,5},{8,11},{9,10},{10,... | collective-permute-start | bytes 135176 | tf_op jit(solution)/shard_map/ppermute | solution.py:262
  9.5 0.0 collective-permute-done.after.refs_1_
  9.5 1.5 %collective-permute-start.1 = (f32[88,128]{1,0:T(8,128)S(1)}, f32[88,128]{1,0:T(8,128)S(1)}, u32[]{:S(2)}, u32[]{:S(2)}) collective-permute-start(f32[88,128]{1,0:T(8,128)S(1)} %get-tuple-element.9), channel_id=1, source_target_pairs={{0,1},{1,0},{2,3},{3,2},{4,5},{5,4},{6,7},{7,6},{8,9},{9,8},{10,11... | collective-permute-start | bytes 135176 | tf_op jit(solution)/shard_map/ppermute | solution.py:217
  11.0 0.6 %flux.1.partial.after = f32[1,5,4,16,128]{4,3,2,1,0:T(8,128)S(1)} custom-call(f32[1,5,4,16,128]{4,3,2,1,0:T(8,128)S(1)} %collective-permute-done.after.refs_1_, f32[1,5,4,16,128]{4,3,2,1,0:T(8,128)S(1)} %copy-done.1, f32[1,5,4,16,128]{4,3,2,1,0:T(8,128)S(1)} %copy-done.2, f32[1,7,5,5,4,16,128]{6,5,4,3,2,1,0:T(8,128)S(1)} %copy-done), custom_call_target="tpu_custom_call" | custom-call | flops 2867200 | tf_op jit(solution)/shard_map/flux/pallas_call | solution.py:223
  11.6 0.0 copy-start.3
  11.6 0.0 copy-start.6
  11.6 0.3 %collective-permute-done.4.refs_2_ = f32[1,5,4,16,128]{4,3,2,1,0:T(8,128)S(1)} collective-permute-done((f32[1,5,4,16,128]{4,3,2,1,0:T(8,128)}, f32[1,5,4,16,128]{4,3,2,1,0:T(8,128)S(1)}, u32[]{:S(2)}, u32[]{:S(2)}) %collective-permute-start.4) | collective-permute-done | bytes 163872 | tf_op jit(solution)/shard_map/ppermute | solution.py:235
  12.0 0.1 collective-permute-start.6
  12.1 0.8 %collective-permute-done.5.refs_3_ = f32[1,5,4,16,128]{4,3,2,1,0:T(8,128)S(1)} collective-permute-done((f32[1,5,4,16,128]{4,3,2,1,0:T(8,128)}, f32[1,5,4,16,128]{4,3,2,1,0:T(8,128)S(1)}, u32[]{:S(2)}, u32[]{:S(2)}) %collective-permute-start.5) | collective-permute-done | bytes 163872 | tf_op jit(solution)/shard_map/ppermute | solution.py:235
  12.9 0.1 collective-permute-start.7
  13.0 0.0 collective-permute-done.2.first
  13.0 0.7 %collective-permute-done.3.second = f32[88,128]{1,0:T(8,128)S(1)} collective-permute-done((f32[88,128]{1,0:T(8,128)S(1)}, f32[88,128]{1,0:T(8,128)S(1)}, u32[]{:S(2)}, u32[]{:S(2)}) %collective-permute-start.3) | collective-permute-done | bytes 45088 | tf_op jit(solution)/shard_map/ppermute | solution.py:262
  13.7 0.3 %collective-permute-done.1.near = f32[88,128]{1,0:T(8,128)S(1)} collective-permute-done((f32[88,128]{1,0:T(8,128)S(1)}, f32[88,128]{1,0:T(8,128)S(1)}, u32[]{:S(2)}, u32[]{:S(2)}) %collective-permute-start.1) | collective-permute-done | bytes 45088 | tf_op jit(solution)/shard_map/ppermute | solution.py:217
  14.0 0.0 copy-done.3
  14.0 0.2 %beam.1 = (f32[1,5,4,16,128]{4,3,2,1,0:T(8,128)S(1)}, f32[1,40]{1,0:T(1,128)S(1)}) custom-call(f32[1,5,4,16,128]{4,3,2,1,0:T(8,128)S(1)} %flux.1.partial.after, f32[4,16,128]{2,1,0:T(8,128)S(1)} %copy-done.3, f32[4,40,128]{2,1,0:T(8,128)S(1)} %get-tuple-element.8.modes, f32[5,4,128]{2,1,0:T(4,128)S(1)} %copy-done.6, ...), custom_call_target="tpu_custom_call" | custom-call | tf_op jit(solution)/shard_map/beam/pallas_call | solution.py:223
  14.2 0.0 collective-permute-done.6.mix
  14.2 0.1 collective-permute-done.7.refs_0_
  14.3 0.7 %final.1 = (f32[1,5,4,16,128]{4,3,2,1,0:T(8,128)}, f32[1,40]{1,0:T(1,128)}) custom-call(f32[1,5,4,16,128]{4,3,2,1,0:T(8,128)S(1)} %get-tuple-element.12.partial, f32[4,16,128]{2,1,0:T(8,128)S(1)} %copy-done.3, f32[1,40]{1,0:T(1,128)S(1)} %get-tuple-element.13.line, f32[1,5,4,16,128]{4,3,2,1,0:T(8,128)S(1)} %collective-permute-done.6.mix, ...), custom_call_target="tpu_custom_call" | custom-call | tf_op jit(solution)/shard_map/final/pallas_call | solution.py:223
  (9 shorter events, 0.1 us)
Async XLA Ops:
  0.6 4.6 %copy-start.1 = (f32[1,5,4,16,128]{4,3,2,1,0:T(8,128)S(1)}, f32[1,5,4,16,128]{4,3,2,1,0:T(8,128)}, u32[]{:S(2)}) copy-start(f32[1,5,4,16,128]{4,3,2,1,0:T(8,128)} %refs_0_.3) | copy-start | bytes 491524
  0.6 4.6 %copy-start.8 = (f32[40]{0:T(128)S(1)}, f32[40]{0:T(128)}, u32[]{:S(2)}) copy-start(f32[40]{0:T(128)} %param.17) | copy-start | bytes 484
  0.7 4.6 %copy-start = (f32[1,7,5,5,4,16,128]{6,5,4,3,2,1,0:T(8,128)S(1)}, f32[1,7,5,5,4,16,128]{6,5,4,3,2,1,0:T(8,128)}, u32[]{:S(2)}) copy-start(f32[1,7,5,5,4,16,128]{6,5,4,3,2,1,0:T(8,128)} %jac.3) | copy-start | bytes 17203204
  0.7 4.6 %copy-start.5 = (f32[5,4,128]{2,1,0:T(4,128)S(1)}, f32[5,4,128]{2,1,0:T(4,128)}, u32[]{:S(2)}) copy-start(f32[5,4,128]{2,1,0:T(4,128)} %outward.1) | copy-start | bytes 30724
  0.7 4.6 %copy-start.7 = (s32[4,128]{1,0:T(4,128)S(1)}, s32[4,128]{1,0:T(4,128)}, u32[]{:S(2)}) copy-start(s32[4,128]{1,0:T(4,128)} %station.1) | copy-start | bytes 6148
  0.7 4.6 %copy-start.4 = (f32[40,256]{1,0:T(8,128)S(1)}, f32[40,256]{1,0:T(8,128)}, u32[]{:S(2)}) copy-start(f32[40,256]{1,0:T(8,128)} %phi.1) | copy-start | bytes 122884
  0.7 10.3 %copy-start.2 = (f32[1,5,4,16,128]{4,3,2,1,0:T(8,128)S(1)}, f32[1,5,4,16,128]{4,3,2,1,0:T(8,128)}, u32[]{:S(2)}) copy-start(f32[1,5,4,16,128]{4,3,2,1,0:T(8,128)} %source.1) | copy-start | bytes 491524
  0.7 8.8 %collective-permute-start = (f32[1,5,4,16,128]{4,3,2,1,0:T(8,128)}, f32[1,5,4,16,128]{4,3,2,1,0:T(8,128)S(1)}, u32[]{:S(2)}, u32[]{:S(2)}) collective-permute-start(f32[1,5,4,16,128]{4,3,2,1,0:T(8,128)} %refs_0_.3), channel_id=1, source_target_pairs={{0,8},{4,20},{8,0},{12,28},{16,24},{20,4},{24,16},{28,12},{1,9},{5... | collective-permute-start | bytes 491528 | tf_op jit(solution)/shard_map/ppermute | solution.py:235
  3.7 8.2 %collective-permute-start.4 = (f32[1,5,4,16,128]{4,3,2,1,0:T(8,128)}, f32[1,5,4,16,128]{4,3,2,1,0:T(8,128)S(1)}, u32[]{:S(2)}, u32[]{:S(2)}) collective-permute-start(f32[1,5,4,16,128]{4,3,2,1,0:T(8,128)} %refs_0_.3), channel_id=1, source_target_pairs={{0,16},{4,12},{8,24},{12,4},{16,0},{20,28},{24,8},{28,20},{1,17},{... | collective-permute-start | bytes 491528 | tf_op jit(solution)/shard_map/ppermute | solution.py:235
  5.2 7.7 %collective-permute-start.5 = (f32[1,5,4,16,128]{4,3,2,1,0:T(8,128)}, f32[1,5,4,16,128]{4,3,2,1,0:T(8,128)S(1)}, u32[]{:S(2)}, u32[]{:S(2)}) collective-permute-start(f32[1,5,4,16,128]{4,3,2,1,0:T(8,128)} %refs_0_.3), channel_id=1, source_target_pairs={{0,28},{4,24},{8,20},{12,16},{16,12},{20,8},{24,4},{28,0},{1,29},{... | collective-permute-start | bytes 491528 | tf_op jit(solution)/shard_map/ppermute | solution.py:235
  5.7 7.4 %collective-permute-start.2 = (f32[88,128]{1,0:T(8,128)S(1)}, f32[88,128]{1,0:T(8,128)S(1)}, u32[]{:S(2)}, u32[]{:S(2)}) collective-permute-start(f32[88,128]{1,0:T(8,128)S(1)} %get-tuple-element.11), channel_id=1, source_target_pairs={{3,0},{2,1},{0,2},{1,3},{7,4},{6,5},{4,6},{5,7},{11,8},{10,9},{8,1... | collective-permute-start | bytes 135176 | tf_op jit(solution)/shard_map/ppermute | solution.py:261
  8.3 5.4 %collective-permute-start.3 = (f32[88,128]{1,0:T(8,128)S(1)}, f32[88,128]{1,0:T(8,128)S(1)}, u32[]{:S(2)}, u32[]{:S(2)}) collective-permute-start(f32[88,128]{1,0:T(8,128)S(1)} %get-tuple-element.11), channel_id=1, source_target_pairs={{0,3},{1,2},{2,0},{3,1},{4,7},{5,6},{6,4},{7,5},{8,11},{9,10},{10,... | collective-permute-start | bytes 135176 | tf_op jit(solution)/shard_map/ppermute | solution.py:262
  9.5 4.5 %collective-permute-start.1 = (f32[88,128]{1,0:T(8,128)S(1)}, f32[88,128]{1,0:T(8,128)S(1)}, u32[]{:S(2)}, u32[]{:S(2)}) collective-permute-start(f32[88,128]{1,0:T(8,128)S(1)} %get-tuple-element.9), channel_id=1, source_target_pairs={{0,1},{1,0},{2,3},{3,2},{4,5},{5,4},{6,7},{7,6},{8,9},{9,8},{10,11... | collective-permute-start | bytes 135176 | tf_op jit(solution)/shard_map/ppermute | solution.py:217
  11.6 2.4 %copy-start.3 = (f32[4,16,128]{2,1,0:T(8,128)S(1)}, f32[4,16,128]{2,1,0:T(8,128)}, u32[]{:S(2)}) copy-start(f32[4,16,128]{2,1,0:T(8,128)} %volume.3) | copy-start | bytes 98308
  11.6 2.4 %copy-start.6 = (f32[5,4,128]{2,1,0:T(4,128)S(1)}, f32[5,4,128]{2,1,0:T(4,128)}, u32[]{:S(2)}) copy-start(f32[5,4,128]{2,1,0:T(4,128)} %surface_in.1) | copy-start | bytes 30724
  12.0 2.2 %collective-permute-start.6 = (f32[1,5,4,16,128]{4,3,2,1,0:T(8,128)S(1)}, f32[1,5,4,16,128]{4,3,2,1,0:T(8,128)S(1)}, u32[]{:S(2)}, u32[]{:S(2)}) collective-permute-start(f32[1,5,4,16,128]{4,3,2,1,0:T(8,128)S(1)} %share.1), channel_id=1, source_target_pairs={{0,4},{4,0},{8,12},{12,8},{16,20},{20,16},{24,28},{28,24},{1,5},{5... | collective-permute-start | bytes 491528 | tf_op jit(solution)/shard_map/ppermute | solution.py:217
  12.9 1.4 %collective-permute-start.7 = (f32[1,5,4,16,128]{4,3,2,1,0:T(8,128)S(1)}, f32[1,5,4,16,128]{4,3,2,1,0:T(8,128)S(1)}, u32[]{:S(2)}, u32[]{:S(2)}) collective-permute-start(f32[1,5,4,16,128]{4,3,2,1,0:T(8,128)S(1)} %collective-permute-done.5.refs_3_), channel_id=1, source_target_pairs={{0,4},{4,0},{8,12},{12,8},{16,20},{20,16},{24,28},{28,24},{1,5},{5... | collective-permute-start | bytes 491528 | tf_op jit(solution)/shard_map/ppermute | solution.py:217

commit v8 on v7

--- a/solution.py
+++ b/solution.py
@@ -108,12 +108,13 @@
     return lambda j: sum(weight * block[0, j] for weight, block in zip(weights, held))
 
 
-def share_kernel(after, *refs):
-    held, out = refs[:-1], refs[-1]
-    share = mix_of(held, 1)
+def share_kernel(partial, volume, *refs):
+    held, (out, own) = refs[:-2], refs[-2:]
+    there, here = mix_of(held, 1), mix_of(held, 0)
 
     def columns(j, carry):
-        out[0, j] = share(j)
+        out[0, j] = there(j)
+        own[0, j] = volume[...] * here(j) + partial[0, j]
         return carry
 
     lax.fori_loop(0, out.shape[1], columns, 0)
@@ -158,7 +159,7 @@
     held, (out, modal) = refs[:-2], refs[-2:]
     nv, nx, ny, nz = partial.shape[1:]
     groups = modal.shape[1] // 8
-    own = mix_of(held, 0)
+    own = mix_of(held, 0, len(held_masks(0)) - len(held))
     even = lax.rem(lax.axis_index("space"), 2) == 0
     tile = near[nv * ny :, :] + wrap[nv * ny :, :]
     columns = [tile[:, group : group + 1] for group in range(groups)]
@@ -237,7 +238,7 @@
     steps = sum(mask & (mask - 1) == 0 for mask in range(2, count, 2))
     rows = nv * ny + 8
     lam, jac = fast(adjoint), fast(jacobian)
-    weights = call(table_kernel, "table", pltpu.SMEM((1, 1), F32), 2**31)
+    weights = call(table_kernel, "table", pltpu.SMEM((1, 1), F32), 2**33)
     near, wrap, packed, modes = call(
         prep_kernel,
         "prep",
@@ -274,7 +275,7 @@
         near_in = near_in.at[nv * ny :].set(0.0)
     partial = call(flux_kernel, "flux", block, 2 * jacobian.size, raws[0], lam, fast(source), jac, specs=[ANY] + [VMEM] * 3)
     vol = fast(volume)
-    share = call(share_kernel, "share", block, 0, partial, lam, *raws[:steps], specs=[ANY] + [VMEM] * (1 + steps))
+    share, partial = call(share_kernel, "share", (block, block), 0, partial, vol, lam, *raws[:steps])
     mix = swap(share, "inst", 1)
     last = [swap(block, "inst", 1) for block in raws[steps:]]
     partial, line = call(
@@ -288,8 +289,7 @@
         fast(surface_in),
         near_in,
         wrap_in,
-        lam,
-        *raws,
+        *raws[steps:],
     )
     shapes = (jax.ShapeDtypeStruct(adjoint.shape, F32), jax.ShapeDtypeStruct((1, modes_k), F32))
     residual, modal = call(final_kernel, "final", shapes, 0, partial, vol, line, mix, *last)

time: 15.2 us -> 15.2 us (level)
  no operation moved by 1% of the time
where the time goes in v8:
time: 15.2 us; the launch traced here: 15 us
  starting transfers between devices  10 us (66%)
  waiting for transfers between devices  2.3 us (15%)
  Pallas kernels  1.88 us (12%)
  between operations  0.78 us (5%)
    ppermute x3, starting transfers between devices, body(): lax.ppermute(adjoint, 'inst', [(i, i ^ pair[i % 2]) for i in range(count)])  4.53 us
    ppermute x1, starting transfers between devices, body(): first = lax.ppermute(wrap, 'space', [(3, 0), (2, 1), (0, 2), (1, 3)])  2.6 us
    pallas_call x7, Pallas kernels, call(): pl.pallas_call(kernel, out_shape=out_shape, in_specs=[VMEM] * len(operand...  1.88 us
    ppermute x3, starting transfers between devices, swap(): return lax.ppermute(value, axis, [(i, i ^ mask) for i in range(size)])  1.65 us
    ppermute x1, starting transfers between devices, body(): second = lax.ppermute(wrap, 'space', [(0, 3), (1, 2), (2, 0), (3, 1)])  1.23 us
    ppermute x3, waiting for transfers between devices, body(): lax.ppermute(adjoint, 'inst', [(i, i ^ pair[i % 2]) for i in range(count)])  1.2 us
    ppermute x1, waiting for transfers between devices, body(): second = lax.ppermute(wrap, 'space', [(0, 3), (1, 2), (2, 0), (3, 1)])  0.68 us
    ppermute x3, waiting for transfers between devices, swap(): return lax.ppermute(value, axis, [(i, i ^ mask) for i in range(size)])  0.41 us
  transfers between devices with their start and end apart: 8, of which 5 were waited for; matrix products, arithmetic and copies ran while one was open for 0% of the time, Pallas kernels for 8%

profile of v8, /device:TPU:0, one launch (start us, length us, event | category | flops | bytes accessed | tf_op | source)
XLA Modules:
  0.0 15.0 jit_solution(1553044834492562279)
XLA Ops:
  0.6 0.0 copy-start.1
  0.6 0.0 copy-start
  0.7 0.0 copy-start.5
  0.7 0.0 copy-start.7
  0.7 0.0 copy-start.4
  0.7 0.0 copy-start.8
  0.7 3.0 %collective-permute-start = (f32[1,5,4,16,128]{4,3,2,1,0:T(8,128)}, f32[1,5,4,16,128]{4,3,2,1,0:T(8,128)S(1)}, u32[]{:S(2)}, u32[]{:S(2)}) collective-permute-start(f32[1,5,4,16,128]{4,3,2,1,0:T(8,128)} %lam.3), channel_id=1, source_target_pairs={{0,8},{4,20},{8,0},{12,28},{16,24},{20,4},{24,16},{28,12},{1,9},{5... | collective-permute-start | bytes 491528 | tf_op jit(solution)/shard_map/ppermute | solution.py:236
  3.7 1.5 %collective-permute-start.1 = (f32[1,5,4,16,128]{4,3,2,1,0:T(8,128)}, f32[1,5,4,16,128]{4,3,2,1,0:T(8,128)S(1)}, u32[]{:S(2)}, u32[]{:S(2)}) collective-permute-start(f32[1,5,4,16,128]{4,3,2,1,0:T(8,128)} %lam.3), channel_id=1, source_target_pairs={{0,16},{4,12},{8,24},{12,4},{16,0},{20,28},{24,8},{28,20},{1,17},{... | collective-permute-start | bytes 491528 | tf_op jit(solution)/shard_map/ppermute | solution.py:236
  5.2 0.0 collective-permute-start.5
  5.2 0.0 copy-done.1
  5.2 0.0 copy-done
  5.3 0.0 copy-start.2
  5.3 0.4 %prep.1 = (f32[88,128]{1,0:T(8,128)S(1)}, f32[88,128]{1,0:T(8,128)S(1)}, f32[8,128]{1,0:T(8,128)S(1)}, f32[4,40,128]{2,1,0:T(8,128)S(1)}) custom-call(f32[1,1]{1,0:T(1,128)S(4)} %table.1.token, f32[1,5,4,16,128]{4,3,2,1,0:T(8,128)S(1)} %copy-done.1, f32[5,4,128]{2,1,0:T(4,128)S(1)} %copy-done.5, s32[4,128]{1,0:T(4,128)S(1)} %copy-done.7, ...), custom_call_target="tpu_custom_call" | custom-call | tf_op jit(solution)/shard_map/prep/pallas_call | solution.py:224
  5.7 2.6 %collective-permute-start.3 = (f32[88,128]{1,0:T(8,128)S(1)}, f32[88,128]{1,0:T(8,128)S(1)}, u32[]{:S(2)}, u32[]{:S(2)}) collective-permute-start(f32[88,128]{1,0:T(8,128)S(1)} %get-tuple-element.14), channel_id=1, source_target_pairs={{3,0},{2,1},{0,2},{1,3},{7,4},{6,5},{4,6},{5,7},{11,8},{10,9},{8,1... | collective-permute-start | bytes 135176 | tf_op jit(solution)/shard_map/ppermute | solution.py:262
  8.3 1.2 %collective-permute-start.4 = (f32[88,128]{1,0:T(8,128)S(1)}, f32[88,128]{1,0:T(8,128)S(1)}, u32[]{:S(2)}, u32[]{:S(2)}) collective-permute-start(f32[88,128]{1,0:T(8,128)S(1)} %get-tuple-element.14), channel_id=1, source_target_pairs={{0,3},{1,2},{2,0},{3,1},{4,7},{5,6},{6,4},{7,5},{8,11},{9,10},{10,... | collective-permute-start | bytes 135176 | tf_op jit(solution)/shard_map/ppermute | solution.py:263
  9.5 0.0 collective-permute-done.after.refs_1_
  9.5 1.5 %collective-permute-start.2 = (f32[88,128]{1,0:T(8,128)S(1)}, f32[88,128]{1,0:T(8,128)S(1)}, u32[]{:S(2)}, u32[]{:S(2)}) collective-permute-start(f32[88,128]{1,0:T(8,128)S(1)} %get-tuple-element.12), channel_id=1, source_target_pairs={{0,1},{1,0},{2,3},{3,2},{4,5},{5,4},{6,7},{7,6},{8,9},{9,8},{10,11... | collective-permute-start | bytes 135176 | tf_op jit(solution)/shard_map/ppermute | solution.py:218
  11.0 0.5 %flux.1.partial = f32[1,5,4,16,128]{4,3,2,1,0:T(8,128)S(1)} custom-call(f32[1,5,4,16,128]{4,3,2,1,0:T(8,128)S(1)} %collective-permute-done.after.refs_1_, f32[1,5,4,16,128]{4,3,2,1,0:T(8,128)S(1)} %copy-done.1, f32[1,5,4,16,128]{4,3,2,1,0:T(8,128)S(1)} %copy-done.3, f32[1,7,5,5,4,16,128]{6,5,4,3,2,1,0:T(8,128)S(1)} %copy-done), custom_call_target="tpu_custom_call" | custom-call | flops 2867200 | tf_op jit(solution)/shard_map/flux/pallas_call | solution.py:224
  11.5 0.0 copy-start.6
  11.5 0.4 %collective-permute-done.1.refs_2_ = f32[1,5,4,16,128]{4,3,2,1,0:T(8,128)S(1)} collective-permute-done((f32[1,5,4,16,128]{4,3,2,1,0:T(8,128)}, f32[1,5,4,16,128]{4,3,2,1,0:T(8,128)S(1)}, u32[]{:S(2)}, u32[]{:S(2)}) %collective-permute-start.1) | collective-permute-done | bytes 163872 | tf_op jit(solution)/shard_map/ppermute | solution.py:236
  11.9 0.0 copy-done.2
  11.9 0.1 share.1
  12.0 0.1 collective-permute-start.6
  12.1 0.8 %collective-permute-done.5.refs_0_ = f32[1,5,4,16,128]{4,3,2,1,0:T(8,128)S(1)} collective-permute-done((f32[1,5,4,16,128]{4,3,2,1,0:T(8,128)}, f32[1,5,4,16,128]{4,3,2,1,0:T(8,128)S(1)}, u32[]{:S(2)}, u32[]{:S(2)}) %collective-permute-start.5) | collective-permute-done | bytes 163872 | tf_op jit(solution)/shard_map/ppermute | solution.py:236
  12.9 0.1 collective-permute-start.7
  13.0 0.0 collective-permute-done.3.first
  13.0 0.7 %collective-permute-done.4.second = f32[88,128]{1,0:T(8,128)S(1)} collective-permute-done((f32[88,128]{1,0:T(8,128)S(1)}, f32[88,128]{1,0:T(8,128)S(1)}, u32[]{:S(2)}, u32[]{:S(2)}) %collective-permute-start.4) | collective-permute-done | bytes 45088 | tf_op jit(solution)/shard_map/ppermute | solution.py:263
  13.7 0.3 %collective-permute-done.2.near = f32[88,128]{1,0:T(8,128)S(1)} collective-permute-done((f32[88,128]{1,0:T(8,128)S(1)}, f32[88,128]{1,0:T(8,128)S(1)}, u32[]{:S(2)}, u32[]{:S(2)}) %collective-permute-start.2) | collective-permute-done | bytes 45088 | tf_op jit(solution)/shard_map/ppermute | solution.py:218
  14.0 0.1 beam.1
  14.1 0.0 collective-permute-done.6.mix
  14.2 0.1 collective-permute-done.7.refs_0_
  14.3 0.7 %final.1 = (f32[1,5,4,16,128]{4,3,2,1,0:T(8,128)}, f32[1,40]{1,0:T(1,128)}) custom-call(f32[1,5,4,16,128]{4,3,2,1,0:T(8,128)S(1)} %get-tuple-element.15.partial, f32[4,16,128]{2,1,0:T(8,128)S(1)} %copy-done.2, f32[1,40]{1,0:T(1,128)S(1)} %get-tuple-element.16.line, f32[1,5,4,16,128]{4,3,2,1,0:T(8,128)S(1)} %collective-permute-done.6.mix, ...), custom_call_target="tpu_custom_call" | custom-call | tf_op jit(solution)/shard_map/final/pallas_call | solution.py:224
  (9 shorter events, 0.0 us)
Async XLA Ops:
  0.6 4.6 %copy-start.1 = (f32[1,5,4,16,128]{4,3,2,1,0:T(8,128)S(1)}, f32[1,5,4,16,128]{4,3,2,1,0:T(8,128)}, u32[]{:S(2)}) copy-start(f32[1,5,4,16,128]{4,3,2,1,0:T(8,128)} %lam.3) | copy-start | bytes 491524
  0.6 4.6 %copy-start = (f32[1,7,5,5,4,16,128]{6,5,4,3,2,1,0:T(8,128)S(1)}, f32[1,7,5,5,4,16,128]{6,5,4,3,2,1,0:T(8,128)}, u32[]{:S(2)}) copy-start(f32[1,7,5,5,4,16,128]{6,5,4,3,2,1,0:T(8,128)} %jac.3) | copy-start | bytes 17203204
  0.7 4.6 %copy-start.5 = (f32[5,4,128]{2,1,0:T(4,128)S(1)}, f32[5,4,128]{2,1,0:T(4,128)}, u32[]{:S(2)}) copy-start(f32[5,4,128]{2,1,0:T(4,128)} %outward.1) | copy-start | bytes 30724
  0.7 4.6 %copy-start.7 = (s32[4,128]{1,0:T(4,128)S(1)}, s32[4,128]{1,0:T(4,128)}, u32[]{:S(2)}) copy-start(s32[4,128]{1,0:T(4,128)} %station.1) | copy-start | bytes 6148
  0.7 4.6 %copy-start.4 = (f32[40,256]{1,0:T(8,128)S(1)}, f32[40,256]{1,0:T(8,128)}, u32[]{:S(2)}) copy-start(f32[40,256]{1,0:T(8,128)} %phi.1) | copy-start | bytes 122884
  0.7 4.6 %copy-start.8 = (f32[40]{0:T(128)S(1)}, f32[40]{0:T(128)}, u32[]{:S(2)}) copy-start(f32[40]{0:T(128)} %param.17) | copy-start | bytes 484
  0.7 8.8 %collective-permute-start = (f32[1,5,4,16,128]{4,3,2,1,0:T(8,128)}, f32[1,5,4,16,128]{4,3,2,1,0:T(8,128)S(1)}, u32[]{:S(2)}, u32[]{:S(2)}) collective-permute-start(f32[1,5,4,16,128]{4,3,2,1,0:T(8,128)} %lam.3), channel_id=1, source_target_pairs={{0,8},{4,20},{8,0},{12,28},{16,24},{20,4},{24,16},{28,12},{1,9},{5... | collective-permute-start | bytes 491528 | tf_op jit(solution)/shard_map/ppermute | solution.py:236
  3.7 8.2 %collective-permute-start.1 = (f32[1,5,4,16,128]{4,3,2,1,0:T(8,128)}, f32[1,5,4,16,128]{4,3,2,1,0:T(8,128)S(1)}, u32[]{:S(2)}, u32[]{:S(2)}) collective-permute-start(f32[1,5,4,16,128]{4,3,2,1,0:T(8,128)} %lam.3), channel_id=1, source_target_pairs={{0,16},{4,12},{8,24},{12,4},{16,0},{20,28},{24,8},{28,20},{1,17},{... | collective-permute-start | bytes 491528 | tf_op jit(solution)/shard_map/ppermute | solution.py:236
  5.2 7.7 %collective-permute-start.5 = (f32[1,5,4,16,128]{4,3,2,1,0:T(8,128)}, f32[1,5,4,16,128]{4,3,2,1,0:T(8,128)S(1)}, u32[]{:S(2)}, u32[]{:S(2)}) collective-permute-start(f32[1,5,4,16,128]{4,3,2,1,0:T(8,128)} %lam.3), channel_id=1, source_target_pairs={{0,28},{4,24},{8,20},{12,16},{16,12},{20,8},{24,4},{28,0},{1,29},{... | collective-permute-start | bytes 491528 | tf_op jit(solution)/shard_map/ppermute | solution.py:236
  5.2 5.7 %copy-start.3 = (f32[1,5,4,16,128]{4,3,2,1,0:T(8,128)S(1)}, f32[1,5,4,16,128]{4,3,2,1,0:T(8,128)}, u32[]{:S(2)}) copy-start(f32[1,5,4,16,128]{4,3,2,1,0:T(8,128)} %source.1) | copy-start | bytes 491524
  5.3 6.6 %copy-start.2 = (f32[4,16,128]{2,1,0:T(8,128)S(1)}, f32[4,16,128]{2,1,0:T(8,128)}, u32[]{:S(2)}) copy-start(f32[4,16,128]{2,1,0:T(8,128)} %volume.5) | copy-start | bytes 98308
  5.7 7.4 %collective-permute-start.3 = (f32[88,128]{1,0:T(8,128)S(1)}, f32[88,128]{1,0:T(8,128)S(1)}, u32[]{:S(2)}, u32[]{:S(2)}) collective-permute-start(f32[88,128]{1,0:T(8,128)S(1)} %get-tuple-element.14), channel_id=1, source_target_pairs={{3,0},{2,1},{0,2},{1,3},{7,4},{6,5},{4,6},{5,7},{11,8},{10,9},{8,1... | collective-permute-start | bytes 135176 | tf_op jit(solution)/shard_map/ppermute | solution.py:262
  8.3 5.4 %collective-permute-start.4 = (f32[88,128]{1,0:T(8,128)S(1)}, f32[88,128]{1,0:T(8,128)S(1)}, u32[]{:S(2)}, u32[]{:S(2)}) collective-permute-start(f32[88,128]{1,0:T(8,128)S(1)} %get-tuple-element.14), channel_id=1, source_target_pairs={{0,3},{1,2},{2,0},{3,1},{4,7},{5,6},{6,4},{7,5},{8,11},{9,10},{10,... | collective-permute-start | bytes 135176 | tf_op jit(solution)/shard_map/ppermute | solution.py:263
  9.5 4.5 %collective-permute-start.2 = (f32[88,128]{1,0:T(8,128)S(1)}, f32[88,128]{1,0:T(8,128)S(1)}, u32[]{:S(2)}, u32[]{:S(2)}) collective-permute-start(f32[88,128]{1,0:T(8,128)S(1)} %get-tuple-element.12), channel_id=1, source_target_pairs={{0,1},{1,0},{2,3},{3,2},{4,5},{5,4},{6,7},{7,6},{8,9},{9,8},{10,11... | collective-permute-start | bytes 135176 | tf_op jit(solution)/shard_map/ppermute | solution.py:218
  11.5 2.5 %copy-start.6 = (f32[5,4,128]{2,1,0:T(4,128)S(1)}, f32[5,4,128]{2,1,0:T(4,128)}, u32[]{:S(2)}) copy-start(f32[5,4,128]{2,1,0:T(4,128)} %surface_in.1) | copy-start | bytes 30724
  12.0 2.1 %collective-permute-start.6 = (f32[1,5,4,16,128]{4,3,2,1,0:T(8,128)S(1)}, f32[1,5,4,16,128]{4,3,2,1,0:T(8,128)S(1)}, u32[]{:S(2)}, u32[]{:S(2)}) collective-permute-start(f32[1,5,4,16,128]{4,3,2,1,0:T(8,128)S(1)} %get-tuple-element.17), channel_id=1, source_target_pairs={{0,4},{4,0},{8,12},{12,8},{16,20},{20,16},{24,28},{28,24},{1,5},{5... | collective-permute-start | bytes 491528 | tf_op jit(solution)/shard_map/ppermute | solution.py:218
  12.9 1.4 %collective-permute-start.7 = (f32[1,5,4,16,128]{4,3,2,1,0:T(8,128)S(1)}, f32[1,5,4,16,128]{4,3,2,1,0:T(8,128)S(1)}, u32[]{:S(2)}, u32[]{:S(2)}) collective-permute-start(f32[1,5,4,16,128]{4,3,2,1,0:T(8,128)S(1)} %collective-permute-done.5.refs_0_), channel_id=1, source_target_pairs={{0,4},{4,0},{8,12},{12,8},{16,20},{20,16},{24,28},{28,24},{1,5},{5... | collective-permute-start | bytes 491528 | tf_op jit(solution)/shard_map/ppermute | solution.py:218

commit v9 on v8

--- a/solution.py
+++ b/solution.py
@@ -53,6 +53,10 @@
 def table_kernel(out):
     me = lax.axis_index("inst")
     out[0, 0] = weight_of(lax.axis_size("inst"), me, me)
+
+
+def hold_kernel(token, lam, out):
+    out[...] = lam[...]
 
 
 def prep_kernel(token, lam, outward, station, phi, inv_stiff, jac, near, wrap, packed, modes):
@@ -232,13 +236,15 @@
         )(*operands)
 
     block = pltpu.VMEM(adjoint.shape, F32)
-    raws = [
-        lax.ppermute(adjoint, "inst", [(i, i ^ pair[i % 2]) for i in range(count)]) for pair in raw_masks(count)
-    ]
     steps = sum(mask & (mask - 1) == 0 for mask in range(2, count, 2))
-    rows = nv * ny + 8
     lam, jac = fast(adjoint), fast(jacobian)
     weights = call(table_kernel, "table", pltpu.SMEM((1, 1), F32), 2**33)
+    held = call(hold_kernel, "hold", block, 0, weights, lam, specs=[SMEM, VMEM])
+    raws = [
+        lax.ppermute(adjoint if k < steps else held, "inst", [(i, i ^ pair[i % 2]) for i in range(count)])
+        for k, pair in enumerate(raw_masks(count))
+    ]
+    rows = nv * ny + 8
     near, wrap, packed, modes = call(
         prep_kernel,
         "prep",

time: 15.2 us -> 15.1 us (level)
  waiting for transfers between devices: 2.3 us -> 2.11 us
    ppermute x3, waiting for transfers between devices: 0.41 us -> 0.25 us  [swap(): return lax.ppermute(value, axis, [(i, i ^ mask) for i in range(size)])]
    pallas_call x7 -> x8, Pallas kernels: 1.88 us -> 1.92 us  [call(): pl.pallas_call(kernel, out_shape=out_shape, in_specs=[VMEM] * len(operand...]
  transfers between devices with their start and end apart: 8 -> 8, of which waited for: 5 -> 4; matrix products, arithmetic and copies ran while one was open for 0% -> 0% of each run, Pallas kernels for 8% -> 8%
where the time goes in v9:
time: 15.1 us; the launch traced here: 15 us
  starting transfers between devices  10.1 us (67%)
  waiting for transfers between devices  2.11 us (14%)
  Pallas kernels  1.92 us (13%)
  between operations  0.79 us (5%)
    ppermute x3, starting transfers between devices, body(): lax.ppermute(adjoint if k < steps else held, 'inst', [(i, i ^ pair[i % 2]...  4.59 us
    ppermute x1, starting transfers between devices, body(): first = lax.ppermute(wrap, 'space', [(3, 0), (2, 1), (0, 2), (1, 3)])  2.6 us
    pallas_call x8, Pallas kernels, call(): pl.pallas_call(kernel, out_shape=out_shape, in_specs=[VMEM] * len(operand...  1.92 us
    ppermute x3, starting transfers between devices, swap(): return lax.ppermute(value, axis, [(i, i ^ mask) for i in range(size)])  1.69 us
    ppermute x1, starting transfers between devices, body(): second = lax.ppermute(wrap, 'space', [(0, 3), (1, 2), (2, 0), (3, 1)])  1.23 us
    ppermute x3, waiting for transfers between devices, body(): lax.ppermute(adjoint if k < steps else held, 'inst', [(i, i ^ pair[i % 2]...  1.08 us
    ppermute x1, waiting for transfers between devices, body(): second = lax.ppermute(wrap, 'space', [(0, 3), (1, 2), (2, 0), (3, 1)])  0.78 us
  transfers between devices with their start and end apart: 8, of which 4 were waited for; matrix products, arithmetic and copies ran while one was open for 0% of the time, Pallas kernels for 8%

profile of v9, /device:TPU:0, one launch (start us, length us, event | category | flops | bytes accessed | tf_op | source)
XLA Modules:
  0.0 15.0 jit_solution(5747513609418602634)
XLA Ops:
  0.6 0.0 copy-start.1
  0.6 0.0 copy-start
  0.7 0.0 copy-start.5
  0.7 0.0 copy-start.7
  0.7 0.0 copy-start.4
  0.7 0.0 copy-start.8
  0.7 3.0 %collective-permute-start = (f32[1,5,4,16,128]{4,3,2,1,0:T(8,128)}, f32[1,5,4,16,128]{4,3,2,1,0:T(8,128)S(1)}, u32[]{:S(2)}, u32[]{:S(2)}) collective-permute-start(f32[1,5,4,16,128]{4,3,2,1,0:T(8,128)} %lam.5), channel_id=1, source_target_pairs={{0,8},{4,20},{8,0},{12,28},{16,24},{20,4},{24,16},{28,12},{1,9},{5... | collective-permute-start | bytes 491528 | tf_op jit(solution)/shard_map/ppermute | solution.py:244
  3.7 1.5 %collective-permute-start.1 = (f32[1,5,4,16,128]{4,3,2,1,0:T(8,128)}, f32[1,5,4,16,128]{4,3,2,1,0:T(8,128)S(1)}, u32[]{:S(2)}, u32[]{:S(2)}) collective-permute-start(f32[1,5,4,16,128]{4,3,2,1,0:T(8,128)} %lam.5), channel_id=1, source_target_pairs={{0,16},{4,12},{8,24},{12,4},{16,0},{20,28},{24,8},{28,20},{1,17},{... | collective-permute-start | bytes 491528 | tf_op jit(solution)/shard_map/ppermute | solution.py:244
  5.2 0.0 copy-done.1
  5.2 0.1 collective-permute-start.5
  5.3 0.0 copy-done
  5.4 0.0 copy-start.2
  5.4 0.4 %prep.1 = (f32[88,128]{1,0:T(8,128)S(1)}, f32[88,128]{1,0:T(8,128)S(1)}, f32[8,128]{1,0:T(8,128)S(1)}, f32[4,40,128]{2,1,0:T(8,128)S(1)}) custom-call(f32[1,1]{1,0:T(1,128)S(4)} %table.1.token, f32[1,5,4,16,128]{4,3,2,1,0:T(8,128)S(1)} %copy-done.1, f32[5,4,128]{2,1,0:T(4,128)S(1)} %copy-done.5, s32[4,128]{1,0:T(4,128)S(1)} %copy-done.7, ...), custom_call_target="tpu_custom_call" | custom-call | tf_op jit(solution)/shard_map/prep/pallas_call | solution.py:228
  5.8 2.6 %collective-permute-start.3 = (f32[88,128]{1,0:T(8,128)S(1)}, f32[88,128]{1,0:T(8,128)S(1)}, u32[]{:S(2)}, u32[]{:S(2)}) collective-permute-start(f32[88,128]{1,0:T(8,128)S(1)} %get-tuple-element.14), channel_id=1, source_target_pairs={{3,0},{2,1},{0,2},{1,3},{7,4},{6,5},{4,6},{5,7},{11,8},{10,9},{8,1... | collective-permute-start | bytes 135176 | tf_op jit(solution)/shard_map/ppermute | solution.py:268
  8.4 1.2 %collective-permute-start.4 = (f32[88,128]{1,0:T(8,128)S(1)}, f32[88,128]{1,0:T(8,128)S(1)}, u32[]{:S(2)}, u32[]{:S(2)}) collective-permute-start(f32[88,128]{1,0:T(8,128)S(1)} %get-tuple-element.14), channel_id=1, source_target_pairs={{0,3},{1,2},{2,0},{3,1},{4,7},{5,6},{6,4},{7,5},{8,11},{9,10},{10,... | collective-permute-start | bytes 135176 | tf_op jit(solution)/shard_map/ppermute | solution.py:269
  9.6 0.0 collective-permute-done.after.refs_1_
  9.6 1.4 %collective-permute-start.2 = (f32[88,128]{1,0:T(8,128)S(1)}, f32[88,128]{1,0:T(8,128)S(1)}, u32[]{:S(2)}, u32[]{:S(2)}) collective-permute-start(f32[88,128]{1,0:T(8,128)S(1)} %get-tuple-element.12), channel_id=1, source_target_pairs={{0,1},{1,0},{2,3},{3,2},{4,5},{5,4},{6,7},{7,6},{8,9},{9,8},{10,11... | collective-permute-start | bytes 135176 | tf_op jit(solution)/shard_map/ppermute | solution.py:222
  11.0 0.5 %flux.1.partial = f32[1,5,4,16,128]{4,3,2,1,0:T(8,128)S(1)} custom-call(f32[1,5,4,16,128]{4,3,2,1,0:T(8,128)S(1)} %collective-permute-done.after.refs_1_, f32[1,5,4,16,128]{4,3,2,1,0:T(8,128)S(1)} %copy-done.1, f32[1,5,4,16,128]{4,3,2,1,0:T(8,128)S(1)} %copy-done.3, f32[1,7,5,5,4,16,128]{6,5,4,3,2,1,0:T(8,128)S(1)} %copy-done), custom_call_target="tpu_custom_call" | custom-call | flops 2867200 | tf_op jit(solution)/shard_map/flux/pallas_call | solution.py:228
  11.5 0.0 copy-start.6
  11.5 0.4 %collective-permute-done.1.refs_2_ = f32[1,5,4,16,128]{4,3,2,1,0:T(8,128)S(1)} collective-permute-done((f32[1,5,4,16,128]{4,3,2,1,0:T(8,128)}, f32[1,5,4,16,128]{4,3,2,1,0:T(8,128)S(1)}, u32[]{:S(2)}, u32[]{:S(2)}) %collective-permute-start.1) | collective-permute-done | bytes 163872 | tf_op jit(solution)/shard_map/ppermute | solution.py:244
  11.9 0.0 copy-done.2
  11.9 0.1 share.1
  12.0 0.1 collective-permute-start.6
  12.1 0.7 %collective-permute-done.5.refs_0_ = f32[1,5,4,16,128]{4,3,2,1,0:T(8,128)S(1)} collective-permute-done((f32[1,5,4,16,128]{4,3,2,1,0:T(8,128)S(1)}, f32[1,5,4,16,128]{4,3,2,1,0:T(8,128)S(1)}, u32[]{:S(2)}, u32[]{:S(2)}) %collective-permute-start.5) | collective-permute-done | bytes 163872 | tf_op jit(solution)/shard_map/ppermute | solution.py:244
  12.8 0.3 %collective-permute-start.7 = (f32[1,5,4,16,128]{4,3,2,1,0:T(8,128)S(1)}, f32[1,5,4,16,128]{4,3,2,1,0:T(8,128)S(1)}, u32[]{:S(2)}, u32[]{:S(2)}) collective-permute-start(f32[1,5,4,16,128]{4,3,2,1,0:T(8,128)S(1)} %collective-permute-done.5.refs_0_), channel_id=1, source_target_pairs={{0,4},{4,0},{8,12},{12,8},{16,20},{20,16},{24,28},{28,24},{1,5},{5... | collective-permute-start | bytes 491528 | tf_op jit(solution)/shard_map/ppermute | solution.py:222
  13.0 0.0 collective-permute-done.3.first
  13.0 0.8 %collective-permute-done.4.second = f32[88,128]{1,0:T(8,128)S(1)} collective-permute-done((f32[88,128]{1,0:T(8,128)S(1)}, f32[88,128]{1,0:T(8,128)S(1)}, u32[]{:S(2)}, u32[]{:S(2)}) %collective-permute-start.4) | collective-permute-done | bytes 45088 | tf_op jit(solution)/shard_map/ppermute | solution.py:269
  13.8 0.2 %collective-permute-done.2.near = f32[88,128]{1,0:T(8,128)S(1)} collective-permute-done((f32[88,128]{1,0:T(8,128)S(1)}, f32[88,128]{1,0:T(8,128)S(1)}, u32[]{:S(2)}, u32[]{:S(2)}) %collective-permute-start.2) | collective-permute-done | bytes 45088 | tf_op jit(solution)/shard_map/ppermute | solution.py:222
  14.1 0.2 %beam.1 = (f32[1,5,4,16,128]{4,3,2,1,0:T(8,128)S(1)}, f32[1,40]{1,0:T(1,128)S(1)}) custom-call(f32[1,5,4,16,128]{4,3,2,1,0:T(8,128)S(1)} %get-tuple-element.10.partial, f32[4,16,128]{2,1,0:T(8,128)S(1)} %copy-done.2, f32[4,40,128]{2,1,0:T(8,128)S(1)} %get-tuple-element.11.modes, f32[5,4,128]{2,1,0:T(4,128)S(1)} %copy-done.6, ...), custom_call_target="tpu_custom_call" | custom-call | tf_op jit(solution)/shard_map/beam/pallas_call | solution.py:228
  14.2 0.0 collective-permute-done.6.mix
  14.2 0.0 collective-permute-done.7.refs_0_
  14.2 0.7 %final.1 = (f32[1,5,4,16,128]{4,3,2,1,0:T(8,128)}, f32[1,40]{1,0:T(1,128)}) custom-call(f32[1,5,4,16,128]{4,3,2,1,0:T(8,128)S(1)} %get-tuple-element.15.partial, f32[4,16,128]{2,1,0:T(8,128)S(1)} %copy-done.2, f32[1,40]{1,0:T(1,128)S(1)} %get-tuple-element.16.line, f32[1,5,4,16,128]{4,3,2,1,0:T(8,128)S(1)} %collective-permute-done.6.mix, ...), custom_call_target="tpu_custom_call" | custom-call | tf_op jit(solution)/shard_map/final/pallas_call | solution.py:228
  (10 shorter events, 0.0 us)
Async XLA Ops:
  0.6 4.6 %copy-start.1 = (f32[1,5,4,16,128]{4,3,2,1,0:T(8,128)S(1)}, f32[1,5,4,16,128]{4,3,2,1,0:T(8,128)}, u32[]{:S(2)}) copy-start(f32[1,5,4,16,128]{4,3,2,1,0:T(8,128)} %lam.5) | copy-start | bytes 491524
  0.6 4.7 %copy-start = (f32[1,7,5,5,4,16,128]{6,5,4,3,2,1,0:T(8,128)S(1)}, f32[1,7,5,5,4,16,128]{6,5,4,3,2,1,0:T(8,128)}, u32[]{:S(2)}) copy-start(f32[1,7,5,5,4,16,128]{6,5,4,3,2,1,0:T(8,128)} %jac.3) | copy-start | bytes 17203204
  0.7 4.7 %copy-start.5 = (f32[5,4,128]{2,1,0:T(4,128)S(1)}, f32[5,4,128]{2,1,0:T(4,128)}, u32[]{:S(2)}) copy-start(f32[5,4,128]{2,1,0:T(4,128)} %outward.1) | copy-start | bytes 30724
  0.7 4.7 %copy-start.7 = (s32[4,128]{1,0:T(4,128)S(1)}, s32[4,128]{1,0:T(4,128)}, u32[]{:S(2)}) copy-start(s32[4,128]{1,0:T(4,128)} %station.1) | copy-start | bytes 6148
  0.7 4.7 %copy-start.4 = (f32[40,256]{1,0:T(8,128)S(1)}, f32[40,256]{1,0:T(8,128)}, u32[]{:S(2)}) copy-start(f32[40,256]{1,0:T(8,128)} %phi.1) | copy-start | bytes 122884
  0.7 4.7 %copy-start.8 = (f32[40]{0:T(128)S(1)}, f32[40]{0:T(128)}, u32[]{:S(2)}) copy-start(f32[40]{0:T(128)} %param.17) | copy-start | bytes 484
  0.7 8.9 %collective-permute-start = (f32[1,5,4,16,128]{4,3,2,1,0:T(8,128)}, f32[1,5,4,16,128]{4,3,2,1,0:T(8,128)S(1)}, u32[]{:S(2)}, u32[]{:S(2)}) collective-permute-start(f32[1,5,4,16,128]{4,3,2,1,0:T(8,128)} %lam.5), channel_id=1, source_target_pairs={{0,8},{4,20},{8,0},{12,28},{16,24},{20,4},{24,16},{28,12},{1,9},{5... | collective-permute-start | bytes 491528 | tf_op jit(solution)/shard_map/ppermute | solution.py:244
  3.7 8.2 %collective-permute-start.1 = (f32[1,5,4,16,128]{4,3,2,1,0:T(8,128)}, f32[1,5,4,16,128]{4,3,2,1,0:T(8,128)S(1)}, u32[]{:S(2)}, u32[]{:S(2)}) collective-permute-start(f32[1,5,4,16,128]{4,3,2,1,0:T(8,128)} %lam.5), channel_id=1, source_target_pairs={{0,16},{4,12},{8,24},{12,4},{16,0},{20,28},{24,8},{28,20},{1,17},{... | collective-permute-start | bytes 491528 | tf_op jit(solution)/shard_map/ppermute | solution.py:244
  5.2 5.7 %copy-start.3 = (f32[1,5,4,16,128]{4,3,2,1,0:T(8,128)S(1)}, f32[1,5,4,16,128]{4,3,2,1,0:T(8,128)}, u32[]{:S(2)}) copy-start(f32[1,5,4,16,128]{4,3,2,1,0:T(8,128)} %source.1) | copy-start | bytes 491524
  5.2 7.5 %collective-permute-start.5 = (f32[1,5,4,16,128]{4,3,2,1,0:T(8,128)S(1)}, f32[1,5,4,16,128]{4,3,2,1,0:T(8,128)S(1)}, u32[]{:S(2)}, u32[]{:S(2)}) collective-permute-start(f32[1,5,4,16,128]{4,3,2,1,0:T(8,128)S(1)} %hold.1), channel_id=1, source_target_pairs={{0,28},{4,24},{8,20},{12,16},{16,12},{20,8},{24,4},{28,0},{1,29},{... | collective-permute-start | bytes 491528 | tf_op jit(solution)/shard_map/ppermute | solution.py:244
  5.4 6.5 %copy-start.2 = (f32[4,16,128]{2,1,0:T(8,128)S(1)}, f32[4,16,128]{2,1,0:T(8,128)}, u32[]{:S(2)}) copy-start(f32[4,16,128]{2,1,0:T(8,128)} %volume.5) | copy-start | bytes 98308
  5.8 7.3 %collective-permute-start.3 = (f32[88,128]{1,0:T(8,128)S(1)}, f32[88,128]{1,0:T(8,128)S(1)}, u32[]{:S(2)}, u32[]{:S(2)}) collective-permute-start(f32[88,128]{1,0:T(8,128)S(1)} %get-tuple-element.14), channel_id=1, source_target_pairs={{3,0},{2,1},{0,2},{1,3},{7,4},{6,5},{4,6},{5,7},{11,8},{10,9},{8,1... | collective-permute-start | bytes 135176 | tf_op jit(solution)/shard_map/ppermute | solution.py:268
  8.4 5.4 %collective-permute-start.4 = (f32[88,128]{1,0:T(8,128)S(1)}, f32[88,128]{1,0:T(8,128)S(1)}, u32[]{:S(2)}, u32[]{:S(2)}) collective-permute-start(f32[88,128]{1,0:T(8,128)S(1)} %get-tuple-element.14), channel_id=1, source_target_pairs={{0,3},{1,2},{2,0},{3,1},{4,7},{5,6},{6,4},{7,5},{8,11},{9,10},{10,... | collective-permute-start | bytes 135176 | tf_op jit(solution)/shard_map/ppermute | solution.py:269
  9.6 4.5 %collective-permute-start.2 = (f32[88,128]{1,0:T(8,128)S(1)}, f32[88,128]{1,0:T(8,128)S(1)}, u32[]{:S(2)}, u32[]{:S(2)}) collective-permute-start(f32[88,128]{1,0:T(8,128)S(1)} %get-tuple-element.12), channel_id=1, source_target_pairs={{0,1},{1,0},{2,3},{3,2},{4,5},{5,4},{6,7},{7,6},{8,9},{9,8},{10,11... | collective-permute-start | bytes 135176 | tf_op jit(solution)/shard_map/ppermute | solution.py:222
  11.5 2.6 %copy-start.6 = (f32[5,4,128]{2,1,0:T(4,128)S(1)}, f32[5,4,128]{2,1,0:T(4,128)}, u32[]{:S(2)}) copy-start(f32[5,4,128]{2,1,0:T(4,128)} %surface_in.1) | copy-start | bytes 30724
  12.0 2.2 %collective-permute-start.6 = (f32[1,5,4,16,128]{4,3,2,1,0:T(8,128)S(1)}, f32[1,5,4,16,128]{4,3,2,1,0:T(8,128)S(1)}, u32[]{:S(2)}, u32[]{:S(2)}) collective-permute-start(f32[1,5,4,16,128]{4,3,2,1,0:T(8,128)S(1)} %get-tuple-element.17), channel_id=1, source_target_pairs={{0,4},{4,0},{8,12},{12,8},{16,20},{20,16},{24,28},{28,24},{1,5},{5... | collective-permute-start | bytes 491528 | tf_op jit(solution)/shard_map/ppermute | solution.py:222
  12.8 1.5 %collective-permute-start.7 = (f32[1,5,4,16,128]{4,3,2,1,0:T(8,128)S(1)}, f32[1,5,4,16,128]{4,3,2,1,0:T(8,128)S(1)}, u32[]{:S(2)}, u32[]{:S(2)}) collective-permute-start(f32[1,5,4,16,128]{4,3,2,1,0:T(8,128)S(1)} %collective-permute-done.5.refs_0_), channel_id=1, source_target_pairs={{0,4},{4,0},{8,12},{12,8},{16,20},{20,16},{24,28},{28,24},{1,5},{5... | collective-permute-start | bytes 491528 | tf_op jit(solution)/shard_map/ppermute | solution.py:222

commit v10 on v9

--- a/solution.py
+++ b/solution.py
@@ -90,7 +90,7 @@
         for j in range(1, nv):
             face = face + outward[j, x : x + 1, :] * lam[0, j, x, 0:1, :]
         share = share + at_face * face
-    lax.fori_loop(0, nv, columns, 0)
+    lax.fori_loop(0, nv, columns, 0, unroll=True)
     row = lax.broadcasted_iota(jnp.int32, (modes_k, modes_k), 0)
     lane = lax.broadcasted_iota(jnp.int32, (modes_k, modes_k), 1)
     stiff = jnp.sum(jnp.where(row == lane, inv_stiff[...], 0.0), axis=1, keepdims=True)
@@ -121,7 +121,7 @@
         own[0, j] = volume[...] * here(j) + partial[0, j]
         return carry
 
-    lax.fori_loop(0, out.shape[1], columns, 0)
+    lax.fori_loop(0, out.shape[1], columns, 0, unroll=True)
 
 
 def flux_kernel(after, lam, source, jac, out):
@@ -149,7 +149,7 @@
             out[0, j, x] = total
         return carry
 
-    lax.fori_loop(0, nv, columns, 0)
+    lax.fori_loop(0, nv, columns, 0, unroll=True)
 
 
 def pick_kernel(packed, first, second, out):
@@ -197,7 +197,7 @@
             out[0, j, x] = value + jnp.where(low, inward[x : x + 1, :] * backs[x], 0.0)
         return carry
 
-    lax.fori_loop(0, nv, step, 0)
+    lax.fori_loop(0, nv, step, 0, unroll=True)
 
 
 def final_kernel(partial, volume, line, mix, *refs):
@@ -209,7 +209,7 @@
         out[0, j] = partial[0, j] + volume[...] * (mix[0, j] + rest(j))
         return carry
 
-    lax.fori_loop(0, out.shape[1], columns, 0)
+    lax.fori_loop(0, out.shape[1], columns, 0, unroll=True)
 
 
 def body(adjoint, jacobian, volume, source, surface_out, surface_in, station, phi, inv_stiff):

time: 15.1 us -> 15 us (level)
  Pallas kernels: 1.92 us -> 1.65 us
    pallas_call x8, Pallas kernels: 1.92 us -> 1.65 us  [call(): pl.pallas_call(kernel, out_shape=out_shape, in_specs=[VMEM] * len(operand...]
  transfers between devices with their start and end apart: 8 -> 8, of which waited for: 4 -> 4; matrix products, arithmetic and copies ran while one was open for 0% -> 0% of each run, Pallas kernels for 8% -> 6%
where the time goes in v10:
time: 15 us; the launch traced here: 14.9 us
  starting transfers between devices  10.2 us (68%)
  waiting for transfers between devices  2.19 us (15%)
  Pallas kernels  1.65 us (11%)
  between operations  0.78 us (5%)
    ppermute x3, starting transfers between devices, body(): lax.ppermute(adjoint if k < steps else held, 'inst', [(i, i ^ pair[i % 2]...  4.59 us
    ppermute x1, starting transfers between devices, body(): first = lax.ppermute(wrap, 'space', [(3, 0), (2, 1), (0, 2), (1, 3)])  2.63 us
    ppermute x3, starting transfers between devices, swap(): return lax.ppermute(value, axis, [(i, i ^ mask) for i in range(size)])  1.73 us
    pallas_call x8, Pallas kernels, call(): pl.pallas_call(kernel, out_shape=out_shape, in_specs=[VMEM] * len(operand...  1.65 us
    ppermute x1, starting transfers between devices, body(): second = lax.ppermute(wrap, 'space', [(0, 3), (1, 2), (2, 0), (3, 1)])  1.23 us
    ppermute x3, waiting for transfers between devices, body(): lax.ppermute(adjoint if k < steps else held, 'inst', [(i, i ^ pair[i % 2]...  1.18 us
    ppermute x1, waiting for transfers between devices, body(): second = lax.ppermute(wrap, 'space', [(0, 3), (1, 2), (2, 0), (3, 1)])  0.74 us
  transfers between devices with their start and end apart: 8, of which 4 were waited for; matrix products, arithmetic and copies ran while one was open for 0% of the time, Pallas kernels for 6%

profile of v10, /device:TPU:0, one launch (start us, length us, event | category | flops | bytes accessed | tf_op | source)
XLA Modules:
  0.0 14.9 jit_solution(2728590496534956766)
XLA Ops:
  0.6 0.0 copy-start.1
  0.6 0.0 copy-start
  0.7 0.0 copy-start.5
  0.7 0.0 copy-start.7
  0.7 0.0 copy-start.4
  0.7 0.0 copy-start.8
  0.7 3.0 %collective-permute-start = (f32[1,5,4,16,128]{4,3,2,1,0:T(8,128)}, f32[1,5,4,16,128]{4,3,2,1,0:T(8,128)S(1)}, u32[]{:S(2)}, u32[]{:S(2)}) collective-permute-start(f32[1,5,4,16,128]{4,3,2,1,0:T(8,128)} %lam.5), channel_id=1, source_target_pairs={{0,8},{4,20},{8,0},{12,28},{16,24},{20,4},{24,16},{28,12},{1,9},{5... | collective-permute-start | bytes 491528 | tf_op jit(solution)/shard_map/ppermute | solution.py:244
  3.7 1.5 %collective-permute-start.1 = (f32[1,5,4,16,128]{4,3,2,1,0:T(8,128)}, f32[1,5,4,16,128]{4,3,2,1,0:T(8,128)S(1)}, u32[]{:S(2)}, u32[]{:S(2)}) collective-permute-start(f32[1,5,4,16,128]{4,3,2,1,0:T(8,128)} %lam.5), channel_id=1, source_target_pairs={{0,16},{4,12},{8,24},{12,4},{16,0},{20,28},{24,8},{28,20},{1,17},{... | collective-permute-start | bytes 491528 | tf_op jit(solution)/shard_map/ppermute | solution.py:244
  5.2 0.0 copy-done.1
  5.2 0.1 collective-permute-start.5
  5.3 0.0 copy-done
  5.4 0.0 copy-start.2
  5.4 0.3 %prep.1 = (f32[88,128]{1,0:T(8,128)S(1)}, f32[88,128]{1,0:T(8,128)S(1)}, f32[8,128]{1,0:T(8,128)S(1)}, f32[4,40,128]{2,1,0:T(8,128)S(1)}) custom-call(f32[1,1]{1,0:T(1,128)S(4)} %table.1.token, f32[1,5,4,16,128]{4,3,2,1,0:T(8,128)S(1)} %copy-done.1, f32[5,4,128]{2,1,0:T(4,128)S(1)} %copy-done.5, s32[4,128]{1,0:T(4,128)S(1)} %copy-done.7, ...), custom_call_target="tpu_custom_call" | custom-call | tf_op jit(solution)/shard_map/prep/pallas_call | solution.py:228
  5.7 2.6 %collective-permute-start.3 = (f32[88,128]{1,0:T(8,128)S(1)}, f32[88,128]{1,0:T(8,128)S(1)}, u32[]{:S(2)}, u32[]{:S(2)}) collective-permute-start(f32[88,128]{1,0:T(8,128)S(1)} %get-tuple-element.14), channel_id=1, source_target_pairs={{3,0},{2,1},{0,2},{1,3},{7,4},{6,5},{4,6},{5,7},{11,8},{10,9},{8,1... | collective-permute-start | bytes 135176 | tf_op jit(solution)/shard_map/ppermute | solution.py:268
  8.3 1.2 %collective-permute-start.4 = (f32[88,128]{1,0:T(8,128)S(1)}, f32[88,128]{1,0:T(8,128)S(1)}, u32[]{:S(2)}, u32[]{:S(2)}) collective-permute-start(f32[88,128]{1,0:T(8,128)S(1)} %get-tuple-element.14), channel_id=1, source_target_pairs={{0,3},{1,2},{2,0},{3,1},{4,7},{5,6},{6,4},{7,5},{8,11},{9,10},{10,... | collective-permute-start | bytes 135176 | tf_op jit(solution)/shard_map/ppermute | solution.py:269
  9.5 0.0 collective-permute-done.after.refs_1_
  9.5 1.4 %collective-permute-start.2 = (f32[88,128]{1,0:T(8,128)S(1)}, f32[88,128]{1,0:T(8,128)S(1)}, u32[]{:S(2)}, u32[]{:S(2)}) collective-permute-start(f32[88,128]{1,0:T(8,128)S(1)} %get-tuple-element.12), channel_id=1, source_target_pairs={{0,1},{1,0},{2,3},{3,2},{4,5},{5,4},{6,7},{7,6},{8,9},{9,8},{10,11... | collective-permute-start | bytes 135176 | tf_op jit(solution)/shard_map/ppermute | solution.py:222
  11.0 0.4 %flux.1.partial = f32[1,5,4,16,128]{4,3,2,1,0:T(8,128)S(1)} custom-call(f32[1,5,4,16,128]{4,3,2,1,0:T(8,128)S(1)} %collective-permute-done.after.refs_1_, f32[1,5,4,16,128]{4,3,2,1,0:T(8,128)S(1)} %copy-done.1, f32[1,5,4,16,128]{4,3,2,1,0:T(8,128)S(1)} %copy-done.3, f32[1,7,5,5,4,16,128]{6,5,4,3,2,1,0:T(8,128)S(1)} %copy-done), custom_call_target="tpu_custom_call" | custom-call | flops 2867200 | tf_op jit(solution)/shard_map/flux/pallas_call | solution.py:228
  11.4 0.0 copy-start.6
  11.4 0.5 %collective-permute-done.1.refs_2_ = f32[1,5,4,16,128]{4,3,2,1,0:T(8,128)S(1)} collective-permute-done((f32[1,5,4,16,128]{4,3,2,1,0:T(8,128)}, f32[1,5,4,16,128]{4,3,2,1,0:T(8,128)S(1)}, u32[]{:S(2)}, u32[]{:S(2)}) %collective-permute-start.1) | collective-permute-done | bytes 163872 | tf_op jit(solution)/shard_map/ppermute | solution.py:244
  11.9 0.1 share.1
  12.0 0.1 collective-permute-start.6
  12.1 0.7 %collective-permute-done.5.refs_0_ = f32[1,5,4,16,128]{4,3,2,1,0:T(8,128)S(1)} collective-permute-done((f32[1,5,4,16,128]{4,3,2,1,0:T(8,128)S(1)}, f32[1,5,4,16,128]{4,3,2,1,0:T(8,128)S(1)}, u32[]{:S(2)}, u32[]{:S(2)}) %collective-permute-start.5) | collective-permute-done | bytes 163872 | tf_op jit(solution)/shard_map/ppermute | solution.py:244
  12.8 0.3 %collective-permute-start.7 = (f32[1,5,4,16,128]{4,3,2,1,0:T(8,128)S(1)}, f32[1,5,4,16,128]{4,3,2,1,0:T(8,128)S(1)}, u32[]{:S(2)}, u32[]{:S(2)}) collective-permute-start(f32[1,5,4,16,128]{4,3,2,1,0:T(8,128)S(1)} %collective-permute-done.5.refs_0_), channel_id=1, source_target_pairs={{0,4},{4,0},{8,12},{12,8},{16,20},{20,16},{24,28},{28,24},{1,5},{5... | collective-permute-start | bytes 491528 | tf_op jit(solution)/shard_map/ppermute | solution.py:222
  13.0 0.0 collective-permute-done.3.first
  13.0 0.7 %collective-permute-done.4.second = f32[88,128]{1,0:T(8,128)S(1)} collective-permute-done((f32[88,128]{1,0:T(8,128)S(1)}, f32[88,128]{1,0:T(8,128)S(1)}, u32[]{:S(2)}, u32[]{:S(2)}) %collective-permute-start.4) | collective-permute-done | bytes 45088 | tf_op jit(solution)/shard_map/ppermute | solution.py:269
  13.8 0.2 %collective-permute-done.2.near = f32[88,128]{1,0:T(8,128)S(1)} collective-permute-done((f32[88,128]{1,0:T(8,128)S(1)}, f32[88,128]{1,0:T(8,128)S(1)}, u32[]{:S(2)}, u32[]{:S(2)}) %collective-permute-start.2) | collective-permute-done | bytes 45088 | tf_op jit(solution)/shard_map/ppermute | solution.py:222
  14.0 0.0 copy-done.6
  14.0 0.1 beam.1
  14.1 0.0 collective-permute-done.6.mix
  14.1 0.0 collective-permute-done.7.refs_0_
  14.2 0.7 %final.1 = (f32[1,5,4,16,128]{4,3,2,1,0:T(8,128)}, f32[1,40]{1,0:T(1,128)}) custom-call(f32[1,5,4,16,128]{4,3,2,1,0:T(8,128)S(1)} %get-tuple-element.15.partial, f32[4,16,128]{2,1,0:T(8,128)S(1)} %copy-done.2, f32[1,40]{1,0:T(1,128)S(1)} %get-tuple-element.16.line, f32[1,5,4,16,128]{4,3,2,1,0:T(8,128)S(1)} %collective-permute-done.6.mix, ...), custom_call_target="tpu_custom_call" | custom-call | tf_op jit(solution)/shard_map/final/pallas_call | solution.py:228
  (10 shorter events, 0.0 us)
Async XLA Ops:
  0.6 4.6 %copy-start.1 = (f32[1,5,4,16,128]{4,3,2,1,0:T(8,128)S(1)}, f32[1,5,4,16,128]{4,3,2,1,0:T(8,128)}, u32[]{:S(2)}) copy-start(f32[1,5,4,16,128]{4,3,2,1,0:T(8,128)} %lam.5) | copy-start | bytes 491524
  0.6 4.7 %copy-start = (f32[1,7,5,5,4,16,128]{6,5,4,3,2,1,0:T(8,128)S(1)}, f32[1,7,5,5,4,16,128]{6,5,4,3,2,1,0:T(8,128)}, u32[]{:S(2)}) copy-start(f32[1,7,5,5,4,16,128]{6,5,4,3,2,1,0:T(8,128)} %jac.3) | copy-start | bytes 17203204
  0.7 4.7 %copy-start.5 = (f32[5,4,128]{2,1,0:T(4,128)S(1)}, f32[5,4,128]{2,1,0:T(4,128)}, u32[]{:S(2)}) copy-start(f32[5,4,128]{2,1,0:T(4,128)} %outward.1) | copy-start | bytes 30724
  0.7 4.7 %copy-start.7 = (s32[4,128]{1,0:T(4,128)S(1)}, s32[4,128]{1,0:T(4,128)}, u32[]{:S(2)}) copy-start(s32[4,128]{1,0:T(4,128)} %station.1) | copy-start | bytes 6148
  0.7 4.7 %copy-start.4 = (f32[40,256]{1,0:T(8,128)S(1)}, f32[40,256]{1,0:T(8,128)}, u32[]{:S(2)}) copy-start(f32[40,256]{1,0:T(8,128)} %phi.1) | copy-start | bytes 122884
  0.7 4.7 %copy-start.8 = (f32[40]{0:T(128)S(1)}, f32[40]{0:T(128)}, u32[]{:S(2)}) copy-start(f32[40]{0:T(128)} %param.17) | copy-start | bytes 484
  0.7 8.9 %collective-permute-start = (f32[1,5,4,16,128]{4,3,2,1,0:T(8,128)}, f32[1,5,4,16,128]{4,3,2,1,0:T(8,128)S(1)}, u32[]{:S(2)}, u32[]{:S(2)}) collective-permute-start(f32[1,5,4,16,128]{4,3,2,1,0:T(8,128)} %lam.5), channel_id=1, source_target_pairs={{0,8},{4,20},{8,0},{12,28},{16,24},{20,4},{24,16},{28,12},{1,9},{5... | collective-permute-start | bytes 491528 | tf_op jit(solution)/shard_map/ppermute | solution.py:244
  3.7 8.2 %collective-permute-start.1 = (f32[1,5,4,16,128]{4,3,2,1,0:T(8,128)}, f32[1,5,4,16,128]{4,3,2,1,0:T(8,128)S(1)}, u32[]{:S(2)}, u32[]{:S(2)}) collective-permute-start(f32[1,5,4,16,128]{4,3,2,1,0:T(8,128)} %lam.5), channel_id=1, source_target_pairs={{0,16},{4,12},{8,24},{12,4},{16,0},{20,28},{24,8},{28,20},{1,17},{... | collective-permute-start | bytes 491528 | tf_op jit(solution)/shard_map/ppermute | solution.py:244
  5.2 5.7 %copy-start.3 = (f32[1,5,4,16,128]{4,3,2,1,0:T(8,128)S(1)}, f32[1,5,4,16,128]{4,3,2,1,0:T(8,128)}, u32[]{:S(2)}) copy-start(f32[1,5,4,16,128]{4,3,2,1,0:T(8,128)} %source.1) | copy-start | bytes 491524
  5.2 7.5 %collective-permute-start.5 = (f32[1,5,4,16,128]{4,3,2,1,0:T(8,128)S(1)}, f32[1,5,4,16,128]{4,3,2,1,0:T(8,128)S(1)}, u32[]{:S(2)}, u32[]{:S(2)}) collective-permute-start(f32[1,5,4,16,128]{4,3,2,1,0:T(8,128)S(1)} %hold.1), channel_id=1, source_target_pairs={{0,28},{4,24},{8,20},{12,16},{16,12},{20,8},{24,4},{28,0},{1,29},{... | collective-permute-start | bytes 491528 | tf_op jit(solution)/shard_map/ppermute | solution.py:244
  5.4 6.5 %copy-start.2 = (f32[4,16,128]{2,1,0:T(8,128)S(1)}, f32[4,16,128]{2,1,0:T(8,128)}, u32[]{:S(2)}) copy-start(f32[4,16,128]{2,1,0:T(8,128)} %volume.5) | copy-start | bytes 98308
  5.7 7.3 %collective-permute-start.3 = (f32[88,128]{1,0:T(8,128)S(1)}, f32[88,128]{1,0:T(8,128)S(1)}, u32[]{:S(2)}, u32[]{:S(2)}) collective-permute-start(f32[88,128]{1,0:T(8,128)S(1)} %get-tuple-element.14), channel_id=1, source_target_pairs={{3,0},{2,1},{0,2},{1,3},{7,4},{6,5},{4,6},{5,7},{11,8},{10,9},{8,1... | collective-permute-start | bytes 135176 | tf_op jit(solution)/shard_map/ppermute | solution.py:268
  8.3 5.4 %collective-permute-start.4 = (f32[88,128]{1,0:T(8,128)S(1)}, f32[88,128]{1,0:T(8,128)S(1)}, u32[]{:S(2)}, u32[]{:S(2)}) collective-permute-start(f32[88,128]{1,0:T(8,128)S(1)} %get-tuple-element.14), channel_id=1, source_target_pairs={{0,3},{1,2},{2,0},{3,1},{4,7},{5,6},{6,4},{7,5},{8,11},{9,10},{10,... | collective-permute-start | bytes 135176 | tf_op jit(solution)/shard_map/ppermute | solution.py:269
  9.5 4.5 %collective-permute-start.2 = (f32[88,128]{1,0:T(8,128)S(1)}, f32[88,128]{1,0:T(8,128)S(1)}, u32[]{:S(2)}, u32[]{:S(2)}) collective-permute-start(f32[88,128]{1,0:T(8,128)S(1)} %get-tuple-element.12), channel_id=1, source_target_pairs={{0,1},{1,0},{2,3},{3,2},{4,5},{5,4},{6,7},{7,6},{8,9},{9,8},{10,11... | collective-permute-start | bytes 135176 | tf_op jit(solution)/shard_map/ppermute | solution.py:222
  11.4 2.6 %copy-start.6 = (f32[5,4,128]{2,1,0:T(4,128)S(1)}, f32[5,4,128]{2,1,0:T(4,128)}, u32[]{:S(2)}) copy-start(f32[5,4,128]{2,1,0:T(4,128)} %surface_in.1) | copy-start | bytes 30724
  12.0 2.1 %collective-permute-start.6 = (f32[1,5,4,16,128]{4,3,2,1,0:T(8,128)S(1)}, f32[1,5,4,16,128]{4,3,2,1,0:T(8,128)S(1)}, u32[]{:S(2)}, u32[]{:S(2)}) collective-permute-start(f32[1,5,4,16,128]{4,3,2,1,0:T(8,128)S(1)} %get-tuple-element.17), channel_id=1, source_target_pairs={{0,4},{4,0},{8,12},{12,8},{16,20},{20,16},{24,28},{28,24},{1,5},{5... | collective-permute-start | bytes 491528 | tf_op jit(solution)/shard_map/ppermute | solution.py:222
  12.8 1.4 %collective-permute-start.7 = (f32[1,5,4,16,128]{4,3,2,1,0:T(8,128)S(1)}, f32[1,5,4,16,128]{4,3,2,1,0:T(8,128)S(1)}, u32[]{:S(2)}, u32[]{:S(2)}) collective-permute-start(f32[1,5,4,16,128]{4,3,2,1,0:T(8,128)S(1)} %collective-permute-done.5.refs_0_), channel_id=1, source_target_pairs={{0,4},{4,0},{8,12},{12,8},{16,20},{20,16},{24,28},{28,24},{1,5},{5... | collective-permute-start | bytes 491528 | tf_op jit(solution)/shard_map/ppermute | solution.py:222

commit v11 on v10

--- a/solution.py
+++ b/solution.py
@@ -73,6 +73,9 @@
         return carry
 
     modes_k, stations = phi.shape
+    row = lax.broadcasted_iota(jnp.int32, (modes_k, modes_k), 0)
+    lane = lax.broadcasted_iota(jnp.int32, (modes_k, modes_k), 1)
+    stiff = jnp.sum(jnp.where(row == lane, inv_stiff[...], 0.0), axis=1, keepdims=True)
     full = phi[...]
     high = full.astype(jnp.bfloat16)
     rest = full - high.astype(F32)
@@ -91,9 +94,6 @@
             face = face + outward[j, x : x + 1, :] * lam[0, j, x, 0:1, :]
         share = share + at_face * face
     lax.fori_loop(0, nv, columns, 0, unroll=True)
-    row = lax.broadcasted_iota(jnp.int32, (modes_k, modes_k), 0)
-    lane = lax.broadcasted_iota(jnp.int32, (modes_k, modes_k), 1)
-    stiff = jnp.sum(jnp.where(row == lane, inv_stiff[...], 0.0), axis=1, keepdims=True)
     column = jnp.sum(share, axis=1, keepdims=True) * stiff
     tile_lane = lax.broadcasted_iota(jnp.int32, (8, nz), 1)
     tile = jnp.zeros((8, nz), F32)

time: 15 us -> 15 us (level)
  no operation moved by 1% of the time
where the time goes in v11:
time: 15 us; the launch traced here: 14.9 us
  starting transfers between devices  10.2 us (68%)
  waiting for transfers between devices  2.19 us (15%)
  Pallas kernels  1.65 us (11%)
  between operations  0.78 us (5%)
    ppermute x3, starting transfers between devices, body(): lax.ppermute(adjoint if k < steps else held, 'inst', [(i, i ^ pair[i % 2]...  4.59 us
    ppermute x1, starting transfers between devices, body(): first = lax.ppermute(wrap, 'space', [(3, 0), (2, 1), (0, 2), (1, 3)])  2.63 us
    ppermute x3, starting transfers between devices, swap(): return lax.ppermute(value, axis, [(i, i ^ mask) for i in range(size)])  1.73 us
    pallas_call x8, Pallas kernels, call(): pl.pallas_call(kernel, out_shape=out_shape, in_specs=[VMEM] * len(operand...  1.65 us
    ppermute x1, starting transfers between devices, body(): second = lax.ppermute(wrap, 'space', [(0, 3), (1, 2), (2, 0), (3, 1)])  1.23 us
    ppermute x3, waiting for transfers between devices, body(): lax.ppermute(adjoint if k < steps else held, 'inst', [(i, i ^ pair[i % 2]...  1.18 us
    ppermute x1, waiting for transfers between devices, body(): second = lax.ppermute(wrap, 'space', [(0, 3), (1, 2), (2, 0), (3, 1)])  0.74 us
  transfers between devices with their start and end apart: 8, of which 4 were waited for; matrix products, arithmetic and copies ran while one was open for 0% of the time, Pallas kernels for 6%

profile of v11, /device:TPU:0, one launch (start us, length us, event | category | flops | bytes accessed | tf_op | source)
XLA Modules:
  0.0 14.9 jit_solution(2728590496534956766)
XLA Ops:
  0.6 0.0 copy-start.1
  0.6 0.0 copy-start
  0.7 0.0 copy-start.5
  0.7 0.0 copy-start.7
  0.7 0.0 copy-start.4
  0.7 0.0 copy-start.8
  0.7 3.0 %collective-permute-start = (f32[1,5,4,16,128]{4,3,2,1,0:T(8,128)}, f32[1,5,4,16,128]{4,3,2,1,0:T(8,128)S(1)}, u32[]{:S(2)}, u32[]{:S(2)}) collective-permute-start(f32[1,5,4,16,128]{4,3,2,1,0:T(8,128)} %lam.5), channel_id=1, source_target_pairs={{0,8},{4,20},{8,0},{12,28},{16,24},{20,4},{24,16},{28,12},{1,9},{5... | collective-permute-start | bytes 491528 | tf_op jit(solution)/shard_map/ppermute | solution.py:244
  3.7 1.5 %collective-permute-start.1 = (f32[1,5,4,16,128]{4,3,2,1,0:T(8,128)}, f32[1,5,4,16,128]{4,3,2,1,0:T(8,128)S(1)}, u32[]{:S(2)}, u32[]{:S(2)}) collective-permute-start(f32[1,5,4,16,128]{4,3,2,1,0:T(8,128)} %lam.5), channel_id=1, source_target_pairs={{0,16},{4,12},{8,24},{12,4},{16,0},{20,28},{24,8},{28,20},{1,17},{... | collective-permute-start | bytes 491528 | tf_op jit(solution)/shard_map/ppermute | solution.py:244
  5.2 0.0 copy-done.1
  5.2 0.1 collective-permute-start.5
  5.3 0.0 copy-done
  5.4 0.0 copy-start.2
  5.4 0.3 %prep.1 = (f32[88,128]{1,0:T(8,128)S(1)}, f32[88,128]{1,0:T(8,128)S(1)}, f32[8,128]{1,0:T(8,128)S(1)}, f32[4,40,128]{2,1,0:T(8,128)S(1)}) custom-call(f32[1,1]{1,0:T(1,128)S(4)} %table.1.token, f32[1,5,4,16,128]{4,3,2,1,0:T(8,128)S(1)} %copy-done.1, f32[5,4,128]{2,1,0:T(4,128)S(1)} %copy-done.5, s32[4,128]{1,0:T(4,128)S(1)} %copy-done.7, ...), custom_call_target="tpu_custom_call" | custom-call | tf_op jit(solution)/shard_map/prep/pallas_call | solution.py:228
  5.7 2.6 %collective-permute-start.3 = (f32[88,128]{1,0:T(8,128)S(1)}, f32[88,128]{1,0:T(8,128)S(1)}, u32[]{:S(2)}, u32[]{:S(2)}) collective-permute-start(f32[88,128]{1,0:T(8,128)S(1)} %get-tuple-element.14), channel_id=1, source_target_pairs={{3,0},{2,1},{0,2},{1,3},{7,4},{6,5},{4,6},{5,7},{11,8},{10,9},{8,1... | collective-permute-start | bytes 135176 | tf_op jit(solution)/shard_map/ppermute | solution.py:268
  8.3 1.2 %collective-permute-start.4 = (f32[88,128]{1,0:T(8,128)S(1)}, f32[88,128]{1,0:T(8,128)S(1)}, u32[]{:S(2)}, u32[]{:S(2)}) collective-permute-start(f32[88,128]{1,0:T(8,128)S(1)} %get-tuple-element.14), channel_id=1, source_target_pairs={{0,3},{1,2},{2,0},{3,1},{4,7},{5,6},{6,4},{7,5},{8,11},{9,10},{10,... | collective-permute-start | bytes 135176 | tf_op jit(solution)/shard_map/ppermute | solution.py:269
  9.5 0.0 collective-permute-done.after.refs_1_
  9.5 1.4 %collective-permute-start.2 = (f32[88,128]{1,0:T(8,128)S(1)}, f32[88,128]{1,0:T(8,128)S(1)}, u32[]{:S(2)}, u32[]{:S(2)}) collective-permute-start(f32[88,128]{1,0:T(8,128)S(1)} %get-tuple-element.12), channel_id=1, source_target_pairs={{0,1},{1,0},{2,3},{3,2},{4,5},{5,4},{6,7},{7,6},{8,9},{9,8},{10,11... | collective-permute-start | bytes 135176 | tf_op jit(solution)/shard_map/ppermute | solution.py:222
  11.0 0.4 %flux.1.partial = f32[1,5,4,16,128]{4,3,2,1,0:T(8,128)S(1)} custom-call(f32[1,5,4,16,128]{4,3,2,1,0:T(8,128)S(1)} %collective-permute-done.after.refs_1_, f32[1,5,4,16,128]{4,3,2,1,0:T(8,128)S(1)} %copy-done.1, f32[1,5,4,16,128]{4,3,2,1,0:T(8,128)S(1)} %copy-done.3, f32[1,7,5,5,4,16,128]{6,5,4,3,2,1,0:T(8,128)S(1)} %copy-done), custom_call_target="tpu_custom_call" | custom-call | flops 2867200 | tf_op jit(solution)/shard_map/flux/pallas_call | solution.py:228
  11.4 0.0 copy-start.6
  11.4 0.5 %collective-permute-done.1.refs_2_ = f32[1,5,4,16,128]{4,3,2,1,0:T(8,128)S(1)} collective-permute-done((f32[1,5,4,16,128]{4,3,2,1,0:T(8,128)}, f32[1,5,4,16,128]{4,3,2,1,0:T(8,128)S(1)}, u32[]{:S(2)}, u32[]{:S(2)}) %collective-permute-start.1) | collective-permute-done | bytes 163872 | tf_op jit(solution)/shard_map/ppermute | solution.py:244
  11.9 0.1 share.1
  12.0 0.1 collective-permute-start.6
  12.1 0.7 %collective-permute-done.5.refs_0_ = f32[1,5,4,16,128]{4,3,2,1,0:T(8,128)S(1)} collective-permute-done((f32[1,5,4,16,128]{4,3,2,1,0:T(8,128)S(1)}, f32[1,5,4,16,128]{4,3,2,1,0:T(8,128)S(1)}, u32[]{:S(2)}, u32[]{:S(2)}) %collective-permute-start.5) | collective-permute-done | bytes 163872 | tf_op jit(solution)/shard_map/ppermute | solution.py:244
  12.8 0.3 %collective-permute-start.7 = (f32[1,5,4,16,128]{4,3,2,1,0:T(8,128)S(1)}, f32[1,5,4,16,128]{4,3,2,1,0:T(8,128)S(1)}, u32[]{:S(2)}, u32[]{:S(2)}) collective-permute-start(f32[1,5,4,16,128]{4,3,2,1,0:T(8,128)S(1)} %collective-permute-done.5.refs_0_), channel_id=1, source_target_pairs={{0,4},{4,0},{8,12},{12,8},{16,20},{20,16},{24,28},{28,24},{1,5},{5... | collective-permute-start | bytes 491528 | tf_op jit(solution)/shard_map/ppermute | solution.py:222
  13.0 0.0 collective-permute-done.3.first
  13.0 0.7 %collective-permute-done.4.second = f32[88,128]{1,0:T(8,128)S(1)} collective-permute-done((f32[88,128]{1,0:T(8,128)S(1)}, f32[88,128]{1,0:T(8,128)S(1)}, u32[]{:S(2)}, u32[]{:S(2)}) %collective-permute-start.4) | collective-permute-done | bytes 45088 | tf_op jit(solution)/shard_map/ppermute | solution.py:269
  13.8 0.2 %collective-permute-done.2.near = f32[88,128]{1,0:T(8,128)S(1)} collective-permute-done((f32[88,128]{1,0:T(8,128)S(1)}, f32[88,128]{1,0:T(8,128)S(1)}, u32[]{:S(2)}, u32[]{:S(2)}) %collective-permute-start.2) | collective-permute-done | bytes 45088 | tf_op jit(solution)/shard_map/ppermute | solution.py:222
  14.0 0.0 copy-done.6
  14.0 0.1 beam.1
  14.1 0.0 collective-permute-done.6.mix
  14.1 0.0 collective-permute-done.7.refs_0_
  14.2 0.7 %final.1 = (f32[1,5,4,16,128]{4,3,2,1,0:T(8,128)}, f32[1,40]{1,0:T(1,128)}) custom-call(f32[1,5,4,16,128]{4,3,2,1,0:T(8,128)S(1)} %get-tuple-element.15.partial, f32[4,16,128]{2,1,0:T(8,128)S(1)} %copy-done.2, f32[1,40]{1,0:T(1,128)S(1)} %get-tuple-element.16.line, f32[1,5,4,16,128]{4,3,2,1,0:T(8,128)S(1)} %collective-permute-done.6.mix, ...), custom_call_target="tpu_custom_call" | custom-call | tf_op jit(solution)/shard_map/final/pallas_call | solution.py:228
  (10 shorter events, 0.0 us)
Async XLA Ops:
  0.6 4.6 %copy-start.1 = (f32[1,5,4,16,128]{4,3,2,1,0:T(8,128)S(1)}, f32[1,5,4,16,128]{4,3,2,1,0:T(8,128)}, u32[]{:S(2)}) copy-start(f32[1,5,4,16,128]{4,3,2,1,0:T(8,128)} %lam.5) | copy-start | bytes 491524
  0.6 4.7 %copy-start = (f32[1,7,5,5,4,16,128]{6,5,4,3,2,1,0:T(8,128)S(1)}, f32[1,7,5,5,4,16,128]{6,5,4,3,2,1,0:T(8,128)}, u32[]{:S(2)}) copy-start(f32[1,7,5,5,4,16,128]{6,5,4,3,2,1,0:T(8,128)} %jac.3) | copy-start | bytes 17203204
  0.7 4.7 %copy-start.5 = (f32[5,4,128]{2,1,0:T(4,128)S(1)}, f32[5,4,128]{2,1,0:T(4,128)}, u32[]{:S(2)}) copy-start(f32[5,4,128]{2,1,0:T(4,128)} %outward.1) | copy-start | bytes 30724
  0.7 4.7 %copy-start.7 = (s32[4,128]{1,0:T(4,128)S(1)}, s32[4,128]{1,0:T(4,128)}, u32[]{:S(2)}) copy-start(s32[4,128]{1,0:T(4,128)} %station.1) | copy-start | bytes 6148
  0.7 4.7 %copy-start.4 = (f32[40,256]{1,0:T(8,128)S(1)}, f32[40,256]{1,0:T(8,128)}, u32[]{:S(2)}) copy-start(f32[40,256]{1,0:T(8,128)} %phi.1) | copy-start | bytes 122884
  0.7 4.7 %copy-start.8 = (f32[40]{0:T(128)S(1)}, f32[40]{0:T(128)}, u32[]{:S(2)}) copy-start(f32[40]{0:T(128)} %param.17) | copy-start | bytes 484
  0.7 8.9 %collective-permute-start = (f32[1,5,4,16,128]{4,3,2,1,0:T(8,128)}, f32[1,5,4,16,128]{4,3,2,1,0:T(8,128)S(1)}, u32[]{:S(2)}, u32[]{:S(2)}) collective-permute-start(f32[1,5,4,16,128]{4,3,2,1,0:T(8,128)} %lam.5), channel_id=1, source_target_pairs={{0,8},{4,20},{8,0},{12,28},{16,24},{20,4},{24,16},{28,12},{1,9},{5... | collective-permute-start | bytes 491528 | tf_op jit(solution)/shard_map/ppermute | solution.py:244
  3.7 8.2 %collective-permute-start.1 = (f32[1,5,4,16,128]{4,3,2,1,0:T(8,128)}, f32[1,5,4,16,128]{4,3,2,1,0:T(8,128)S(1)}, u32[]{:S(2)}, u32[]{:S(2)}) collective-permute-start(f32[1,5,4,16,128]{4,3,2,1,0:T(8,128)} %lam.5), channel_id=1, source_target_pairs={{0,16},{4,12},{8,24},{12,4},{16,0},{20,28},{24,8},{28,20},{1,17},{... | collective-permute-start | bytes 491528 | tf_op jit(solution)/shard_map/ppermute | solution.py:244
  5.2 5.7 %copy-start.3 = (f32[1,5,4,16,128]{4,3,2,1,0:T(8,128)S(1)}, f32[1,5,4,16,128]{4,3,2,1,0:T(8,128)}, u32[]{:S(2)}) copy-start(f32[1,5,4,16,128]{4,3,2,1,0:T(8,128)} %source.1) | copy-start | bytes 491524
  5.2 7.5 %collective-permute-start.5 = (f32[1,5,4,16,128]{4,3,2,1,0:T(8,128)S(1)}, f32[1,5,4,16,128]{4,3,2,1,0:T(8,128)S(1)}, u32[]{:S(2)}, u32[]{:S(2)}) collective-permute-start(f32[1,5,4,16,128]{4,3,2,1,0:T(8,128)S(1)} %hold.1), channel_id=1, source_target_pairs={{0,28},{4,24},{8,20},{12,16},{16,12},{20,8},{24,4},{28,0},{1,29},{... | collective-permute-start | bytes 491528 | tf_op jit(solution)/shard_map/ppermute | solution.py:244
  5.4 6.5 %copy-start.2 = (f32[4,16,128]{2,1,0:T(8,128)S(1)}, f32[4,16,128]{2,1,0:T(8,128)}, u32[]{:S(2)}) copy-start(f32[4,16,128]{2,1,0:T(8,128)} %volume.5) | copy-start | bytes 98308
  5.7 7.3 %collective-permute-start.3 = (f32[88,128]{1,0:T(8,128)S(1)}, f32[88,128]{1,0:T(8,128)S(1)}, u32[]{:S(2)}, u32[]{:S(2)}) collective-permute-start(f32[88,128]{1,0:T(8,128)S(1)} %get-tuple-element.14), channel_id=1, source_target_pairs={{3,0},{2,1},{0,2},{1,3},{7,4},{6,5},{4,6},{5,7},{11,8},{10,9},{8,1... | collective-permute-start | bytes 135176 | tf_op jit(solution)/shard_map/ppermute | solution.py:268
  8.3 5.4 %collective-permute-start.4 = (f32[88,128]{1,0:T(8,128)S(1)}, f32[88,128]{1,0:T(8,128)S(1)}, u32[]{:S(2)}, u32[]{:S(2)}) collective-permute-start(f32[88,128]{1,0:T(8,128)S(1)} %get-tuple-element.14), channel_id=1, source_target_pairs={{0,3},{1,2},{2,0},{3,1},{4,7},{5,6},{6,4},{7,5},{8,11},{9,10},{10,... | collective-permute-start | bytes 135176 | tf_op jit(solution)/shard_map/ppermute | solution.py:269
  9.5 4.5 %collective-permute-start.2 = (f32[88,128]{1,0:T(8,128)S(1)}, f32[88,128]{1,0:T(8,128)S(1)}, u32[]{:S(2)}, u32[]{:S(2)}) collective-permute-start(f32[88,128]{1,0:T(8,128)S(1)} %get-tuple-element.12), channel_id=1, source_target_pairs={{0,1},{1,0},{2,3},{3,2},{4,5},{5,4},{6,7},{7,6},{8,9},{9,8},{10,11... | collective-permute-start | bytes 135176 | tf_op jit(solution)/shard_map/ppermute | solution.py:222
  11.4 2.6 %copy-start.6 = (f32[5,4,128]{2,1,0:T(4,128)S(1)}, f32[5,4,128]{2,1,0:T(4,128)}, u32[]{:S(2)}) copy-start(f32[5,4,128]{2,1,0:T(4,128)} %surface_in.1) | copy-start | bytes 30724
  12.0 2.1 %collective-permute-start.6 = (f32[1,5,4,16,128]{4,3,2,1,0:T(8,128)S(1)}, f32[1,5,4,16,128]{4,3,2,1,0:T(8,128)S(1)}, u32[]{:S(2)}, u32[]{:S(2)}) collective-permute-start(f32[1,5,4,16,128]{4,3,2,1,0:T(8,128)S(1)} %get-tuple-element.17), channel_id=1, source_target_pairs={{0,4},{4,0},{8,12},{12,8},{16,20},{20,16},{24,28},{28,24},{1,5},{5... | collective-permute-start | bytes 491528 | tf_op jit(solution)/shard_map/ppermute | solution.py:222
  12.8 1.4 %collective-permute-start.7 = (f32[1,5,4,16,128]{4,3,2,1,0:T(8,128)S(1)}, f32[1,5,4,16,128]{4,3,2,1,0:T(8,128)S(1)}, u32[]{:S(2)}, u32[]{:S(2)}) collective-permute-start(f32[1,5,4,16,128]{4,3,2,1,0:T(8,128)S(1)} %collective-permute-done.5.refs_0_), channel_id=1, source_target_pairs={{0,4},{4,0},{8,12},{12,8},{16,20},{20,16},{24,28},{28,24},{1,5},{5... | collective-permute-start | bytes 491528 | tf_op jit(solution)/shard_map/ppermute | solution.py:222
